TPU v7x, 32 devices: a whole 2x2x4 slice. The times are simulated.
32 devices in a mesh: groups: 2 (over y), band: 4 (over z), lon: 2 (over x), mp: 2 (over core).
Axes of the slice: x: 2, y: 2, z: 4, core: 2. Of those that a mesh axis runs over, the one named last changes fastest.
Arguments:
- cycle_field: bfloat16 [128, 83, 3072], P(('groups', 'band'), None, ('lon', 'mp')), parts along dimension 0, may hold values from -6 to 6
- cycle_length: int32 [64], P('band'), may hold values from 768 to 3072, as said below
- metric_weight: float32 [9, 64, 1440], P(None, 'band', ('lon', 'mp')), may hold values from -0.5 to 0.5
- patch_weight: bfloat16 [1328, 1024], P(None, 'mp'), may hold values from -0.15625 to 0.15625
- patch_bias: float32 [1024], P('mp'), may hold values from -4 to 4
- owner: int32 [4, 2, 720, 1], P('band', 'lon'), may hold values from 0 to 3; in each aligned block of 720 rows (0 to 719, 720 to 1439, ..., all dimensions but the last counted through in order) at most 360 rows name the same one
Outputs:
- owned: bfloat16 [8, 2, 4, 360, 1024], P(('groups', 'band'), 'lon', None, None, 'mp'), parts along dimension 0
There are 2 independent parts, one for each index of `groups`. A program takes and returns all parts, laid end to end along the dimension named above; an argument that names none is the same for every part. Nothing has to cross between parts.
Inputs may be any that keep to these rules, and one draw needn't show every extreme that they name: `cycle_length`: the longest cycle has exactly 3072 points in every draw. Within one group of 720 tokens no owner is named more than 360 times.
All inputs are finite; a program needn't handle non-finite values.
Results may differ from a plain program's by a relative error of at most 0.0052.
Values may be sent and summed in bfloat16 or wider, within the bound.
A program may use at most 64 MiB of HBM per device.

v0:
```python
import jax
import jax.numpy as jnp
from jax import lax
from jax.sharding import PartitionSpec as P

NOUT = 1440
PATCH = 4


def extended(block, sides, width, periodic):
    for axis, dim in sides:
        count = lax.axis_size(axis)
        forward = [(i, i + 1) for i in range(count - 1)]
        if periodic:
            forward.append((count - 1, 0))
        backward = [(target, source) for source, target in forward]
        low = lax.ppermute(
            lax.slice_in_dim(block, block.shape[dim] - width, None, axis=dim), axis, forward
        )
        high = lax.ppermute(lax.slice_in_dim(block, 0, width, axis=dim), axis, backward)
        block = jnp.concatenate([low, block, high], axis=dim)
    return block


def swapped(array, axis, distance):
    return lax.ppermute(array, axis, [(i, i ^ 1 << distance) for i in range(lax.axis_size(axis))])


def band_matrix(length, count, jstart, width):
    kpos = jnp.arange(count, dtype=jnp.int32).astype(jnp.float32)[None, :, None]
    jpos = (jstart + jnp.arange(width, dtype=jnp.int32)).astype(jnp.float32)[None, None, :]
    size = length.astype(jnp.float32)[:, None, None]
    centre = jpos * size / NOUT
    dist = jnp.abs(kpos - centre)
    dist = jnp.minimum(dist, size - dist)
    weight = jnp.maximum(0.0, 1.0 - dist) * (kpos < size).astype(jnp.float32)
    return weight.astype(jnp.bfloat16)


def per_device(cycle_field, cycle_length, metric_weight, patch_weight, patch_bias, owner):
    cycle_rows, nvars, pts_local = cycle_field.shape
    cols_local = metric_weight.shape[2]
    place = lax.axis_index(("lon", "mp"))
    jstart = place * cols_local
    piece = lax.all_gather(cycle_field, ("lon", "mp"), axis=2, tiled=True)
    matrix = band_matrix(cycle_length, piece.shape[2], jstart, cols_local)
    gridded = jnp.einsum("rvk,rkj->rvj", piece, matrix, preferred_element_type=jnp.float32).astype(
        jnp.bfloat16
    )
    sideways = extended(gridded, ((("lon", "mp"), 2),), 1, True)
    padded = extended(sideways, (("band", 0),), 1, False).astype(jnp.float32)
    total = gridded.astype(jnp.float32)
    for first in range(3):
        for second in range(3):
            shifted = padded[first : first + cycle_rows, :, second : second + cols_local]
            total = total + metric_weight[3 * first + second][:, None, :] * shifted
    stenciled = total.astype(jnp.bfloat16)
    partner = swapped(stenciled, "mp", 0)
    lower = lax.axis_index("mp") == 0
    left_half = jnp.where(lower, stenciled, partner)
    right_half = jnp.where(lower, partner, stenciled)
    joined = jnp.concatenate([left_half, right_half], axis=2)
    rows_dev = cycle_rows // PATCH
    cols_lon = 2 * cols_local // PATCH
    patches = (
        joined.reshape(rows_dev, PATCH, nvars, cols_lon, PATCH)
        .transpose(0, 3, 1, 2, 4)
        .reshape(rows_dev * cols_lon, -1)
    )
    encoded = (
        jnp.dot(patches, patch_weight, preferred_element_type=jnp.float32) + patch_bias[None, :]
    ).astype(jnp.bfloat16)
    bands = lax.axis_size("band")
    dest = owner.reshape(-1)
    count_tok = dest.shape[0]
    capacity = max(2, 2 * count_tok // bands)
    onehot = (dest[:, None] == jnp.arange(bands, dtype=jnp.int32)[None, :]).astype(jnp.int32)
    before = jnp.cumsum(onehot, axis=0) - onehot
    slot = jnp.sum(before * onehot, axis=1)
    select = (dest[None, None, :] == jnp.arange(bands, dtype=jnp.int32)[:, None, None]) & (
        slot[None, None, :] == jnp.arange(capacity, dtype=jnp.int32)[None, :, None]
    )
    outbox = jnp.einsum(
        "oct,tw->ocw", select.astype(jnp.bfloat16), encoded, preferred_element_type=jnp.float32
    ).astype(jnp.bfloat16)
    inbox = lax.all_to_all(outbox, "band", split_axis=0, concat_axis=0, tiled=True)
    return inbox.reshape(1, 1, bands, capacity, encoded.shape[1])


def solution(mesh):
    return jax.shard_map(
        per_device,
        mesh=mesh,
        in_specs=(
            P(("groups", "band"), None, ("lon", "mp")),
            P("band"),
            P(None, "band", ("lon", "mp")),
            P(None, "mp"),
            P("mp"),
            P("band", "lon", None, None),
        ),
        out_specs=P(("groups", "band"), "lon", None, None, "mp"),
        check_vma=False,
    )
```

profile of v0, /device:TPU:0, one launch (start us, length us, event | category | flops | bytes accessed | tf_op | source)
XLA Modules:
  0.0 190.8 jit_solution(2175776056551835897)
XLA Ops:
  6.5 0.0 copy-start
  6.5 0.0 copy-start.12
  6.5 0.0 all-gather.2.cloned.1.call-start
  6.5 3.7 %copy.11 = bf16[16,83,768]{2,1,0:T(8,128)(2,1)} copy(bf16[16,83,768]{2,0,1:T(8,128)(2,1)} %param.6) | data formatting | bytes 4079616 | tf_op args[0]
  10.3 0.0 all-gather.2.cloned.1.call-update
  10.3 0.0 copy-done.12
  10.4 0.1 multiply_multiply_fusion
  10.4 0.1 compare_convert_fusion
  10.5 62.4 %all-gather.2.cloned.1.call-done = bf16[16,83,3072]{2,1,0:T(8,128)(2,1)} async-done(((bf16[16,83,768]{2,1,0:T(8,128)(2,1)}), bf16[16,83,3072]{2,1,0:T(8,128)(2,1)}) %all-gather.2.cloned.1.call-update) | async-done | bytes 8159248 | tf_op jit(solution)/shard_map/all_gather | solution.py:45
  72.9 20.7 %fusion.26 = bf16[16,83,360]{2,1,0:T(8,128)(2,1)S(1)} fusion(bf16[16,83,3072]{2,1,0:T(8,128)(2,1)} %all-gather.2.cloned.1.call-done, f32[16,3072]{1,0:T(8,128)S(1)} %compare_convert_fusion, f32[16]{0:T(128)S(1)} %convert_element_type.57, f32[16,360]{1,0:T(8,128)S(1)} %multiply_multiply_fusion, f32[3072]{0:T(1024)S(1)} %iota_convert_fusion), kind=kOutput, calls=%fused_computation.33 | convolution fusion | flops 3079359488 | bytes 9347392 | tf_op jit(solution)/shard_map/rvk,rkj->rvj/dot_general | solution.py:47
  93.6 0.0 copy-start.1
  93.7 0.0 copy-start.10
  93.7 0.2 fusion.34
  93.9 0.3 collective-permute-start
  94.2 1.5 collective-permute-start.1
  95.7 8.4 %collective-permute-done = bf16[16,83,1]{2,1,0:T(8,128)(2,1)S(1)} collective-permute-done((bf16[16,83,1]{2,1,0:T(8,128)(2,1)S(1)}, bf16[16,83,1]{2,1,0:T(8,128)(2,1)S(1)}, u32[]{:S(2)}, u32[]{:S(2)}) %collective-permute-start) | collective-permute-done | bytes 2688 | tf_op jit(solution)/shard_map/ppermute | solution.py:17
  104.1 0.0 collective-permute-done.1
  104.1 0.1 pad_maximum_fusion.3
  104.2 3.1 %collective-permute-start.2 = (bf16[1,83,362]{2,1,0:T(8,128)(2,1)S(1)}, bf16[1,83,362]{2,1,0:T(8,128)(2,1)S(1)}, u32[]{:S(2)}, u32[]{:S(2)}) collective-permute-start(bf16[1,83,362]{2,1,0:T(8,128)(2,1)S(1)} %get-tuple-element.7), channel_id=1, source_target_pairs={{0,4},{4,8},{8,12},{1,5},{5,9},{9,13},{2,6},{6,10},{10,14},{3,7},{... | collective-permute-start | bytes 180284 | tf_op jit(solution)/shard_map/ppermute | solution.py:17
  107.3 1.5 collective-permute-start.3
  108.8 0.0 copy-done.1
  108.8 0.7 slice_bitcast_fusion.8
  109.5 0.0 copy-done.10
  109.5 0.0 copy-start.2
  109.5 0.0 copy-start.3
  109.5 0.0 copy-start.4
  109.5 0.0 copy-start.5
  109.5 0.0 copy-start.6
  109.6 0.0 copy-start.7
  109.6 0.0 copy-start.8
  109.6 0.0 copy-start.9
  109.6 0.0 collective-permute-done.2
  109.6 4.0 %collective-permute-done.3 = bf16[1,83,362]{2,1,0:T(8,128)(2,1)S(1)} collective-permute-done((bf16[1,83,362]{2,1,0:T(8,128)(2,1)S(1)}, bf16[1,83,362]{2,1,0:T(8,128)(2,1)S(1)}, u32[]{:S(2)}, u32[]{:S(2)}) %collective-permute-start.3) | collective-permute-done | bytes 60124 | tf_op jit(solution)/shard_map/ppermute | solution.py:20
  113.6 0.6 maximum_convert_fusion
  114.3 0.0 copy-done.2
  114.3 0.0 copy-done.3
  114.3 0.0 copy-done.4
  114.3 0.0 copy-done.5
  114.3 0.0 copy-done.6
  114.3 0.0 copy-done.7
  114.3 0.0 copy-done.8
  114.3 0.0 copy-done.9
  114.3 3.9 %fusion.11 = bf16[16,83,360]{2,1,0:T(8,128)(2,1)S(1)} fusion(f32[18,83,362]{2,1,0:T(8,128)S(1)} %maximum_convert_fusion, bf16[16,83,360]{2,1,0:T(8,128)(2,1)S(1)} %fusion.26, f32[16,360]{1,0:T(8,128)S(1)} %copy-done.8, f32[16,360]{1,0:T(8,128)S(1)} %copy-done.9, f32[16,360]{1,0:T(8,128)S(1)} %copy-done.2, f32[16,360]{1,0:T(8,128)S(1)} %copy-done.3, ...), kind=kLoop, calls=%fused_computation.12 | loop fusion | flops 9561600 | bytes 19330560 | tf_op jit(solution)/shard_map/convert_element_type | solution.py:57
  118.2 0.1 copy.12
  118.4 0.1 collective-permute-start.4
  118.5 1.1 reduce-window.6
  119.7 0.2 slice_reduce_fusion
  119.9 0.2 reduce-window.9
  120.1 0.1 add_bitcast_fusion
  120.2 0.9 iota_compare_fusion
  121.0 0.2 collective-permute-done.4
  121.2 1.5 broadcast_select_fusion.1
  122.7 0.8 pad_maximum_fusion
  123.5 2.8 %copy.15 = bf16[16,83,720]{1,2,0:T(8,128)(2,1)} copy(bf16[16,83,720]{2,1,0:T(8,128)(2,1)S(1)} %pad_maximum_fusion) | data formatting | bytes 3824640 | tf_op jit(solution)/shard_map/concatenate | solution.py:62
  126.4 7.8 %copy.16 = bf16[4,180,4,83,4]{1,0,4,3,2:T(4,128)(2,1)} copy(bf16[4,180,4,83,4]{3,4,1,2,0:T(4,128)(2,1)} %bitcast.42) | data formatting | bytes 3824640 | tf_op jit(solution)/shard_map/transpose | solution.py:67
  134.2 0.0 copy-start.11
  134.2 4.9 %reshape.151 = bf16[720,1328]{0,1:T(8,128)(2,1)S(1)} reshape(bf16[4,180,4,83,4]{1,0,4,3,2:T(4,128)(2,1)} %copy.16) | data formatting | bytes 3824640 | tf_op jit(solution)/shard_map/reshape | solution.py:68
  139.1 0.0 copy-done
  139.1 0.0 copy-done.11
  139.1 4.6 %fusion.20 = bf16[4,360,512]{2,1,0:T(8,128)(2,1)} fusion(pred[360,720]{1,0:T(8,128)(4,1)} %iota_compare_fusion, pred[4,720]{1,0:T(4,128)(4,1)S(1)} %iota_compare_fusion.2, bf16[720,1328]{0,1:T(8,128)(2,1)S(1)} %reshape.151, bf16[1328,512]{1,0:T(8,128)(2,1)S(1)} %copy-done, f32[512]{0:T(512)S(1)} %copy-done.11), kind=kOutput, calls=%fused_computation.30 | convolution fusion | flops 2043302400 | bytes 5010880 | tf_op jit(solution)/shard_map/oct,tw->ocw/dot_general | solution.py:83
  143.7 39.1 %all_to_all.5 = bf16[4,360,512]{2,1,0:T(8,128)(2,1)S(1)} all-to-all(bf16[4,360,512]{2,1,0:T(8,128)(2,1)} %fusion.20), channel_id=1, replica_groups=mesh['groups'=2,'band'=4,'lon'=2,'mp'=2] {'band'}, dimensions={0} | all-to-all | bytes 2949120 | tf_op jit(solution)/shard_map/all_to_all | solution.py:86
  182.8 1.1 copy.23
  (9 shorter events, 0.1 us)
Async XLA Ops:
  6.5 132.5 %copy-start = (bf16[1328,512]{1,0:T(8,128)(2,1)S(1)}, bf16[1328,512]{1,0:T(8,128)(2,1)}, u32[]{:S(2)}) copy-start(bf16[1328,512]{1,0:T(8,128)(2,1)} %param.9) | copy-start | bytes 4079620
  6.5 3.8 %copy-start.12 = (s32[16]{0:T(128)S(1)}, s32[16]{0:T(128)}, u32[]{:S(2)}) copy-start(s32[16]{0:T(128)} %param.7) | copy-start | bytes 196
  6.5 66.4 %all-gather.2.cloned.1.call-start = ((), (), s32[]{:S(2)}) async-start(), calls=%async_computation.1 | async-start | bytes 10813440 | tf_op jit(solution)/shard_map/all_gather | solution.py:45
  93.6 15.2 %copy-start.1 = (f32[9,16,360]{2,1,0:T(8,128)S(1)}, f32[9,16,360]{2,1,0:T(8,128)}, u32[]{:S(2)}) copy-start(f32[9,16,360]{2,1,0:T(8,128)} %param.8) | copy-start | bytes 622084
  93.7 15.8 %copy-start.10 = (s32[1,1,720,1]{2,3,1,0:T(1,128)S(1)}, s32[1,1,720,1]{2,3,1,0:T(1,128)}, u32[]{:S(2)}) copy-start(s32[1,1,720,1]{2,3,1,0:T(1,128)} %param.11) | copy-start | bytes 8644
  93.9 10.2 %collective-permute-start = (bf16[16,83,1]{2,1,0:T(8,128)(2,1)S(1)}, bf16[16,83,1]{2,1,0:T(8,128)(2,1)S(1)}, u32[]{:S(2)}, u32[]{:S(2)}) collective-permute-start(bf16[16,83,1]{2,1,0:T(8,128)(2,1)S(1)} %get-tuple-element.9), channel_id=1, source_target_pairs={{0,1},{1,2},{2,3},{3,0},{4,5},{5,6},{6,7},{7,4},{8,9},{9,10},{10,1... | collective-permute-start | bytes 7976 | tf_op jit(solution)/shard_map/ppermute | solution.py:17
  94.2 9.9 %collective-permute-start.1 = (bf16[16,83,1]{2,1,0:T(8,128)(2,1)S(1)}, bf16[16,83,1]{2,1,0:T(8,128)(2,1)S(1)}, u32[]{:S(2)}, u32[]{:S(2)}) collective-permute-start(bf16[16,83,1]{2,1,0:T(8,128)(2,1)S(1)} %get-tuple-element.10), channel_id=1, source_target_pairs={{1,0},{2,1},{3,2},{0,3},{5,4},{6,5},{7,6},{4,7},{9,8},{10,9},{11,1... | collective-permute-start | bytes 7976 | tf_op jit(solution)/shard_map/ppermute | solution.py:20
  104.2 5.4 %collective-permute-start.2 = (bf16[1,83,362]{2,1,0:T(8,128)(2,1)S(1)}, bf16[1,83,362]{2,1,0:T(8,128)(2,1)S(1)}, u32[]{:S(2)}, u32[]{:S(2)}) collective-permute-start(bf16[1,83,362]{2,1,0:T(8,128)(2,1)S(1)} %get-tuple-element.7), channel_id=1, source_target_pairs={{0,4},{4,8},{8,12},{1,5},{5,9},{9,13},{2,6},{6,10},{10,14},{3,7},{... | collective-permute-start | bytes 180284 | tf_op jit(solution)/shard_map/ppermute | solution.py:17
  107.3 6.3 %collective-permute-start.3 = (bf16[1,83,362]{2,1,0:T(8,128)(2,1)S(1)}, bf16[1,83,362]{2,1,0:T(8,128)(2,1)S(1)}, u32[]{:S(2)}, u32[]{:S(2)}) collective-permute-start(bf16[1,83,362]{2,1,0:T(8,128)(2,1)S(1)} %get-tuple-element.8), channel_id=1, source_target_pairs={{4,0},{8,4},{12,8},{5,1},{9,5},{13,9},{6,2},{10,6},{14,10},{7,3},{... | collective-permute-start | bytes 180284 | tf_op jit(solution)/shard_map/ppermute | solution.py:20
  109.5 4.8 %copy-start.2 = (f32[16,360]{1,0:T(8,128)S(1)}, f32[16,360]{1,0:T(8,128)}, u32[]{:S(2)}) copy-start(f32[16,360]{1,0:T(8,128)} %get-tuple-element.12) | copy-start | bytes 69124
  109.5 4.8 %copy-start.3 = (f32[16,360]{1,0:T(8,128)S(1)}, f32[16,360]{1,0:T(8,128)}, u32[]{:S(2)}) copy-start(f32[16,360]{1,0:T(8,128)} %get-tuple-element.13) | copy-start | bytes 69124
  109.5 4.8 %copy-start.4 = (f32[16,360]{1,0:T(8,128)S(1)}, f32[16,360]{1,0:T(8,128)}, u32[]{:S(2)}) copy-start(f32[16,360]{1,0:T(8,128)} %get-tuple-element.14) | copy-start | bytes 69124
  109.5 4.8 %copy-start.5 = (f32[16,360]{1,0:T(8,128)S(1)}, f32[16,360]{1,0:T(8,128)}, u32[]{:S(2)}) copy-start(f32[16,360]{1,0:T(8,128)} %get-tuple-element.15) | copy-start | bytes 69124
  109.5 4.8 %copy-start.6 = (f32[16,360]{1,0:T(8,128)S(1)}, f32[16,360]{1,0:T(8,128)}, u32[]{:S(2)}) copy-start(f32[16,360]{1,0:T(8,128)} %get-tuple-element.16) | copy-start | bytes 69124
  109.6 4.8 %copy-start.7 = (f32[16,360]{1,0:T(8,128)S(1)}, f32[16,360]{1,0:T(8,128)}, u32[]{:S(2)}) copy-start(f32[16,360]{1,0:T(8,128)} %get-tuple-element.17) | copy-start | bytes 69124
  109.6 4.8 %copy-start.8 = (f32[16,360]{1,0:T(8,128)S(1)}, f32[16,360]{1,0:T(8,128)}, u32[]{:S(2)}) copy-start(f32[16,360]{1,0:T(8,128)} %get-tuple-element.18) | copy-start | bytes 69124
  109.6 4.8 %copy-start.9 = (f32[16,360]{1,0:T(8,128)S(1)}, f32[16,360]{1,0:T(8,128)}, u32[]{:S(2)}) copy-start(f32[16,360]{1,0:T(8,128)} %get-tuple-element.19) | copy-start | bytes 69124
  118.4 2.8 %collective-permute-start.4 = (bf16[16,83,360]{2,0,1:T(8,128)(2,1)S(1)}, bf16[16,83,360]{2,0,1:T(8,128)(2,1)}, u32[]{:S(2)}, u32[]{:S(2)}) collective-permute-start(bf16[16,83,360]{2,0,1:T(8,128)(2,1)S(1)} %copy.12), channel_id=1, source_target_pairs={{0,1},{1,0},{2,3},{3,2},{4,5},{5,4},{6,7},{7,6},{8,9},{9,8},{10,11... | collective-permute-start | bytes 2868488 | tf_op jit(solution)/shard_map/ppermute | solution.py:26
  134.2 4.9 %copy-start.11 = (f32[512]{0:T(512)S(1)}, f32[512]{0:T(512)}, u32[]{:S(2)}) copy-start(f32[512]{0:T(512)} %param.10) | copy-start | bytes 6148
Sparse Core Ops, SparseCore 0:
  10.4 62.4 all-gather.1
where the time goes:
time: 191 us
  waiting for transfers between devices  75 us (39%)
  blocking collectives  39.1 us (20%)
  matrix products  25.3 us (13%)
  local copies, waits for them, and re-layouts  21.7 us (11%)
  between operations  13.7 us (7%)
  other arithmetic  9.46 us (5%)
  starting transfers between devices  6.48 us (3%)
    all_gather x1, waiting for transfers between devices, per_device(): piece = lax.all_gather(cycle_field, ('lon', 'mp'), axis=2, tiled=True)  62.4 us
    all_to_all x1, blocking collectives, per_device(): lax.all_to_all(outbox, 'band', split_axis=0, concat_axis=0, tiled=True)  39.1 us
    dot_general x1, matrix products, per_device(): jnp.einsum('rvk,rkj->rvj', piece, matrix, preferred_element_type=jnp.floa...  20.7 us
    ppermute x2, waiting for transfers between devices, extended(): lax.ppermute(lax.slice_in_dim(block, block.shape[dim] - width, None, axis...  8.39 us
    transpose x1, local copies, waits for them, and re-layouts, per_device(): patches = joined.reshape(rows_dev, PATCH, nvars, cols_lon, PATCH).transpo...  7.79 us
    unnamed x29, local copies, waits for them, and re-layouts  4.92 us
    reshape x1, local copies, waits for them, and re-layouts, per_device(): patches = joined.reshape(rows_dev, PATCH, nvars, cols_lon, PATCH).transpo...  4.91 us
    dot_general x1, matrix products, per_device(): jnp.einsum('oct,tw->ocw', select.astype(jnp.bfloat16), encoded, preferred...  4.55 us
  transfers between devices with their start and end apart: 6, of which 4 were waited for; matrix products, arithmetic and copies ran while one was open for 2% of the time, Pallas kernels for 0%

commit v1 on v0

v1 whole, which is shorter than its diff:
```python
import jax
import jax.numpy as jnp
from jax import lax
from jax.sharding import PartitionSpec as P

NOUT = 1440
PATCH = 4
CHUNKS = 4


def swap(array, axis="mp"):
    return lax.ppermute(array, axis, [(0, 1), (1, 0)])


def column_targets(jstart, stride):
    col = jnp.arange(PATCH * stride, dtype=jnp.int32)
    phase = col // stride
    place = col % stride - (phase == PATCH - 1).astype(jnp.int32)
    return (jstart + PATCH * place + phase + NOUT) % NOUT


def band_matrix(length, kstart, count, jpos):
    kpos = (kstart + jnp.arange(count, dtype=jnp.int32)).astype(jnp.float32)[None, :, None]
    size = length.astype(jnp.float32)[:, None, None]
    centre = jpos.astype(jnp.float32)[None, None, :] * size / NOUT
    dist = jnp.abs(kpos - centre)
    dist = jnp.minimum(dist, size - dist)
    weight = jnp.maximum(0.0, 1.0 - dist) * (kpos < size).astype(jnp.float32)
    return weight.astype(jnp.bfloat16)


def interpolate(field, length, kstart, jpos):
    matrix = band_matrix(length, kstart, field.shape[2], jpos)
    return jnp.einsum("rvk,rkj->rvj", field, matrix, preferred_element_type=jnp.float32).astype(
        jnp.bfloat16
    )


def stencil(padded, weights, stride):
    wide = padded.astype(jnp.float32)
    rows = padded.shape[0] - 2
    phase = jnp.arange(PATCH * stride, dtype=jnp.int32) // stride
    one = jnp.roll(wide, -1, axis=2)
    centre = jnp.where(phase < PATCH - 1, wide, one)
    left = jnp.roll(wide, stride, axis=2)
    right = jnp.where(
        phase < PATCH - 2, jnp.roll(wide, -stride, axis=2), jnp.roll(wide, -stride - 1, axis=2)
    )
    total = centre[1 : rows + 1]
    for first in range(3):
        for second, shifted in enumerate((left, centre, right)):
            total = total + weights[3 * first + second][:, None, :] * shifted[first : first + rows]
    return total.astype(jnp.bfloat16)


def per_device(cycle_field, cycle_length, metric_weight, patch_weight, patch_bias, owner):
    cycle_rows, nvars, pts_local = cycle_field.shape
    cols_local = metric_weight.shape[2]
    cells = cols_local // PATCH
    stride = -(-(cells + 1) * PATCH // 128) * 128 // PATCH
    nlon = lax.axis_size("lon")
    lon, mp = lax.axis_index("lon"), lax.axis_index("mp")
    bands = lax.axis_size("band")
    width = patch_weight.shape[1]
    kstart = (lon * 2 + mp) * pts_local

    kpad = -nvars % 16
    weight4 = patch_weight.reshape(PATCH, nvars, PATCH, width).transpose(0, 2, 1, 3)
    weight4 = jnp.pad(weight4, ((0, 0), (0, 0), (0, kpad), (0, 0)))
    bias = patch_bias[None, :]
    partner_weight = swap(weight4)
    partner_bias = swap(bias)

    metric = metric_weight.reshape(9, cycle_rows, cells, PATCH).transpose(0, 1, 3, 2)
    metric = jnp.pad(metric, ((0, 0), (0, 0), (0, 0), (0, stride - cells)))
    metric = metric.reshape(9, cycle_rows, PATCH * stride)

    def targets(mp_to):
        return jnp.concatenate(
            [
                column_targets(((lon + d) % nlon * 2 + mp_to) * cols_local, stride)
                for d in range(nlon)
            ]
        )

    own_cols, other_cols = targets(mp), targets(1 - mp)
    step = cycle_rows // CHUNKS
    span = PATCH * stride
    gridded = [None] * CHUNKS
    for chunk in [0, CHUNKS - 1] + list(range(1, CHUNKS - 1)):
        field = cycle_field[chunk * step : (chunk + 1) * step]
        length = cycle_length[chunk * step : (chunk + 1) * step]
        sent = swap(interpolate(field, length, kstart, other_cols))
        both = interpolate(field, length, kstart, own_cols) + sent
        total = both[:, :, :span]
        for d in range(1, nlon):
            total = total + lax.ppermute(
                both[:, :, d * span : (d + 1) * span],
                "lon",
                [(i, (i + d) % nlon) for i in range(nlon)],
            )
        gridded[chunk] = total
    up = [(i, i + 1) for i in range(bands - 1)]
    before = lax.ppermute(gridded[-1][-1:], "band", up)
    after = lax.ppermute(gridded[0][:1], "band", [(b, a) for a, b in up])
    padded = jnp.concatenate([before] + gridded + [after], axis=0)
    stenciled = stencil(padded, metric, stride)
    rows_dev = cycle_rows // PATCH
    patches = stenciled.reshape(rows_dev, PATCH, nvars, PATCH, stride)[..., :cells]
    patches = patches.transpose(0, 1, 3, 2, 4)
    patches = jnp.pad(patches, ((0, 0), (0, 0), (0, 0), (0, kpad), (0, 0)))
    patches = patches.reshape(rows_dev, -1, cells)

    def encode(weight, offset):
        out = jnp.einsum(
            "qkc,kw->qcw", patches, weight.reshape(-1, width), preferred_element_type=jnp.float32
        )
        return (out + offset[None]).astype(jnp.bfloat16)

    partner = swap(encode(partner_weight, partner_bias))
    mine = encode(weight4, bias)

    dest = owner.reshape(-1)
    count_tok = dest.shape[0]
    capacity = max(2, 2 * count_tok // bands)
    onehot = (dest[:, None] == jnp.arange(bands, dtype=jnp.int32)[None, :]).astype(jnp.int32)
    earlier = jnp.cumsum(onehot, axis=0) - onehot
    slot = jnp.sum(earlier * onehot, axis=1)
    where = (dest * capacity + slot).reshape(rows_dev, 2, cells)
    lower = mp == 0
    halves = jnp.stack(
        [
            jnp.where(lower, where[:, 0], where[:, 1]),
            jnp.where(lower, where[:, 1], where[:, 0]),
        ]
    ).reshape(-1)
    select = (
        halves[None, :] == jnp.arange(bands * capacity, dtype=jnp.int32)[:, None]
    ).astype(jnp.bfloat16)
    tokens = jnp.concatenate([mine.reshape(-1, width), partner.reshape(-1, width)], axis=0)
    outbox = (
        jnp.dot(select, tokens, preferred_element_type=jnp.float32)
        .astype(jnp.bfloat16)
        .reshape(bands, capacity, width)
    )
    inbox = lax.all_to_all(outbox, "band", split_axis=0, concat_axis=0, tiled=True)
    return inbox.reshape(1, 1, bands, capacity, width)


def solution(mesh):
    return jax.shard_map(
        per_device,
        mesh=mesh,
        in_specs=(
            P(("groups", "band"), None, ("lon", "mp")),
            P("band"),
            P(None, "band", ("lon", "mp")),
            P(None, "mp"),
            P("mp"),
            P("band", "lon", None, None),
        ),
        out_specs=P(("groups", "band"), "lon", None, None, "mp"),
        check_vma=False,
    )
```

time: 191 us -> 130 us (0.68)
  waiting for transfers between devices: 75 us -> 5.23 us
  between operations: 13.7 us -> 0.59 us
  local copies, waits for them, and re-layouts: 21.7 us -> 29.3 us
  matrix products: 25.3 us -> 32.4 us
  starting transfers between devices: 6.48 us -> 12.4 us
    all_gather x1 -> x0, waiting for transfers between devices: 62.4 us -> none  [per_device(): piece = lax.all_gather(cycle_field, ('lon', 'mp'), axis=2, tiled=True)]
    slice x2 -> x23, local copies, waits for them, and re-layouts: 0.4 us -> 13.4 us  [the longest x10 8.59 us: stencil(): weights[3 * first + second][:, None, :] * shifted[first:first + rows]]
    transpose x1 -> x0, local copies, waits for them, and re-layouts: 7.79 us -> none  [per_device(): patches = joined.reshape(rows_dev, PATCH, nvars, cols_lon, PATCH).transpo...]
    ppermute x5 -> x13, waiting for transfers between devices: 12.6 us -> 5.23 us  [the longest x4 5.2 us: per_device(): lax.ppermute(both[:, :, d * span:(d + 1) * span], 'lon', [(i, (i + d) % n...]
    dot_general x2 -> x11, matrix products: 25.3 us -> 32.4 us  [the longest x8 25.9 us: interpolate(): jnp.einsum('rvk,rkj->rvj', field, matrix, preferred_element_type=jnp.floa...]
    ppermute x5 -> x13, starting transfers between devices: 6.48 us -> 12.4 us  [the longest x4 5.76 us: per_device(): lax.ppermute(both[:, :, d * span:(d + 1) * span], 'lon', [(i, (i + d) % n...]
    convert_element_type x1 -> x4, local copies, waits for them, and re-layouts: 0.13 us -> 4.04 us  [interpolate(): jnp.einsum('rvk,rkj->rvj', field, matrix, preferred_element_type=jnp.floa...]
    concatenate x1, local copies, waits for them, and re-layouts: 2.83 us -> 0.02 us  [per_device(): padded = jnp.concatenate([before] + gridded + [after], axis=0)]
  transfers between devices with their start and end apart: 6 -> 13, of which waited for: 4 -> 1; matrix products, arithmetic and copies ran while one was open for 2% -> 44% of each run, Pallas kernels for 0% -> 0%
where the time goes in v1:
time: 130 us
  blocking collectives  39.7 us (31%)
  matrix products  32.4 us (25%)
  local copies, waits for them, and re-layouts  29.3 us (23%)
  starting transfers between devices  12.4 us (10%)
  other arithmetic  9.97 us (8%)
  waiting for transfers between devices  5.23 us (4%)
    all_to_all x1, blocking collectives, per_device(): lax.all_to_all(outbox, 'band', split_axis=0, concat_axis=0, tiled=True)  39.7 us
    dot_general x8, matrix products, interpolate(): jnp.einsum('rvk,rkj->rvj', field, matrix, preferred_element_type=jnp.floa...  25.9 us
    slice x10, local copies, waits for them, and re-layouts, stencil(): weights[3 * first + second][:, None, :] * shifted[first:first + rows]  8.59 us
    ppermute x4, starting transfers between devices, per_device(): lax.ppermute(both[:, :, d * span:(d + 1) * span], 'lon', [(i, (i + d) % n...  5.76 us
    ppermute x4, waiting for transfers between devices, per_device(): lax.ppermute(both[:, :, d * span:(d + 1) * span], 'lon', [(i, (i + d) % n...  5.2 us
    dot_general x2, matrix products, encode(): jnp.einsum('qkc,kw->qcw', patches, weight.reshape(-1, width), preferred_e...  5.16 us
    convert_element_type x1, other arithmetic, stencil(): return total.astype(jnp.bfloat16)  4.53 us
    unnamed x50, local copies, waits for them, and re-layouts  4.16 us
  transfers between devices with their start and end apart: 13, of which 1 were waited for; matrix products, arithmetic and copies ran while one was open for 44% of the time, Pallas kernels for 0%

profile of v1, /device:TPU:0, one launch (start us, length us, event | category | flops | bytes accessed | tf_op | source)
XLA Modules:
  0.0 129.5 jit_solution(5385222593535710453)
XLA Ops:
  0.0 0.9 slice_convert_fusion
  0.9 2.9 %fusion.211 = (bf16[4,83,768]{2,0,1:T(4,128)(2,1)S(1)}, bf16[4,83,768]{2,0,1:T(4,128)(2,1)S(1)}, bf16[4,83,768]{2,0,1:T(4,128)(2,1)S(1)}, bf16[4,83,768]{2,0,1:T(4,128)(2,1)S(1)}) fusion(bf16[16,83,768]{2,0,1:T(8,128)(2,1)} %param.6), kind=kLoop, calls=%fused_computation.218 | loop fusion | bytes 4079616 | tf_op jit(solution)/shard_map/slice | solution.py:91
  4.0 1.0 multiply_multiply_fusion
  5.0 2.7 %fusion.144 = bf16[4,83,768]{2,1,0:T(8,128)(2,1)S(1)} fusion(f32[4,768]{1,0:T(4,128)S(1)} %get-tuple-element.37, f32[4,768]{1,0:T(4,128)S(1)} %get-tuple-element.33, f32[4]{0:T(128)S(1)} %get-tuple-element.47, f32[768]{0:T(1024)S(1)} %add_convert_fusion.2, bf16[4,83,768]{2,0,1:T(4,128)(2,1)S(1)} %get-tuple-element.12), kind=kOutput, calls=%fused_computation.106 | convolution fusion | flops 410772480 | bytes 1047568 | tf_op jit(solution)/shard_map/rvk,rkj->rvj/dot_general | solution.py:34
  7.7 1.0 copy.63
  8.7 0.5 collective-permute-start
  9.1 2.7 %fusion.138 = bf16[4,83,768]{2,1,0:T(8,128)(2,1)S(1)} fusion(f32[4,768]{1,0:T(4,128)S(1)} %get-tuple-element.35, f32[4,768]{1,0:T(4,128)S(1)} %get-tuple-element.31, f32[4]{0:T(128)S(1)} %get-tuple-element.46, f32[768]{0:T(1024)S(1)} %add_convert_fusion.2, bf16[4,83,768]{2,0,1:T(4,128)(2,1)S(1)} %get-tuple-element.11), kind=kOutput, calls=%fused_computation.104 | convolution fusion | flops 410772480 | bytes 1047568 | tf_op jit(solution)/shard_map/rvk,rkj->rvj/dot_general | solution.py:34
  11.8 1.0 copy.66
  12.9 2.7 %fusion.132 = bf16[4,83,768]{2,1,0:T(8,128)(2,1)S(1)} fusion(f32[4,768]{1,0:T(4,128)S(1)} %get-tuple-element.36, f32[4,768]{1,0:T(4,128)S(1)} %get-tuple-element.32, f32[4]{0:T(128)S(1)} %get-tuple-element.48, f32[768]{0:T(1024)S(1)} %add_convert_fusion.2, bf16[4,83,768]{2,0,1:T(4,128)(2,1)S(1)} %get-tuple-element.10), kind=kOutput, calls=%fused_computation.102 | convolution fusion | flops 410772480 | bytes 1047568 | tf_op jit(solution)/shard_map/rvk,rkj->rvj/dot_general | solution.py:34
  15.6 1.0 copy.69
  16.6 0.5 collective-permute-start.5
  17.0 2.8 %fusion.126 = bf16[4,83,768]{2,1,0:T(8,128)(2,1)S(1)} fusion(f32[4,768]{1,0:T(4,128)S(1)} %get-tuple-element.34, f32[4,768]{1,0:T(4,128)S(1)} %get-tuple-element.30, f32[4]{0:T(128)S(1)} %get-tuple-element.45, f32[768]{0:T(1024)S(1)} %add_convert_fusion.2, bf16[4,83,768]{2,0,1:T(4,128)(2,1)S(1)} %get-tuple-element.9), kind=kOutput, calls=%fused_computation.100 | convolution fusion | flops 410772480 | bytes 1047568 | tf_op jit(solution)/shard_map/rvk,rkj->rvj/dot_general | solution.py:34
  19.9 1.0 copy.72
  20.9 0.3 reshape.487
  21.3 0.3 copy.130
  21.6 1.4 %pad.19 = bf16[4,4,96,512]{3,2,1,0:T(8,128)(2,1)} pad(bf16[4,4,83,512]{3,2,1,0:T(8,128)(2,1)S(1)} %bitcast.92, bf16[]{:T(256)} %constant.114.clone.1), padding=0_0x0_0x0_13x0_0 | pad | bytes 2932738 | tf_op jit(solution)/shard_map/jit(_pad)/pad | solution.py:69
  22.9 0.5 collective-permute-start.10
  23.4 0.5 broadcast_compare_fusion.1
  23.9 0.5 copy.74
  24.4 1.3 pad_slice_fusion.12
  25.7 1.1 copy.75
  26.8 0.1 mul.368
  26.9 1.0 copy.76
  28.0 1.0 copy.77
  29.0 0.1 mul.374
  29.1 1.0 copy.78
  30.1 0.1 mul.377
  30.3 1.0 copy.79
  31.3 0.1 mul.380
  31.4 1.0 copy.80
  32.4 0.1 mul.383
  32.5 1.0 copy.81
  33.7 0.1 mul.389
  33.9 0.1 mul.392
  34.1 1.1 reduce-window.6
  35.2 0.2 slice_reduce_fusion
  35.5 0.2 reduce-window.9
  36.0 0.1 collective-permute-start.11
  36.2 3.8 %copy_add_fusion.3 = bf16[4,83,768]{2,1,0:T(8,128)(2,1)S(1)} fusion(bf16[4,83,768]{2,0,1:T(4,128)(2,1)} %collective-permute-done, bf16[4,83,768]{2,0,1:T(4,128)(2,1)S(1)} %copy-done.9, f32[4,768]{1,0:T(4,128)S(1)} %get-tuple-element.33, f32[4]{0:T(128)S(1)} %copy-done.18, f32[4,768]{1,0:T(4,128)S(1)} %copy-done.14, f32[768]{0:T(1024)S(1)} %add_convert_fusion.2), kind=kOutput, calls=%fused_computation.114 | convolution fusion | flops 411027456 | bytes 1557520 | tf_op jit(solution)/shard_map/rvk,rkj->rvj/dot_general | solution.py:34
  40.0 3.0 %collective-permute-start.1 = (bf16[4,83,384]{2,1,0:T(8,128)(2,1)S(1)}, bf16[4,83,384]{2,1,0:T(8,128)(2,1)S(1)}, u32[]{:S(2)}, u32[]{:S(2)}) collective-permute-start(bf16[4,83,384]{2,1,0:T(8,128)(2,1)S(1)} %slice.225), channel_id=1, source_target_pairs={{0,2},{2,0},{1,3},{3,1},{4,6},{6,4},{5,7},{7,5},{8,10},{10,8},{9,1... | collective-permute-start | bytes 764936 | tf_op jit(solution)/shard_map/ppermute | solution.py:97
  43.0 3.8 %copy_add_fusion.2 = bf16[4,83,768]{2,1,0:T(8,128)(2,1)S(1)} fusion(bf16[4,83,768]{2,0,1:T(4,128)(2,1)} %collective-permute-done.3, bf16[4,83,768]{2,0,1:T(4,128)(2,1)S(1)} %copy-done.7, f32[4,768]{1,0:T(4,128)S(1)} %get-tuple-element.31, f32[4]{0:T(128)S(1)} %copy-done.16, f32[4,768]{1,0:T(4,128)S(1)} %copy-done.13, f32[768]{0:T(1024)S(1)} %add_convert_fusion.2), kind=kOutput, calls=%fused_computation.113 | convolution fusion | flops 411027456 | bytes 1557520 | tf_op jit(solution)/shard_map/rvk,rkj->rvj/dot_general | solution.py:34
  47.0 3.8 %copy_add_fusion.1 = bf16[4,83,768]{2,1,0:T(8,128)(2,1)S(1)} fusion(bf16[4,83,768]{2,0,1:T(4,128)(2,1)} %collective-permute-done.5, bf16[4,83,768]{2,0,1:T(4,128)(2,1)S(1)} %copy-done.5, f32[4,768]{1,0:T(4,128)S(1)} %get-tuple-element.32, f32[4]{0:T(128)S(1)} %get-tuple-element.48, f32[4,768]{1,0:T(4,128)S(1)} %copy-done.12, f32[768]{0:T(1024)S(1)} %add_convert_fusion.2), kind=kOutput, calls=%fused_computation.112 | convolution fusion | flops 411027456 | bytes 1557520 | tf_op jit(solution)/shard_map/rvk,rkj->rvj/dot_general | solution.py:34
  50.8 2.1 %collective-permute-start.6 = (bf16[4,83,384]{2,1,0:T(8,128)(2,1)S(1)}, bf16[4,83,384]{2,1,0:T(8,128)(2,1)S(1)}, u32[]{:S(2)}, u32[]{:S(2)}) collective-permute-start(bf16[4,83,384]{2,1,0:T(8,128)(2,1)S(1)} %slice.230), channel_id=1, source_target_pairs={{0,2},{2,0},{1,3},{3,1},{4,6},{6,4},{5,7},{7,5},{8,10},{10,8},{9,1... | collective-permute-start | bytes 764936 | tf_op jit(solution)/shard_map/ppermute | solution.py:97
  52.9 3.7 %collective-permute-start.2 = (bf16[1,83,384]{2,1,0:T(8,128)(2,1)S(1)}, bf16[1,83,384]{2,1,0:T(8,128)(2,1)S(1)}, u32[]{:S(2)}, u32[]{:S(2)}) collective-permute-start(bf16[1,83,384]{2,1,0:T(8,128)(2,1)S(1)} %slice.226), channel_id=1, source_target_pairs={{0,4},{4,8},{8,12},{1,5},{5,9},{9,13},{2,6},{6,10},{10,14},{3,7},{... | collective-permute-start | bytes 191240 | tf_op jit(solution)/shard_map/ppermute | solution.py:104
  56.7 3.7 %copy_add_fusion = bf16[4,83,768]{2,1,0:T(8,128)(2,1)S(1)} fusion(bf16[4,83,768]{2,0,1:T(4,128)(2,1)} %collective-permute-done.7, bf16[4,83,768]{2,0,1:T(4,128)(2,1)S(1)} %copy-done.3, f32[4,768]{1,0:T(4,128)S(1)} %get-tuple-element.30, f32[4]{0:T(128)S(1)} %get-tuple-element.45, f32[4,768]{1,0:T(4,128)S(1)} %copy-done.11, f32[768]{0:T(1024)S(1)} %add_convert_fusion.2), kind=kOutput, calls=%fused_computation.111 | convolution fusion | flops 411027456 | bytes 1557520 | tf_op jit(solution)/shard_map/rvk,rkj->rvj/dot_general | solution.py:34
  60.5 0.6 collective-permute-start.8
  61.1 0.1 constant_dynamic-update-slice_fusion.2
  61.2 1.3 collective-permute-start.9
  62.6 5.2 %collective-permute-done.8 = bf16[4,83,384]{2,1,0:T(8,128)(2,1)S(1)} collective-permute-done((bf16[4,83,384]{2,1,0:T(8,128)(2,1)S(1)}, bf16[4,83,384]{2,1,0:T(8,128)(2,1)S(1)}, u32[]{:S(2)}, u32[]{:S(2)}) %collective-permute-start.8) | collective-permute-done | bytes 255008 | tf_op jit(solution)/shard_map/ppermute | solution.py:97
  68.0 0.6 fusion.212
  68.6 0.5 slice.234
  69.1 0.5 slice.244
  69.7 0.2 fusion.213
  69.9 0.6 maximum_select_fusion.1
  70.5 0.4 maximum_select_fusion
  70.9 4.5 %fusion.59 = bf16[16,83,384]{2,1,0:T(8,128)(2,1)} fusion(f32[18,83,288]{2,1,0:T(8,128)S(1)} %get-tuple-element.23, f32[18,83,96]{2,1,0:T(8,128)S(1)} %get-tuple-element.25, f32[18,83,384]{2,1,0:T(8,128)S(1)} %maximum_select_fusion.1, f32[18,83,384]{2,1,0:T(8,128)S(1)} %maximum_select_fusion, f32[16,384]{1,0:T(8,128)S(1)} %mul.392, f32[16,384]{1,0:T(8,128)S(1)} %mul.389, ...), kind=kLoop, calls=%fused_computation.66 | loop fusion | flops 11218944 | bytes 15774720 | tf_op jit(solution)/shard_map/convert_element_type | solution.py:53
  75.4 3.0 %reshape.497 = bf16[4,4,83,4,96]{4,3,2,1,0:T(4,128)(2,1)S(1)} reshape(bf16[16,83,384]{2,1,0:T(8,128)(2,1)} %fusion.59) | data formatting | bytes 2039808 | tf_op jit(solution)/shard_map/reshape | solution.py:109
  78.5 2.4 %copy.98 = bf16[4,4,83,4,90]{2,4,3,0,1:T(8,128)(2,1)} copy(bf16[4,4,83,4,90]{4,3,2,1,0:T(4,128)(2,1)S(1)} %bitcast.94) | data formatting | bytes 1912320
  80.9 3.6 %fusion.121 = bf16[4,90,512]{2,1,0:T(8,128)(2,1)} fusion(bf16[4,4,96,512]{3,2,1,0:T(8,128)(2,1)} %collective-permute-done.10, bf16[4,4,4,83,90]{3,4,2,0,1:T(8,128)(2,1)} %bitcast.95, f32[512]{0:T(512)S(1)} %bitcast.104), kind=kOutput, calls=%fused_computation.99 | convolution fusion | flops 566599680 | bytes 2899712 | tf_op jit(solution)/shard_map/qkc,kw->qcw/dot_general | solution.py:115
  84.6 1.6 %fusion.116 = bf16[4,90,512]{2,1,0:T(8,128)(2,1)} fusion(bf16[4,4,4,83,90]{3,4,2,0,1:T(8,128)(2,1)S(1)} %bitcast.96, f32[512]{0:T(512)S(1)} %copy-done.21, bf16[4,4,83,512]{3,2,1,0:T(8,128)(2,1)S(1)} %bitcast.93), kind=kOutput, calls=%fused_computation.98 | convolution fusion | flops 566599680 | bytes 2686720 | tf_op jit(solution)/shard_map/qkc,kw->qcw/dot_general | solution.py:115
  86.2 1.1 reshape.488
  87.4 1.3 %fusion.49 = bf16[1440,512]{1,0:T(8,128)(2,1)S(1)} fusion(s32[720]{0:T(1024)S(1)} %eq.82, bf16[360,512]{1,0:T(8,128)(2,1)S(1)} %reshape.489, bf16[360,512]{1,0:T(8,128)(2,1)S(1)} %reshape.488), kind=kOutput, calls=%fused_computation.52 | convolution fusion | flops 1064931840 | bytes 2214720 | tf_op jit(solution)/shard_map/dot_general | solution.py:142
  88.7 39.7 %all_to_all.5 = bf16[4,360,512]{2,1,0:T(8,128)(2,1)S(1)} all-to-all(bf16[4,360,512]{2,1,0:T(8,128)(2,1)S(1)} %bitcast.97), channel_id=1, replica_groups=mesh['groups'=2,'band'=4,'lon'=2,'mp'=2] {'band'}, dimensions={0} | all-to-all | bytes 2949120 | tf_op jit(solution)/shard_map/all_to_all | solution.py:146
  128.4 1.1 copy.138
  (100 shorter events, 2.0 us)
Async XLA Ops:
  0.9 6.8 %copy-start.17 = (f32[4]{0:T(128)}, f32[4]{0:T(128)S(1)}, u32[]{:S(2)}) copy-start(f32[4]{0:T(128)S(1)} %get-tuple-element.47) | copy-start | bytes 52
  0.9 8.3 %copy-start.15 = (f32[4]{0:T(128)}, f32[4]{0:T(128)S(1)}, u32[]{:S(2)}) copy-start(f32[4]{0:T(128)S(1)} %get-tuple-element.46) | copy-start | bytes 52
  3.8 3.9 %copy-start.8 = (bf16[4,83,768]{2,0,1:T(4,128)(2,1)}, bf16[4,83,768]{2,0,1:T(4,128)(2,1)S(1)}, u32[]{:S(2)}) copy-start(bf16[4,83,768]{2,0,1:T(4,128)(2,1)S(1)} %get-tuple-element.12) | copy-start | bytes 1529860
  3.8 5.3 %copy-start.6 = (bf16[4,83,768]{2,0,1:T(4,128)(2,1)}, bf16[4,83,768]{2,0,1:T(4,128)(2,1)S(1)}, u32[]{:S(2)}) copy-start(bf16[4,83,768]{2,0,1:T(4,128)(2,1)S(1)} %get-tuple-element.11) | copy-start | bytes 1529860
  3.8 9.1 %copy-start.4 = (bf16[4,83,768]{2,0,1:T(4,128)(2,1)}, bf16[4,83,768]{2,0,1:T(4,128)(2,1)S(1)}, u32[]{:S(2)}) copy-start(bf16[4,83,768]{2,0,1:T(4,128)(2,1)S(1)} %get-tuple-element.10) | copy-start | bytes 1529860
  3.9 13.2 %copy-start.2 = (bf16[4,83,768]{2,0,1:T(4,128)(2,1)}, bf16[4,83,768]{2,0,1:T(4,128)(2,1)S(1)}, u32[]{:S(2)}) copy-start(bf16[4,83,768]{2,0,1:T(4,128)(2,1)S(1)} %get-tuple-element.9) | copy-start | bytes 1529860
  8.7 27.3 %collective-permute-start = (bf16[4,83,768]{2,0,1:T(4,128)(2,1)}, bf16[4,83,768]{2,0,1:T(4,128)(2,1)}, u32[]{:S(2)}, u32[]{:S(2)}) collective-permute-start(bf16[4,83,768]{2,0,1:T(4,128)(2,1)} %copy.63), channel_id=1, source_target_pairs={{0,1},{1,0},{2,3},{3,2},{4,5},{5,4},{6,7},{7,6},{8,9},{9,8},{10,11... | collective-permute-start | bytes 1529864 | tf_op jit(solution)/shard_map/ppermute | solution.py:12
  12.8 27.1 %collective-permute-start.3 = (bf16[4,83,768]{2,0,1:T(4,128)(2,1)}, bf16[4,83,768]{2,0,1:T(4,128)(2,1)}, u32[]{:S(2)}, u32[]{:S(2)}) collective-permute-start(bf16[4,83,768]{2,0,1:T(4,128)(2,1)} %copy.66), channel_id=1, source_target_pairs={{0,1},{1,0},{2,3},{3,2},{4,5},{5,4},{6,7},{7,6},{8,9},{9,8},{10,11... | collective-permute-start | bytes 1529864 | tf_op jit(solution)/shard_map/ppermute | solution.py:12
  16.6 30.3 %collective-permute-start.5 = (bf16[4,83,768]{2,0,1:T(4,128)(2,1)}, bf16[4,83,768]{2,0,1:T(4,128)(2,1)}, u32[]{:S(2)}, u32[]{:S(2)}) collective-permute-start(bf16[4,83,768]{2,0,1:T(4,128)(2,1)} %copy.69), channel_id=1, source_target_pairs={{0,1},{1,0},{2,3},{3,2},{4,5},{5,4},{6,7},{7,6},{8,9},{9,8},{10,11... | collective-permute-start | bytes 1529864 | tf_op jit(solution)/shard_map/ppermute | solution.py:12
  17.0 3.9 %copy-start.1 = (bf16[1328,512]{1,0:T(8,128)(2,1)S(1)}, bf16[1328,512]{1,0:T(8,128)(2,1)}, u32[]{:S(2)}) copy-start(bf16[1328,512]{1,0:T(8,128)(2,1)} %param.9) | copy-start | bytes 4079620
  20.9 32.1 %collective-permute-start.7 = (bf16[4,83,768]{2,0,1:T(4,128)(2,1)}, bf16[4,83,768]{2,0,1:T(4,128)(2,1)}, u32[]{:S(2)}, u32[]{:S(2)}) collective-permute-start(bf16[4,83,768]{2,0,1:T(4,128)(2,1)} %copy.72), channel_id=1, source_target_pairs={{0,1},{1,0},{2,3},{3,2},{4,5},{5,4},{6,7},{7,6},{8,9},{9,8},{10,11... | collective-permute-start | bytes 1529864 | tf_op jit(solution)/shard_map/ppermute | solution.py:12
  21.6 2.4 %copy-start.10 = (f32[9,16,360]{2,1,0:T(8,128)S(1)}, f32[9,16,360]{2,1,0:T(8,128)}, u32[]{:S(2)}) copy-start(f32[9,16,360]{2,1,0:T(8,128)} %param.8) | copy-start | bytes 622084
  22.9 58.0 %collective-permute-start.10 = (bf16[4,4,96,512]{3,2,1,0:T(8,128)(2,1)}, bf16[4,4,96,512]{3,2,1,0:T(8,128)(2,1)}, u32[]{:S(2)}, u32[]{:S(2)}) collective-permute-start(bf16[4,4,96,512]{3,2,1,0:T(8,128)(2,1)} %pad.19), channel_id=1, source_target_pairs={{0,1},{1,0},{2,3},{3,2},{4,5},{5,4},{6,7},{7,6},{8,9},{9,8},{10,11... | collective-permute-start | bytes 4718600 | tf_op jit(solution)/shard_map/ppermute | solution.py:12
  25.7 8.3 %copy-start.19 = (s32[1,1,720,1]{2,3,1,0:T(1,128)S(1)}, s32[1,1,720,1]{2,3,1,0:T(1,128)}, u32[]{:S(2)}) copy-start(s32[1,1,720,1]{2,3,1,0:T(1,128)} %param.11) | copy-start | bytes 8644
  25.7 10.3 %copy-start.21 = (f32[512]{0:T(512)S(1)}, f32[512]{0:T(512)}, u32[]{:S(2)}) copy-start(f32[512]{0:T(512)} %param.10) | copy-start | bytes 6148
  25.7 10.4 %copy-start.9 = (bf16[4,83,768]{2,0,1:T(4,128)(2,1)S(1)}, bf16[4,83,768]{2,0,1:T(4,128)(2,1)}, u32[]{:S(2)}) copy-start(bf16[4,83,768]{2,0,1:T(4,128)(2,1)} %copy-done.8) | copy-start | bytes 1529860
  25.7 10.4 %copy-start.14 = (f32[4,768]{1,0:T(4,128)S(1)}, f32[4,768]{1,0:T(4,128)}, u32[]{:S(2)}) copy-start(f32[4,768]{1,0:T(4,128)} %get-tuple-element.41) | copy-start | bytes 36868
  25.7 10.4 %copy-start.18 = (f32[4]{0:T(128)S(1)}, f32[4]{0:T(128)}, u32[]{:S(2)}) copy-start(f32[4]{0:T(128)} %copy-done.17) | copy-start | bytes 52
  36.0 44.9 %collective-permute-start.11 = (f32[1,512]{1,0:T(1,128)S(1)}, f32[1,512]{1,0:T(1,128)S(1)}, u32[]{:S(2)}, u32[]{:S(2)}) collective-permute-start(f32[1,512]{1,0:T(1,128)S(1)} %bitcast.103), channel_id=1, source_target_pairs={{0,1},{1,0},{2,3},{3,2},{4,5},{5,4},{6,7},{7,6},{8,9},{9,8},{10,11... | collective-permute-start | bytes 6152 | tf_op jit(solution)/shard_map/ppermute | solution.py:12
  36.1 6.9 %copy-start.7 = (bf16[4,83,768]{2,0,1:T(4,128)(2,1)S(1)}, bf16[4,83,768]{2,0,1:T(4,128)(2,1)}, u32[]{:S(2)}) copy-start(bf16[4,83,768]{2,0,1:T(4,128)(2,1)} %copy-done.6) | copy-start | bytes 1529860
  36.1 6.9 %copy-start.13 = (f32[4,768]{1,0:T(4,128)S(1)}, f32[4,768]{1,0:T(4,128)}, u32[]{:S(2)}) copy-start(f32[4,768]{1,0:T(4,128)} %get-tuple-element.43) | copy-start | bytes 36868
  36.2 6.9 %copy-start.16 = (f32[4]{0:T(128)S(1)}, f32[4]{0:T(128)}, u32[]{:S(2)}) copy-start(f32[4]{0:T(128)} %copy-done.15) | copy-start | bytes 52
  40.0 10.8 %collective-permute-start.1 = (bf16[4,83,384]{2,1,0:T(8,128)(2,1)S(1)}, bf16[4,83,384]{2,1,0:T(8,128)(2,1)S(1)}, u32[]{:S(2)}, u32[]{:S(2)}) collective-permute-start(bf16[4,83,384]{2,1,0:T(8,128)(2,1)S(1)} %slice.225), channel_id=1, source_target_pairs={{0,2},{2,0},{1,3},{3,1},{4,6},{6,4},{5,7},{7,5},{8,10},{10,8},{9,1... | collective-permute-start | bytes 764936 | tf_op jit(solution)/shard_map/ppermute | solution.py:97
  43.0 4.0 %copy-start.5 = (bf16[4,83,768]{2,0,1:T(4,128)(2,1)S(1)}, bf16[4,83,768]{2,0,1:T(4,128)(2,1)}, u32[]{:S(2)}) copy-start(bf16[4,83,768]{2,0,1:T(4,128)(2,1)} %copy-done.4) | copy-start | bytes 1529860
  43.0 4.0 %copy-start.12 = (f32[4,768]{1,0:T(4,128)S(1)}, f32[4,768]{1,0:T(4,128)}, u32[]{:S(2)}) copy-start(f32[4,768]{1,0:T(4,128)} %get-tuple-element.42) | copy-start | bytes 36868
  46.9 14.2 %collective-permute-start.4 = (bf16[4,83,384]{2,1,0:T(8,128)(2,1)S(1)}, bf16[4,83,384]{2,1,0:T(8,128)(2,1)S(1)}, u32[]{:S(2)}, u32[]{:S(2)}) collective-permute-start(bf16[4,83,384]{2,1,0:T(8,128)(2,1)S(1)} %slice.228), channel_id=1, source_target_pairs={{0,2},{2,0},{1,3},{3,1},{4,6},{6,4},{5,7},{7,5},{8,10},{10,8},{9,1... | collective-permute-start | bytes 764936 | tf_op jit(solution)/shard_map/ppermute | solution.py:97
  47.0 9.7 %copy-start.3 = (bf16[4,83,768]{2,0,1:T(4,128)(2,1)S(1)}, bf16[4,83,768]{2,0,1:T(4,128)(2,1)}, u32[]{:S(2)}) copy-start(bf16[4,83,768]{2,0,1:T(4,128)(2,1)} %copy-done.2) | copy-start | bytes 1529860
  47.0 9.7 %copy-start.11 = (f32[4,768]{1,0:T(4,128)S(1)}, f32[4,768]{1,0:T(4,128)}, u32[]{:S(2)}) copy-start(f32[4,768]{1,0:T(4,128)} %get-tuple-element.44) | copy-start | bytes 36868
  50.8 11.7 %collective-permute-start.6 = (bf16[4,83,384]{2,1,0:T(8,128)(2,1)S(1)}, bf16[4,83,384]{2,1,0:T(8,128)(2,1)S(1)}, u32[]{:S(2)}, u32[]{:S(2)}) collective-permute-start(bf16[4,83,384]{2,1,0:T(8,128)(2,1)S(1)} %slice.230), channel_id=1, source_target_pairs={{0,2},{2,0},{1,3},{3,1},{4,6},{6,4},{5,7},{7,5},{8,10},{10,8},{9,1... | collective-permute-start | bytes 764936 | tf_op jit(solution)/shard_map/ppermute | solution.py:97
  52.9 7.5 %collective-permute-start.2 = (bf16[1,83,384]{2,1,0:T(8,128)(2,1)S(1)}, bf16[1,83,384]{2,1,0:T(8,128)(2,1)S(1)}, u32[]{:S(2)}, u32[]{:S(2)}) collective-permute-start(bf16[1,83,384]{2,1,0:T(8,128)(2,1)S(1)} %slice.226), channel_id=1, source_target_pairs={{0,4},{4,8},{8,12},{1,5},{5,9},{9,13},{2,6},{6,10},{10,14},{3,7},{... | collective-permute-start | bytes 191240 | tf_op jit(solution)/shard_map/ppermute | solution.py:104
  60.5 7.4 %collective-permute-start.8 = (bf16[4,83,384]{2,1,0:T(8,128)(2,1)S(1)}, bf16[4,83,384]{2,1,0:T(8,128)(2,1)S(1)}, u32[]{:S(2)}, u32[]{:S(2)}) collective-permute-start(bf16[4,83,384]{2,1,0:T(8,128)(2,1)S(1)} %slice.232), channel_id=1, source_target_pairs={{0,2},{2,0},{1,3},{3,1},{4,6},{6,4},{5,7},{7,5},{8,10},{10,8},{9,1... | collective-permute-start | bytes 764936 | tf_op jit(solution)/shard_map/ppermute | solution.py:97
  61.2 6.8 %collective-permute-start.9 = (bf16[1,83,384]{2,1,0:T(8,128)(2,1)S(1)}, bf16[1,83,384]{2,1,0:T(8,128)(2,1)S(1)}, u32[]{:S(2)}, u32[]{:S(2)}) collective-permute-start(bf16[1,83,384]{2,1,0:T(8,128)(2,1)S(1)} %slice.233), channel_id=1, source_target_pairs={{4,0},{8,4},{12,8},{5,1},{9,5},{13,9},{6,2},{10,6},{14,10},{7,3},{... | collective-permute-start | bytes 191240 | tf_op jit(solution)/shard_map/ppermute | solution.py:105
  69.9 0.6 copy-start.20
  80.9 3.7 %copy-start = (bf16[4,4,83,4,90]{2,4,3,0,1:T(8,128)(2,1)S(1)}, bf16[4,4,83,4,90]{2,4,3,0,1:T(8,128)(2,1)}, u32[]{:S(2)}) copy-start(bf16[4,4,83,4,90]{2,4,3,0,1:T(8,128)(2,1)} %copy.98) | copy-start | bytes 2868484
  84.5 2.8 %collective-permute-start.12 = (bf16[4,90,512]{2,1,0:T(8,128)(2,1)}, bf16[4,90,512]{2,1,0:T(8,128)(2,1)S(1)}, u32[]{:S(2)}, u32[]{:S(2)}) collective-permute-start(bf16[4,90,512]{2,1,0:T(8,128)(2,1)} %fusion.121), channel_id=1, source_target_pairs={{0,1},{1,0},{2,3},{3,2},{4,5},{5,4},{6,7},{7,6},{8,9},{9,8},{10,11... | collective-permute-start | bytes 1105928 | tf_op jit(solution)/shard_map/ppermute | solution.py:12

commit v2 on v1

v2 whole, which is shorter than its diff:
```python
import functools

import jax
import jax.numpy as jnp
from jax import lax
from jax.experimental import pallas as pl
from jax.experimental.pallas import tpu as pltpu
from jax.sharding import PartitionSpec as P

NOUT = 1440
PATCH = 4
CHUNKS = 4


def swap(array, axis="mp"):
    return lax.ppermute(array, axis, [(0, 1), (1, 0)])


def interpolate_kernel(nlon, row0, cols, length_ref, place_ref, field_ref, other_ref, own_ref, total):
    nvars, points = field_ref.shape[1:]
    span = own_ref.shape[3]
    stride = span // PATCH
    tile = 256 if points % 256 == 0 else 128
    lon, mp = place_ref[0], place_ref[1]
    kstart = (lon * 2 + mp) * points
    length = length_ref[row0 + pl.program_id(0)]
    size = length.astype(jnp.float32)
    col = lax.broadcasted_iota(jnp.int32, (1, span), 1)
    phase = sum((col >= b * stride).astype(jnp.int32) for b in range(1, PATCH))
    place = col - phase * stride - (phase == PATCH - 1).astype(jnp.int32)
    relative = PATCH * place + phase
    for e in range(2):
        out_ref = other_ref if e else own_ref
        for d in range(nlon):
            target = lax.rem(lon + d, nlon) * 2 + (1 - mp if e else mp)
            jstart = target * cols
            jpos = jstart + relative
            jpos = jnp.where(jpos < 0, jpos + NOUT, jpos)
            jpos = jnp.where(jpos >= NOUT, jpos - NOUT, jpos)
            centre = jpos.astype(jnp.float32) * size / NOUT
            low = (jstart - 1).astype(jnp.float32) * size / NOUT - 2.0
            high = (jstart + cols).astype(jnp.float32) * size / NOUT + 2.0
            total[...] = jnp.zeros_like(total)
            for t in range(points // tile):
                first = kstart + t * tile
                start = first.astype(jnp.float32)
                near = (start <= high) & (start + tile >= low)
                turned = (target == 0) & (start <= size + 2.0) & (start + tile >= size - 6.0)
                closing = (target == 2 * nlon - 1) & (first == 0)

                @pl.when(near | turned | closing)
                def _():
                    kint = first + lax.broadcasted_iota(jnp.int32, (tile, 1), 0)
                    kpos = jnp.where(kint < length, kint.astype(jnp.float32), -1e6)
                    weight = jnp.maximum(1.0 - jnp.abs(kpos - centre), 0.0)
                    total[...] += jnp.dot(
                        field_ref[0, :, t * tile : (t + 1) * tile],
                        weight.astype(jnp.bfloat16),
                        preferred_element_type=jnp.float32,
                    )

            @pl.when(kstart == 0)
            def _():
                wrap = jnp.maximum(1.0 - (size - centre), 0.0)
                wrap = wrap.astype(jnp.bfloat16).astype(jnp.float32)
                total[...] += field_ref[0, :, 0:128].astype(jnp.float32)[:, 0:1] * wrap

            out_ref[d, 0] = total[...].astype(jnp.bfloat16)


def interpolate(field, length, place, chunk, rows, nlon, cols, span):
    nvars, points = field.shape[1:]
    out = jax.ShapeDtypeStruct((nlon, rows, nvars, span), jnp.bfloat16)
    out_spec = pl.BlockSpec((nlon, 1, nvars, span), lambda r, *_: (0, r, 0, 0))
    return pl.pallas_call(
        functools.partial(interpolate_kernel, nlon, chunk * rows, cols),
        out_shape=(out, out),
        grid_spec=pltpu.PrefetchScalarGridSpec(
            num_scalar_prefetch=2,
            grid=(rows,),
            in_specs=[pl.BlockSpec((1, nvars, points), lambda r, *_: (chunk * rows + r, 0, 0))],
            out_specs=(out_spec, out_spec),
            scratch_shapes=[pltpu.VMEM((nvars, span), jnp.float32)],
        ),
        cost_estimate=pl.CostEstimate(
            flops=4 * nlon * rows * nvars * points * span,
            bytes_accessed=rows * nvars * (2 * points + 8 * nlon * span),
            transcendentals=0,
        ),
        name="interpolate",
    )(length, place, field)


def encode_kernel(nchunks, cells, *refs):
    chunk_refs, (before_ref, after_ref) = refs[:nchunks], refs[nchunks : nchunks + 2]
    metric_ref, weight_a, weight_b, bias_a, bias_b, out_a, out_b, patches = refs[nchunks + 2 :]
    step, nvars, span = chunk_refs[0].shape
    stride = span // PATCH
    rows = nchunks * step
    lanes = patches.shape[1]
    vpad = patches.shape[0] // (PATCH * PATCH)
    phase_at = lax.broadcasted_iota(jnp.int32, (1, span), 1)

    def views(row):
        if row < 0:
            block = before_ref[0]
        elif row >= rows:
            block = after_ref[0]
        else:
            block = chunk_refs[row // step][row % step]
        wide = block.astype(jnp.float32)
        centre = jnp.where(
            phase_at < (PATCH - 1) * stride, wide, pltpu.roll(wide, span - 1, 1)
        )
        left = pltpu.roll(wide, stride, 1)
        right = jnp.where(
            phase_at < (PATCH - 2) * stride,
            pltpu.roll(wide, span - stride, 1),
            pltpu.roll(wide, span - stride - 1, 1),
        )
        return left, centre, right

    patches[...] = jnp.zeros_like(patches)
    window = [views(-1), views(0), None]
    for q in range(rows // PATCH):
        for a in range(PATCH):
            row = q * PATCH + a
            window[2] = views(row + 1)
            result = window[1][1]
            for first in range(3):
                for second in range(3):
                    coeff = metric_ref[3 * first + second, row : row + 1, :]
                    result = result + coeff * window[first][second]
            window = [window[1], window[2], None]
            for b in range(PATCH):
                moved = pltpu.roll(result, (span - b * stride) % span, 1) if b else result
                base = (a * PATCH + b) * vpad
                patches[base : base + nvars, :] = moved[:, :lanes].astype(jnp.bfloat16)
        tokens = patches[...].T
        for weight, bias, out in ((weight_b, bias_b, out_b), (weight_a, bias_a, out_a)):
            value = jnp.dot(tokens, weight[...], preferred_element_type=jnp.float32) + bias[...]
            out[q] = value[:cells].astype(jnp.bfloat16)


def encode(chunks, before, after, metric, weights, biases, cells):
    step, nvars, span = chunks[0].shape
    rows_dev = len(chunks) * step // PATCH
    depth, width = weights[0].shape
    out = jax.ShapeDtypeStruct((rows_dev, cells, width), jnp.bfloat16)
    vmem = pl.BlockSpec(memory_space=pltpu.VMEM)
    return pl.pallas_call(
        functools.partial(encode_kernel, len(chunks), cells),
        out_shape=(out, out),
        in_specs=[vmem] * (len(chunks) + 7),
        out_specs=(vmem, vmem),
        scratch_shapes=[pltpu.VMEM((depth, -(-cells // 128) * 128), jnp.bfloat16)],
        compiler_params=pltpu.CompilerParams(vmem_limit_bytes=40 * 1024 * 1024),
        name="encode",
    )(*chunks, before, after, metric, *weights, *biases)


def per_device(cycle_field, cycle_length, metric_weight, patch_weight, patch_bias, owner):
    cycle_rows, nvars, pts_local = cycle_field.shape
    cols_local = metric_weight.shape[2]
    cells = cols_local // PATCH
    stride = -(-(cells + 1) * PATCH // 128) * 128 // PATCH
    nlon = lax.axis_size("lon")
    lon, mp = lax.axis_index("lon"), lax.axis_index("mp")
    bands = lax.axis_size("band")
    width = patch_weight.shape[1]

    kpad = -nvars % 16
    weight4 = patch_weight.reshape(PATCH, nvars, PATCH, width).transpose(0, 2, 1, 3)
    weight4 = jnp.pad(weight4, ((0, 0), (0, 0), (0, kpad), (0, 0)))
    bias = patch_bias[None, :]
    partner_weight = swap(weight4)
    partner_bias = swap(bias)

    metric = metric_weight.reshape(9, cycle_rows, cells, PATCH).transpose(0, 1, 3, 2)
    metric = jnp.pad(metric, ((0, 0), (0, 0), (0, 0), (0, stride - cells)))
    metric = metric.reshape(9, cycle_rows, PATCH * stride)

    step = cycle_rows // CHUNKS
    span = PATCH * stride
    place = jnp.stack([lon, mp]).astype(jnp.int32)
    gridded = [None] * CHUNKS
    for chunk in [0, CHUNKS - 1] + list(range(1, CHUNKS - 1)):
        other, own = interpolate(
            cycle_field, cycle_length, place, chunk, step, nlon, cols_local, span
        )
        sent = swap(other)
        total = own[0] + sent[0]
        for d in range(1, nlon):
            total = total + lax.ppermute(
                own[d] + sent[d], "lon", [(i, (i + d) % nlon) for i in range(nlon)]
            )
        gridded[chunk] = total
    up = [(i, i + 1) for i in range(bands - 1)]
    before = lax.ppermute(gridded[-1][-1:], "band", up)
    after = lax.ppermute(gridded[0][:1], "band", [(b, a) for a, b in up])
    rows_dev = cycle_rows // PATCH
    mine, others = encode(
        gridded,
        before,
        after,
        metric,
        (weight4.reshape(-1, width), partner_weight.reshape(-1, width)),
        (bias, partner_bias),
        cells,
    )
    partner = swap(others)

    dest = owner.reshape(-1)
    count_tok = dest.shape[0]
    capacity = max(2, 2 * count_tok // bands)
    onehot = (dest[:, None] == jnp.arange(bands, dtype=jnp.int32)[None, :]).astype(jnp.int32)
    earlier = jnp.cumsum(onehot, axis=0) - onehot
    slot = jnp.sum(earlier * onehot, axis=1)
    where = (dest * capacity + slot).reshape(rows_dev, 2, cells)
    lower = mp == 0
    halves = jnp.stack(
        [
            jnp.where(lower, where[:, 0], where[:, 1]),
            jnp.where(lower, where[:, 1], where[:, 0]),
        ]
    ).reshape(-1)
    select = (
        halves[None, :] == jnp.arange(bands * capacity, dtype=jnp.int32)[:, None]
    ).astype(jnp.bfloat16)
    tokens = jnp.concatenate([mine.reshape(-1, width), partner.reshape(-1, width)], axis=0)
    outbox = (
        jnp.dot(select, tokens, preferred_element_type=jnp.float32)
        .astype(jnp.bfloat16)
        .reshape(bands, capacity, width)
    )
    inbox = lax.all_to_all(outbox, "band", split_axis=0, concat_axis=0, tiled=True)
    return inbox.reshape(1, 1, bands, capacity, width)


def solution(mesh):
    return jax.shard_map(
        per_device,
        mesh=mesh,
        in_specs=(
            P(("groups", "band"), None, ("lon", "mp")),
            P("band"),
            P(None, "band", ("lon", "mp")),
            P(None, "mp"),
            P("mp"),
            P("band", "lon", None, None),
        ),
        out_specs=P(("groups", "band"), "lon", None, None, "mp"),
        check_vma=False,
    )
```

time: 130 us -> 145 us (1.12)
  Pallas kernels: 0 us -> 43.5 us
  matrix products: 32.4 us -> 1.33 us
  waiting for transfers between devices: 5.23 us -> 19.1 us
  other arithmetic: 9.97 us -> 3.56 us
  local copies, waits for them, and re-layouts: 29.3 us -> 26.8 us
  starting transfers between devices: 12.4 us -> 10.4 us
    pallas_call x0 -> x5, Pallas kernels: none -> 43.5 us  [the longest x4 37.5 us: interpolate(): pl.pallas_call(functools.partial(interpolate_kernel, nlon, chunk * rows,...]
    dot_general x10 -> x0, matrix products: 31 us -> none  [the longest x8 25.9 us: interpolate(): jnp.einsum('rvk,rkj->rvj', field, matrix, preferred_element_type=jnp.floa...]
    ppermute x4, waiting for transfers between devices: 5.2 us -> 14 us  [per_device(): lax.ppermute(own[d] + sent[d], 'lon', [(i, (i + d) % nlon) for i in range...]
    pallas_call x0 -> x4, local copies, waits for them, and re-layouts: none -> 8.2 us  [interpolate(): pl.pallas_call(functools.partial(interpolate_kernel, nlon, chunk * rows,...]
    slice x21 -> x5, local copies, waits for them, and re-layouts: 13.4 us -> 5.25 us  [the longest x4 5.03 us: per_device(): total = own[0] + sent[0]]
    convert_element_type x6 -> x0, other arithmetic: 5.51 us -> none  [the longest x1 4.53 us: stencil(): return total.astype(jnp.bfloat16)]
    unnamed x50 -> x23, local copies, waits for them, and re-layouts: 4.16 us -> 9.19 us
    ppermute x1, waiting for transfers between devices: 0.01 us -> 4.32 us  [per_device(): after = lax.ppermute(gridded[0][:1], 'band', [(b, a) for a, b in up])]
  transfers between devices with their start and end apart: 13 -> 13, of which waited for: 1 -> 4; matrix products, arithmetic and copies ran while one was open for 44% -> 15% of each run, Pallas kernels for 0% -> 20%
where the time goes in v2:
time: 145 us; the launch traced here: 144 us
  Pallas kernels  43.5 us (30%)
  blocking collectives  38.8 us (27%)
  local copies, waits for them, and re-layouts  26.8 us (18%)
  waiting for transfers between devices  19.1 us (13%)
  starting transfers between devices  10.4 us (7%)
  other arithmetic  3.56 us (2%)
    all_to_all x1, blocking collectives, per_device(): lax.all_to_all(outbox, 'band', split_axis=0, concat_axis=0, tiled=True)  38.8 us
    pallas_call x4, Pallas kernels, interpolate(): pl.pallas_call(functools.partial(interpolate_kernel, nlon, chunk * rows,...  37.5 us
    ppermute x4, waiting for transfers between devices, per_device(): lax.ppermute(own[d] + sent[d], 'lon', [(i, (i + d) % nlon) for i in range...  14 us
    unnamed x23, local copies, waits for them, and re-layouts  9.19 us
    pallas_call x4, local copies, waits for them, and re-layouts, interpolate(): pl.pallas_call(functools.partial(interpolate_kernel, nlon, chunk * rows,...  8.2 us
    pallas_call x1, Pallas kernels, encode(): pl.pallas_call(functools.partial(encode_kernel, len(chunks), cells), out_...  5.97 us
    ppermute x1, starting transfers between devices, per_device(): before = lax.ppermute(gridded[-1][-1:], 'band', up)  5.36 us
    slice x4, local copies, waits for them, and re-layouts, per_device(): total = own[0] + sent[0]  5.03 us
  transfers between devices with their start and end apart: 13, of which 4 were waited for; matrix products, arithmetic and copies ran while one was open for 15% of the time, Pallas kernels for 20%

profile of v2, /device:TPU:0, one launch (start us, length us, event | category | flops | bytes accessed | tf_op | source)
XLA Modules:
  0.0 143.9 jit_solution(3927499999059675900)
XLA Ops:
  0.0 3.6 %copy.32.field_ref = bf16[16,83,768]{2,1,0:T(8,128)(2,1)} copy(bf16[16,83,768]{2,0,1:T(8,128)(2,1)} %param.6) | data formatting | bytes 4079616 | tf_op args[0]
  3.6 0.6 pad_add_fusion.1.place_ref
  4.2 9.3 %interpolate.4 = (bf16[2,4,83,384]{3,2,1,0:T(8,128)(2,1)}, bf16[2,4,83,384]{3,2,1,0:T(8,128)(2,1)}) custom-call(s32[16]{0:T(128)} %length_ref.7, s32[2]{0:T(128)} %pad_add_fusion.1.place_ref, bf16[16,83,768]{2,1,0:T(8,128)(2,1)} %copy.32.field_ref), custom_call_target="tpu_custom_call" | custom-call | flops 783286272 | bytes 2549760 | tf_op jit(solution)/shard_map/interpolate/pallas_call | solution.py:75
  13.4 2.0 %copy.33 = bf16[2,4,83,384]{3,1,2,0:T(4,128)(2,1)} copy(bf16[2,4,83,384]{3,2,1,0:T(8,128)(2,1)} %get-tuple-element.16) | data formatting | bytes 1019904 | tf_op jit(solution)/shard_map/interpolate/pallas_call | solution.py:75
  15.5 0.0 collective-permute-start
  15.5 9.5 %interpolate.5 = (bf16[2,4,83,384]{3,2,1,0:T(8,128)(2,1)}, bf16[2,4,83,384]{3,2,1,0:T(8,128)(2,1)}) custom-call(s32[16]{0:T(128)} %length_ref.7, s32[2]{0:T(128)} %pad_add_fusion.1.place_ref, bf16[16,83,768]{2,1,0:T(8,128)(2,1)} %copy.32.field_ref), custom_call_target="tpu_custom_call" | custom-call | flops 783286272 | bytes 2549760 | tf_op jit(solution)/shard_map/interpolate/pallas_call | solution.py:75
  25.0 2.0 %copy.37 = bf16[2,4,83,384]{3,1,2,0:T(4,128)(2,1)} copy(bf16[2,4,83,384]{3,2,1,0:T(8,128)(2,1)} %get-tuple-element.18) | data formatting | bytes 1019904 | tf_op jit(solution)/shard_map/interpolate/pallas_call | solution.py:75
  27.1 9.5 %interpolate.6 = (bf16[2,4,83,384]{3,2,1,0:T(8,128)(2,1)}, bf16[2,4,83,384]{3,2,1,0:T(8,128)(2,1)}) custom-call(s32[16]{0:T(128)} %length_ref.7, s32[2]{0:T(128)} %pad_add_fusion.1.place_ref, bf16[16,83,768]{2,1,0:T(8,128)(2,1)} %copy.32.field_ref), custom_call_target="tpu_custom_call" | custom-call | flops 783286272 | bytes 2549760 | tf_op jit(solution)/shard_map/interpolate/pallas_call | solution.py:75
  36.6 2.1 %copy.41 = bf16[2,4,83,384]{3,1,2,0:T(4,128)(2,1)} copy(bf16[2,4,83,384]{3,2,1,0:T(8,128)(2,1)} %get-tuple-element.20) | data formatting | bytes 1019904 | tf_op jit(solution)/shard_map/interpolate/pallas_call | solution.py:75
  38.6 9.2 %interpolate.7 = (bf16[2,4,83,384]{3,2,1,0:T(8,128)(2,1)}, bf16[2,4,83,384]{3,2,1,0:T(8,128)(2,1)}) custom-call(s32[16]{0:T(128)} %length_ref.7, s32[2]{0:T(128)} %pad_add_fusion.1.place_ref, bf16[16,83,768]{2,1,0:T(8,128)(2,1)} %copy.32.field_ref), custom_call_target="tpu_custom_call" | custom-call | flops 783286272 | bytes 2549760 | tf_op jit(solution)/shard_map/interpolate/pallas_call | solution.py:75
  47.9 2.1 %copy.45 = bf16[2,4,83,384]{3,1,2,0:T(4,128)(2,1)} copy(bf16[2,4,83,384]{3,2,1,0:T(8,128)(2,1)} %get-tuple-element.22) | data formatting | bytes 1019904 | tf_op jit(solution)/shard_map/interpolate/pallas_call | solution.py:75
  49.9 0.0 collective-permute-start.6
  49.9 0.3 reshape.96
  50.3 0.3 copy.96
  50.5 0.0 copy-start.8
  50.5 0.0 copy-start.7
  50.6 0.2 pad.14
  50.7 0.6 collective-permute-start.10
  51.4 1.1 reduce-window.6
  52.5 0.2 slice_reduce_fusion
  52.7 0.2 reduce-window.9
  52.9 0.1 add_bitcast_fusion
  53.0 0.1 mul.15
  53.1 0.1 reduce_sum.12
  53.2 1.7 %copy.48 = f32[9,16,360]{1,2,0:T(8,128)} copy(f32[9,16,360]{2,1,0:T(8,128)S(1)} %copy-done.7) | data formatting | bytes 414720 | tf_op args[2]
  54.9 2.0 %copy.60 = f32[9,16,4,90]{3,2,1,0:T(4,128)S(1)} copy(f32[9,16,4,90]{1,2,3,0:T(4,128)} %bitcast.57) | data formatting | bytes 414720
  57.0 0.8 pad.13.clone
  57.7 1.1 reshape.95.refs_6_
  58.9 0.0 collective-permute-done
  58.9 0.5 collective-permute-start.11
  59.4 1.2 fusion.25
  60.6 1.0 fusion.15
  61.7 0.1 collective-permute-start.1
  61.8 1.3 fusion.24
  63.1 0.1 fusion.12
  63.2 2.0 %collective-permute-start.3 = (bf16[4,83,384]{2,1,0:T(8,128)(2,1)S(1)}, bf16[4,83,384]{2,1,0:T(8,128)(2,1)S(1)}, u32[]{:S(2)}, u32[]{:S(2)}) collective-permute-start(bf16[4,83,384]{2,1,0:T(8,128)(2,1)S(1)} %fusion.12), channel_id=1, source_target_pairs={{0,2},{2,0},{1,3},{3,1},{4,6},{6,4},{5,7},{7,5},{8,10},{10,8},{9,1... | collective-permute-start | bytes 764936 | tf_op jit(solution)/shard_map/ppermute | solution.py:194
  65.2 1.2 fusion.22
  66.4 0.1 fusion.6
  66.5 0.0 collective-permute-done.4
  66.5 0.2 collective-permute-start.7
  66.7 1.2 fusion.23
  67.9 0.1 fusion.9
  68.0 13.8 %collective-permute-done.7 = bf16[4,83,384]{2,1,0:T(8,128)(2,1)S(1)} collective-permute-done((bf16[4,83,384]{2,1,0:T(8,128)(2,1)S(1)}, bf16[4,83,384]{2,1,0:T(8,128)(2,1)S(1)}, u32[]{:S(2)}, u32[]{:S(2)}) %collective-permute-start.7) | collective-permute-done | bytes 255008 | tf_op jit(solution)/shard_map/ppermute | solution.py:194
  81.8 0.3 collective-permute-start.5
  82.1 0.1 fusion.8.refs_3_
  82.2 0.0 collective-permute-done.1
  82.2 5.4 %collective-permute-start.8 = (bf16[1,83,384]{2,1,0:T(8,128)(2,1)S(1)}, bf16[1,83,384]{2,1,0:T(8,128)(2,1)S(1)}, u32[]{:S(2)}, u32[]{:S(2)}) collective-permute-start(bf16[1,83,384]{2,1,0:T(8,128)(2,1)S(1)} %slice.106), channel_id=1, source_target_pairs={{0,4},{4,8},{8,12},{1,5},{5,9},{9,13},{2,6},{6,10},{10,14},{3,7},{... | collective-permute-start | bytes 191240 | tf_op jit(solution)/shard_map/ppermute | solution.py:199
  87.6 0.1 fusion.17.refs_0_
  87.7 1.5 %collective-permute-start.9 = (bf16[1,83,384]{2,1,0:T(8,128)(2,1)S(1)}, bf16[1,83,384]{2,1,0:T(8,128)(2,1)S(1)}, u32[]{:S(2)}, u32[]{:S(2)}) collective-permute-start(bf16[1,83,384]{2,1,0:T(8,128)(2,1)S(1)} %slice.107), channel_id=1, source_target_pairs={{4,0},{8,4},{12,8},{5,1},{9,5},{13,9},{6,2},{10,6},{14,10},{7,3},{... | collective-permute-start | bytes 191240 | tf_op jit(solution)/shard_map/ppermute | solution.py:200
  89.2 0.1 fusion.14.refs_1_
  89.2 0.2 collective-permute-done.5
  89.5 0.1 fusion.11.refs_2_
  89.5 0.0 collective-permute-done.11.refs_10_
  89.5 0.0 collective-permute-done.8.refs_4_
  89.5 4.3 %collective-permute-done.9.refs_5_ = bf16[1,83,384]{2,1,0:T(8,128)(2,1)S(1)} collective-permute-done((bf16[1,83,384]{2,1,0:T(8,128)(2,1)S(1)}, bf16[1,83,384]{2,1,0:T(8,128)(2,1)S(1)}, u32[]{:S(2)}, u32[]{:S(2)}) %collective-permute-start.9) | collective-permute-done | bytes 63776 | tf_op jit(solution)/shard_map/ppermute | solution.py:200
  93.9 6.0 %encode.1 = (bf16[4,90,512]{2,1,0:T(8,128)(2,1)S(1)}, bf16[4,90,512]{2,1,0:T(8,128)(2,1)}) custom-call(bf16[4,83,384]{2,1,0:T(8,128)(2,1)S(1)} %fusion.17.refs_0_, bf16[4,83,384]{2,1,0:T(8,128)(2,1)S(1)} %fusion.14.refs_1_, bf16[4,83,384]{2,1,0:T(8,128)(2,1)S(1)} %fusion.11.refs_2_, bf16[4,83,384]{2,1,0:T(8,128)(2,1)S(1)} %fusion.8.refs_3_, ...), custom_call_target="tpu_custom_call" | custom-call | tf_op jit(solution)/shard_map/encode/pallas_call | solution.py:151
  99.8 0.7 copy-done
  100.6 0.1 eq.48
  100.7 1.1 reshape.99
  101.8 0.7 collective-permute-done.12
  102.5 0.1 reshape.100
  102.6 1.3 fusion.1
  104.0 38.8 %all_to_all.5 = bf16[4,360,512]{2,1,0:T(8,128)(2,1)S(1)} all-to-all(bf16[4,360,512]{2,1,0:T(8,128)(2,1)S(1)} %bitcast.60), channel_id=1, replica_groups=mesh['groups'=2,'band'=4,'lon'=2,'mp'=2] {'band'}, dimensions={0} | all-to-all | bytes 2949120 | tf_op jit(solution)/shard_map/all_to_all | solution.py:236
  142.8 1.1 copy.99
  (34 shorter events, 0.2 us)
Async XLA Ops:
  15.5 43.4 %collective-permute-start = (bf16[2,4,83,384]{3,1,2,0:T(4,128)(2,1)}, bf16[2,4,83,384]{3,1,2,0:T(4,128)(2,1)}, u32[]{:S(2)}, u32[]{:S(2)}) collective-permute-start(bf16[2,4,83,384]{3,1,2,0:T(4,128)(2,1)} %copy.33), channel_id=1, source_target_pairs={{0,1},{1,0},{2,3},{3,2},{4,5},{5,4},{6,7},{7,6},{8,9},{9,8},{10,11... | collective-permute-start | bytes 1529864 | tf_op jit(solution)/shard_map/ppermute | solution.py:16
  27.1 34.6 %collective-permute-start.2 = (bf16[2,4,83,384]{3,1,2,0:T(4,128)(2,1)}, bf16[2,4,83,384]{3,1,2,0:T(4,128)(2,1)}, u32[]{:S(2)}, u32[]{:S(2)}) collective-permute-start(bf16[2,4,83,384]{3,1,2,0:T(4,128)(2,1)} %copy.37), channel_id=1, source_target_pairs={{0,1},{1,0},{2,3},{3,2},{4,5},{5,4},{6,7},{7,6},{8,9},{9,8},{10,11... | collective-permute-start | bytes 1529864 | tf_op jit(solution)/shard_map/ppermute | solution.py:16
  38.6 11.3 %copy-start.2 = (bf16[1328,512]{1,0:T(8,128)(2,1)S(1)}, bf16[1328,512]{1,0:T(8,128)(2,1)}, u32[]{:S(2)}) copy-start(bf16[1328,512]{1,0:T(8,128)(2,1)} %param.9) | copy-start | bytes 4079620
  38.6 27.9 %collective-permute-start.4 = (bf16[2,4,83,384]{3,1,2,0:T(4,128)(2,1)}, bf16[2,4,83,384]{3,1,2,0:T(4,128)(2,1)}, u32[]{:S(2)}, u32[]{:S(2)}) collective-permute-start(bf16[2,4,83,384]{3,1,2,0:T(4,128)(2,1)} %copy.41), channel_id=1, source_target_pairs={{0,1},{1,0},{2,3},{3,2},{4,5},{5,4},{6,7},{7,6},{8,9},{9,8},{10,11... | collective-permute-start | bytes 1529864 | tf_op jit(solution)/shard_map/ppermute | solution.py:16
  49.9 13.2 %collective-permute-start.6 = (bf16[2,4,83,384]{3,1,2,0:T(4,128)(2,1)}, bf16[2,4,83,384]{3,1,2,0:T(4,128)(2,1)}, u32[]{:S(2)}, u32[]{:S(2)}) collective-permute-start(bf16[2,4,83,384]{3,1,2,0:T(4,128)(2,1)} %copy.45), channel_id=1, source_target_pairs={{0,1},{1,0},{2,3},{3,2},{4,5},{5,4},{6,7},{7,6},{8,9},{9,8},{10,11... | collective-permute-start | bytes 1529864 | tf_op jit(solution)/shard_map/ppermute | solution.py:16
  50.5 0.8 copy-start.8
  50.5 2.7 %copy-start.7 = (f32[9,16,360]{2,1,0:T(8,128)S(1)}, f32[9,16,360]{2,1,0:T(8,128)}, u32[]{:S(2)}) copy-start(f32[9,16,360]{2,1,0:T(8,128)} %param.8) | copy-start | bytes 622084
  50.7 43.1 %collective-permute-start.10 = (bf16[4,4,96,512]{3,2,1,0:T(8,128)(2,1)S(1)}, bf16[4,4,96,512]{3,2,1,0:T(8,128)(2,1)S(1)}, u32[]{:S(2)}, u32[]{:S(2)}) collective-permute-start(bf16[4,4,96,512]{3,2,1,0:T(8,128)(2,1)S(1)} %pad.14), channel_id=1, source_target_pairs={{0,1},{1,0},{2,3},{3,2},{4,5},{5,4},{6,7},{7,6},{8,9},{9,8},{10,11... | collective-permute-start | bytes 4718600 | tf_op jit(solution)/shard_map/ppermute | solution.py:16
  54.9 4.0 %copy-start.1 = (f32[512]{0:T(512)S(1)}, f32[512]{0:T(512)}, u32[]{:S(2)}) copy-start(f32[512]{0:T(512)} %param.10) | copy-start | bytes 6148
  58.9 4.2 %copy-start.3 = (bf16[2,4,83,384]{3,2,1,0:T(8,128)(2,1)S(1)}, bf16[2,4,83,384]{3,2,1,0:T(8,128)(2,1)}, u32[]{:S(2)}) copy-start(bf16[2,4,83,384]{3,2,1,0:T(8,128)(2,1)} %get-tuple-element.17) | copy-start | bytes 1529860
  58.9 30.6 %collective-permute-start.11 = (f32[1,512]{1,0:T(1,128)S(1)}, f32[1,512]{1,0:T(1,128)S(1)}, u32[]{:S(2)}, u32[]{:S(2)}) collective-permute-start(f32[1,512]{1,0:T(1,128)S(1)} %bitcast.55), channel_id=1, source_target_pairs={{0,1},{1,0},{2,3},{3,2},{4,5},{5,4},{6,7},{7,6},{8,9},{9,8},{10,11... | collective-permute-start | bytes 6152 | tf_op jit(solution)/shard_map/ppermute | solution.py:16
  61.7 4.8 %copy-start.6 = (bf16[2,4,83,384]{3,2,1,0:T(8,128)(2,1)S(1)}, bf16[2,4,83,384]{3,2,1,0:T(8,128)(2,1)}, u32[]{:S(2)}) copy-start(bf16[2,4,83,384]{3,2,1,0:T(8,128)(2,1)} %get-tuple-element.21) | copy-start | bytes 1529860
  61.7 20.5 %collective-permute-start.1 = (bf16[4,83,384]{2,1,0:T(8,128)(2,1)S(1)}, bf16[4,83,384]{2,1,0:T(8,128)(2,1)S(1)}, u32[]{:S(2)}, u32[]{:S(2)}) collective-permute-start(bf16[4,83,384]{2,1,0:T(8,128)(2,1)S(1)} %fusion.15), channel_id=1, source_target_pairs={{0,2},{2,0},{1,3},{3,1},{4,6},{6,4},{5,7},{7,5},{8,10},{10,8},{9,1... | collective-permute-start | bytes 764936 | tf_op jit(solution)/shard_map/ppermute | solution.py:194
  63.1 4.8 %copy-start.4 = (bf16[2,4,83,384]{3,2,1,0:T(8,128)(2,1)S(1)}, bf16[2,4,83,384]{3,2,1,0:T(8,128)(2,1)}, u32[]{:S(2)}) copy-start(bf16[2,4,83,384]{3,2,1,0:T(8,128)(2,1)} %get-tuple-element.19) | copy-start | bytes 1529860
  63.2 24.5 %collective-permute-start.3 = (bf16[4,83,384]{2,1,0:T(8,128)(2,1)S(1)}, bf16[4,83,384]{2,1,0:T(8,128)(2,1)S(1)}, u32[]{:S(2)}, u32[]{:S(2)}) collective-permute-start(bf16[4,83,384]{2,1,0:T(8,128)(2,1)S(1)} %fusion.12), channel_id=1, source_target_pairs={{0,2},{2,0},{1,3},{3,1},{4,6},{6,4},{5,7},{7,5},{8,10},{10,8},{9,1... | collective-permute-start | bytes 764936 | tf_op jit(solution)/shard_map/ppermute | solution.py:194
  66.5 21.1 %copy-start.5 = (bf16[2,4,83,384]{3,2,1,0:T(8,128)(2,1)S(1)}, bf16[2,4,83,384]{3,2,1,0:T(8,128)(2,1)}, u32[]{:S(2)}) copy-start(bf16[2,4,83,384]{3,2,1,0:T(8,128)(2,1)} %get-tuple-element.15) | copy-start | bytes 1529860
  66.5 15.3 %collective-permute-start.7 = (bf16[4,83,384]{2,1,0:T(8,128)(2,1)S(1)}, bf16[4,83,384]{2,1,0:T(8,128)(2,1)S(1)}, u32[]{:S(2)}, u32[]{:S(2)}) collective-permute-start(bf16[4,83,384]{2,1,0:T(8,128)(2,1)S(1)} %fusion.6), channel_id=1, source_target_pairs={{0,2},{2,0},{1,3},{3,1},{4,6},{6,4},{5,7},{7,5},{8,10},{10,8},{9,1... | collective-permute-start | bytes 764936 | tf_op jit(solution)/shard_map/ppermute | solution.py:194
  81.8 7.6 %collective-permute-start.5 = (bf16[4,83,384]{2,1,0:T(8,128)(2,1)S(1)}, bf16[4,83,384]{2,1,0:T(8,128)(2,1)S(1)}, u32[]{:S(2)}, u32[]{:S(2)}) collective-permute-start(bf16[4,83,384]{2,1,0:T(8,128)(2,1)S(1)} %fusion.9), channel_id=1, source_target_pairs={{0,2},{2,0},{1,3},{3,1},{4,6},{6,4},{5,7},{7,5},{8,10},{10,8},{9,1... | collective-permute-start | bytes 764936 | tf_op jit(solution)/shard_map/ppermute | solution.py:194
  82.2 7.3 %collective-permute-start.8 = (bf16[1,83,384]{2,1,0:T(8,128)(2,1)S(1)}, bf16[1,83,384]{2,1,0:T(8,128)(2,1)S(1)}, u32[]{:S(2)}, u32[]{:S(2)}) collective-permute-start(bf16[1,83,384]{2,1,0:T(8,128)(2,1)S(1)} %slice.106), channel_id=1, source_target_pairs={{0,4},{4,8},{8,12},{1,5},{5,9},{9,13},{2,6},{6,10},{10,14},{3,7},{... | collective-permute-start | bytes 191240 | tf_op jit(solution)/shard_map/ppermute | solution.py:199
  87.7 6.2 %collective-permute-start.9 = (bf16[1,83,384]{2,1,0:T(8,128)(2,1)S(1)}, bf16[1,83,384]{2,1,0:T(8,128)(2,1)S(1)}, u32[]{:S(2)}, u32[]{:S(2)}) collective-permute-start(bf16[1,83,384]{2,1,0:T(8,128)(2,1)S(1)} %slice.107), channel_id=1, source_target_pairs={{4,0},{8,4},{12,8},{5,1},{9,5},{13,9},{6,2},{10,6},{14,10},{7,3},{... | collective-permute-start | bytes 191240 | tf_op jit(solution)/shard_map/ppermute | solution.py:200
  99.8 0.7 copy-start
  100.6 1.9 %collective-permute-start.12 = (bf16[4,90,512]{2,1,0:T(8,128)(2,1)}, bf16[4,90,512]{2,1,0:T(8,128)(2,1)S(1)}, u32[]{:S(2)}, u32[]{:S(2)}) collective-permute-start(bf16[4,90,512]{2,1,0:T(8,128)(2,1)} %get-tuple-element.24), channel_id=1, source_target_pairs={{0,1},{1,0},{2,3},{3,2},{4,5},{5,4},{6,7},{7,6},{8,9},{9,8},{10,11... | collective-permute-start | bytes 1105928 | tf_op jit(solution)/shard_map/ppermute | solution.py:16

commit v3 on v2

--- a/solution.py
+++ b/solution.py
@@ -16,9 +16,10 @@
     return lax.ppermute(array, axis, [(0, 1), (1, 0)])
 
 
-def interpolate_kernel(nlon, row0, cols, length_ref, place_ref, field_ref, other_ref, own_ref, total):
+def interpolate_kernel(nlon, row0, cols, length_ref, place_ref, field_ref, *refs):
     nvars, points = field_ref.shape[1:]
-    span = own_ref.shape[3]
+    out_refs, total = refs[:-1], refs[-1]
+    span = total.shape[1]
     stride = span // PATCH
     tile = 256 if points % 256 == 0 else 128
     lon, mp = place_ref[0], place_ref[1]
@@ -30,7 +31,6 @@
     place = col - phase * stride - (phase == PATCH - 1).astype(jnp.int32)
     relative = PATCH * place + phase
     for e in range(2):
-        out_ref = other_ref if e else own_ref
         for d in range(nlon):
             target = lax.rem(lon + d, nlon) * 2 + (1 - mp if e else mp)
             jstart = target * cols
@@ -59,31 +59,33 @@
                         preferred_element_type=jnp.float32,
                     )
 
-            @pl.when(kstart == 0)
+            edge = (target == 0) | (target == 2 * nlon - 1)
+
+            @pl.when((kstart == 0) & (length < NOUT) & edge)
             def _():
                 wrap = jnp.maximum(1.0 - (size - centre), 0.0)
                 wrap = wrap.astype(jnp.bfloat16).astype(jnp.float32)
                 total[...] += field_ref[0, :, 0:128].astype(jnp.float32)[:, 0:1] * wrap
 
-            out_ref[d, 0] = total[...].astype(jnp.bfloat16)
+            out_refs[e * nlon + d][0] = total[...].astype(jnp.bfloat16)
 
 
 def interpolate(field, length, place, chunk, rows, nlon, cols, span):
     nvars, points = field.shape[1:]
-    out = jax.ShapeDtypeStruct((nlon, rows, nvars, span), jnp.bfloat16)
-    out_spec = pl.BlockSpec((nlon, 1, nvars, span), lambda r, *_: (0, r, 0, 0))
+    out = jax.ShapeDtypeStruct((rows, nvars, span), jnp.bfloat16)
+    out_spec = pl.BlockSpec((1, nvars, span), lambda r, *_: (r, 0, 0))
     return pl.pallas_call(
         functools.partial(interpolate_kernel, nlon, chunk * rows, cols),
-        out_shape=(out, out),
+        out_shape=(out,) * (2 * nlon),
         grid_spec=pltpu.PrefetchScalarGridSpec(
             num_scalar_prefetch=2,
             grid=(rows,),
             in_specs=[pl.BlockSpec((1, nvars, points), lambda r, *_: (chunk * rows + r, 0, 0))],
-            out_specs=(out_spec, out_spec),
+            out_specs=(out_spec,) * (2 * nlon),
             scratch_shapes=[pltpu.VMEM((nvars, span), jnp.float32)],
         ),
         cost_estimate=pl.CostEstimate(
-            flops=4 * nlon * rows * nvars * points * span,
+            flops=32 * nlon * rows * nvars * points * span,
             bytes_accessed=rows * nvars * (2 * points + 8 * nlon * span),
             transcendentals=0,
         ),
@@ -183,16 +185,24 @@
     step = cycle_rows // CHUNKS
     span = PATCH * stride
     place = jnp.stack([lon, mp]).astype(jnp.int32)
-    gridded = [None] * CHUNKS
-    for chunk in [0, CHUNKS - 1] + list(range(1, CHUNKS - 1)):
-        other, own = interpolate(
+    order = [0, CHUNKS - 1] + list(range(1, CHUNKS - 1))
+    messages = [None] * CHUNKS
+    for index, chunk in enumerate(order):
+        if index >= 2:
+            place, messages[order[index - 2]] = lax.optimization_barrier(
+                (place, messages[order[index - 2]])
+            )
+        blocks = interpolate(
             cycle_field, cycle_length, place, chunk, step, nlon, cols_local, span
         )
-        sent = swap(other)
-        total = own[0] + sent[0]
+        sent = [swap(block) for block in blocks[nlon:]]
+        messages[chunk] = [own + got for own, got in zip(blocks[:nlon], sent)]
+    gridded = [None] * CHUNKS
+    for chunk in order:
+        total = messages[chunk][0]
         for d in range(1, nlon):
             total = total + lax.ppermute(
-                own[d] + sent[d], "lon", [(i, (i + d) % nlon) for i in range(nlon)]
+                messages[chunk][d], "lon", [(i, (i + d) % nlon) for i in range(nlon)]
             )
         gridded[chunk] = total
     up = [(i, i + 1) for i in range(bands - 1)]

time: 145 us -> 136 us (0.938)
  other arithmetic: 3.56 us -> 16.6 us
  local copies, waits for them, and re-layouts: 26.8 us -> 15.8 us
  waiting for transfers between devices: 19.1 us -> 13.6 us
  Pallas kernels: 43.5 us -> 38.2 us
    add x8 -> x10, other arithmetic: 1.46 us -> 14.4 us  [the longest x6 9.99 us: per_device(): messages[chunk] = [own + got for own, got in zip(blocks[:nlon], sent)]]
    pallas_call x4 -> x0, local copies, waits for them, and re-layouts: 8.2 us -> none  [interpolate(): pl.pallas_call(functools.partial(interpolate_kernel, nlon, chunk * rows,...]
    ppermute x4, waiting for transfers between devices: 14 us -> 8.72 us  [per_device(): lax.ppermute(messages[chunk][d], 'lon', [(i, (i + d) % nlon) for i in ran...]
    pallas_call x4, Pallas kernels: 37.5 us -> 32.2 us  [interpolate(): pl.pallas_call(functools.partial(interpolate_kernel, nlon, chunk * rows,...]
    slice x5 -> x1, local copies, waits for them, and re-layouts: 5.25 us -> 0.21 us  [the longest x4 5.03 us: per_device(): total = own[0] + sent[0]]
    unnamed x23, local copies, waits for them, and re-layouts: 9.19 us -> 11.4 us
  transfers between devices with their start and end apart: 13 -> 17, of which waited for: 4 -> 4; matrix products, arithmetic and copies ran while one was open for 15% -> 18% of each run, Pallas kernels for 20% -> 18%
where the time goes in v3:
time: 136 us
  blocking collectives  39.9 us (29%)
  Pallas kernels  38.2 us (28%)
  other arithmetic  16.6 us (12%)
  local copies, waits for them, and re-layouts  15.8 us (12%)
  waiting for transfers between devices  13.6 us (10%)
  starting transfers between devices  9.84 us (7%)
    all_to_all x1, blocking collectives, per_device(): lax.all_to_all(outbox, 'band', split_axis=0, concat_axis=0, tiled=True)  39.9 us
    pallas_call x4, Pallas kernels, interpolate(): pl.pallas_call(functools.partial(interpolate_kernel, nlon, chunk * rows,...  32.2 us
    unnamed x23, local copies, waits for them, and re-layouts  11.4 us
    add x6, other arithmetic, per_device(): messages[chunk] = [own + got for own, got in zip(blocks[:nlon], sent)]  9.99 us
    ppermute x4, waiting for transfers between devices, per_device(): lax.ppermute(messages[chunk][d], 'lon', [(i, (i + d) % nlon) for i in ran...  8.72 us
    pallas_call x1, Pallas kernels, encode(): pl.pallas_call(functools.partial(encode_kernel, len(chunks), cells), out_...  5.98 us
    ppermute x1, starting transfers between devices, per_device(): before = lax.ppermute(gridded[-1][-1:], 'band', up)  4.7 us
    add x4, other arithmetic, per_device(): total + lax.ppermute(messages[chunk][d], 'lon', [(i, (i + d) % nlon) for...  4.45 us
  transfers between devices with their start and end apart: 17, of which 4 were waited for; matrix products, arithmetic and copies ran while one was open for 18% of the time, Pallas kernels for 18%

profile of v3, /device:TPU:0, one launch (start us, length us, event | category | flops | bytes accessed | tf_op | source)
XLA Modules:
  0.0 135.6 jit_solution(7265564999248426546)
XLA Ops:
  0.0 3.6 %copy.21.field_ref = bf16[16,83,768]{2,1,0:T(8,128)(2,1)} copy(bf16[16,83,768]{2,0,1:T(8,128)(2,1)} %param.6) | data formatting | bytes 4079616 | tf_op args[0]
  3.6 0.7 pad_add_fusion.1.place_ref
  4.2 7.9 %interpolate.4 = (bf16[4,83,384]{2,1,0:T(8,128)(2,1)}, bf16[4,83,384]{2,1,0:T(8,128)(2,1)}, bf16[4,83,384]{2,1,0:T(8,128)(2,1)}, bf16[4,83,384]{2,1,0:T(8,128)(2,1)}) custom-call(s32[16]{0:T(128)} %length_ref.7, s32[2]{0:T(128)} %pad_add_fusion.1.place_ref, bf16[16,83,768]{2,1,0:T(8,128)(2,1)} %copy.21.field_ref), custom_call_target="tpu_custom_call" | custom-call | flops 6266290176 | bytes 2549760 | tf_op jit(solution)/shard_map/interpolate/pallas_call | solution.py:77
  12.2 0.0 collective-permute-start
  12.2 0.5 collective-permute-start.1
  12.7 7.6 %interpolate.6 = (bf16[4,83,384]{2,1,0:T(8,128)(2,1)}, bf16[4,83,384]{2,1,0:T(8,128)(2,1)}, bf16[4,83,384]{2,1,0:T(8,128)(2,1)}, bf16[4,83,384]{2,1,0:T(8,128)(2,1)}) custom-call(s32[16]{0:T(128)} %length_ref.7, s32[2]{0:T(128)} %pad_add_fusion.1.place_ref, bf16[16,83,768]{2,1,0:T(8,128)(2,1)} %copy.21.field_ref), custom_call_target="tpu_custom_call" | custom-call | flops 6266290176 | bytes 2549760 | tf_op jit(solution)/shard_map/interpolate/pallas_call | solution.py:77
  20.3 0.5 collective-permute-start.7
  20.8 0.3 reshape.88
  21.1 0.3 copy.33
  21.4 0.0 copy-start.8
  21.4 0.0 copy-start.4
  21.4 0.2 pad.14
  21.6 0.1 collective-permute-start.14
  21.7 0.4 copy-done.8
  22.1 0.0 collective-permute-done
  22.1 0.2 copy-done.4
  22.4 1.7 %add.45 = bf16[4,83,384]{2,1,0:T(8,128)(2,1)} add(bf16[4,83,384]{2,1,0:T(8,128)(2,1)S(1)} %copy-done.4, bf16[4,83,384]{2,1,0:T(8,128)(2,1)} %collective-permute-done) | non-fusion elementwise | flops 127488 | bytes 764928 | tf_op jit(solution)/shard_map/add | solution.py:199
  24.1 0.7 copy-done.5
  24.8 1.0 add.46
  25.8 7.6 %interpolate.5 = (bf16[4,83,384]{2,1,0:T(8,128)(2,1)}, bf16[4,83,384]{2,1,0:T(8,128)(2,1)}, bf16[4,83,384]{2,1,0:T(8,128)(2,1)}, bf16[4,83,384]{2,1,0:T(8,128)(2,1)}) custom-call(s32[16]{0:T(128)} %length_ref.7, s32[2]{0:T(128)} %pad_add_fusion.1.place_ref, bf16[16,83,768]{2,1,0:T(8,128)(2,1)} %copy.21.field_ref), custom_call_target="tpu_custom_call" | custom-call | flops 6266290176 | bytes 2549760 | tf_op jit(solution)/shard_map/interpolate/pallas_call | solution.py:77
  33.4 1.8 %add.51 = bf16[4,83,384]{2,1,0:T(8,128)(2,1)} add(bf16[4,83,384]{2,1,0:T(8,128)(2,1)} %get-tuple-element.40, bf16[4,83,384]{2,1,0:T(8,128)(2,1)} %collective-permute-done.6) | non-fusion elementwise | flops 127488 | bytes 764928 | tf_op jit(solution)/shard_map/add | solution.py:199
  35.2 1.8 %add.52 = bf16[4,83,384]{2,1,0:T(8,128)(2,1)} add(bf16[4,83,384]{2,1,0:T(8,128)(2,1)} %get-tuple-element.42, bf16[4,83,384]{2,1,0:T(8,128)(2,1)} %collective-permute-done.7) | non-fusion elementwise | flops 127488 | bytes 764928 | tf_op jit(solution)/shard_map/add | solution.py:199
  37.0 9.1 %interpolate.7 = (bf16[4,83,384]{2,1,0:T(8,128)(2,1)}, bf16[4,83,384]{2,1,0:T(8,128)(2,1)}, bf16[4,83,384]{2,1,0:T(8,128)(2,1)}, bf16[4,83,384]{2,1,0:T(8,128)(2,1)}) custom-call(s32[16]{0:T(128)} %length_ref.7, s32[2]{0:T(128)} %pad_add_fusion.1.place_ref, bf16[16,83,768]{2,1,0:T(8,128)(2,1)} %copy.21.field_ref), custom_call_target="tpu_custom_call" | custom-call | flops 6266290176 | bytes 2549760 | tf_op jit(solution)/shard_map/interpolate/pallas_call | solution.py:77
  46.2 0.0 collective-permute-start.9
  46.2 1.1 reduce-window.6
  47.4 0.1 collective-permute-start.2
  47.4 2.0 %collective-permute-start.11 = (bf16[4,83,384]{2,1,0:T(8,128)(2,1)}, bf16[4,83,384]{2,1,0:T(8,128)(2,1)}, u32[]{:S(2)}, u32[]{:S(2)}) collective-permute-start(bf16[4,83,384]{2,1,0:T(8,128)(2,1)} %add.52), channel_id=1, source_target_pairs={{0,2},{2,0},{1,3},{3,1},{4,6},{6,4},{5,7},{7,5},{8,10},{10,8},{9,1... | collective-permute-start | bytes 764936 | tf_op jit(solution)/shard_map/ppermute | solution.py:204
  49.4 0.2 slice_reduce_fusion
  49.7 0.2 reduce-window.9
  49.8 0.0 collective-permute-start.3
  49.9 1.8 %add.49 = bf16[4,83,384]{2,1,0:T(8,128)(2,1)} add(bf16[4,83,384]{2,1,0:T(8,128)(2,1)} %get-tuple-element.38, bf16[4,83,384]{2,1,0:T(8,128)(2,1)} %collective-permute-done.4) | non-fusion elementwise | flops 127488 | bytes 764928 | tf_op jit(solution)/shard_map/add | solution.py:199
  51.7 0.0 collective-permute-done.9
  51.7 0.3 collective-permute-start.5
  52.0 0.1 add_bitcast_fusion
  52.1 1.8 %add.54 = bf16[4,83,384]{2,1,0:T(8,128)(2,1)} add(bf16[4,83,384]{2,1,0:T(8,128)(2,1)} %get-tuple-element.47, bf16[4,83,384]{2,1,0:T(8,128)(2,1)} %collective-permute-done.9) | non-fusion elementwise | flops 127488 | bytes 764928 | tf_op jit(solution)/shard_map/add | solution.py:199
  53.9 2.9 %collective-permute-done.2 = bf16[4,83,384]{2,1,0:T(8,128)(2,1)} collective-permute-done((bf16[4,83,384]{2,1,0:T(8,128)(2,1)S(1)}, bf16[4,83,384]{2,1,0:T(8,128)(2,1)}, u32[]{:S(2)}, u32[]{:S(2)}) %collective-permute-start.2) | collective-permute-done | bytes 255008 | tf_op jit(solution)/shard_map/ppermute | solution.py:204
  56.8 0.0 collective-permute-start.8
  56.8 5.8 %collective-permute-done.11 = bf16[4,83,384]{2,1,0:T(8,128)(2,1)} collective-permute-done((bf16[4,83,384]{2,1,0:T(8,128)(2,1)}, bf16[4,83,384]{2,1,0:T(8,128)(2,1)}, u32[]{:S(2)}, u32[]{:S(2)}) %collective-permute-start.11) | collective-permute-done | bytes 255008 | tf_op jit(solution)/shard_map/ppermute | solution.py:204
  62.6 0.1 collective-permute-start.10
  62.7 0.1 mul.15
  62.8 0.1 reduce_sum.12
  62.9 2.6 %copy.25 = f32[9,16,360]{1,2,0:T(8,128)} copy(f32[9,16,360]{2,1,0:T(8,128)} %param.8) | data formatting | bytes 414720 | tf_op args[2]
  65.5 2.0 %copy.29 = f32[9,16,4,90]{3,2,1,0:T(4,128)S(1)} copy(f32[9,16,4,90]{1,2,3,0:T(4,128)} %bitcast.33) | data formatting | bytes 414720
  67.5 0.0 copy-start.1
  67.5 0.8 pad.13.clone
  68.3 1.1 reshape.87.refs_6_
  69.5 1.2 add.56.refs_3_
  70.7 1.1 add.47.refs_0_
  71.8 0.0 collective-permute-done.3
  71.8 0.1 collective-permute-start.15
  71.9 4.7 %collective-permute-start.12 = (bf16[1,83,384]{2,1,0:T(8,128)(2,1)S(1)}, bf16[1,83,384]{2,1,0:T(8,128)(2,1)S(1)}, u32[]{:S(2)}, u32[]{:S(2)}) collective-permute-start(bf16[1,83,384]{2,1,0:T(8,128)(2,1)S(1)} %slice.34), channel_id=1, source_target_pairs={{0,4},{4,8},{8,12},{1,5},{5,9},{9,13},{2,6},{6,10},{10,14},{3,7},{... | collective-permute-start | bytes 191240 | tf_op jit(solution)/shard_map/ppermute | solution.py:209
  76.6 1.1 add_add_fusion.1.refs_1_
  77.7 1.5 %collective-permute-start.13 = (bf16[1,83,384]{2,1,0:T(8,128)(2,1)S(1)}, bf16[1,83,384]{2,1,0:T(8,128)(2,1)S(1)}, u32[]{:S(2)}, u32[]{:S(2)}) collective-permute-start(bf16[1,83,384]{2,1,0:T(8,128)(2,1)S(1)} %slice.35), channel_id=1, source_target_pairs={{4,0},{8,4},{12,8},{5,1},{9,5},{13,9},{6,2},{10,6},{14,10},{7,3},{... | collective-permute-start | bytes 191240 | tf_op jit(solution)/shard_map/ppermute | solution.py:210
  79.2 1.1 add_add_fusion.refs_2_
  80.3 4.2 %collective-permute-done.13.refs_5_ = bf16[1,83,384]{2,1,0:T(8,128)(2,1)S(1)} collective-permute-done((bf16[1,83,384]{2,1,0:T(8,128)(2,1)S(1)}, bf16[1,83,384]{2,1,0:T(8,128)(2,1)S(1)}, u32[]{:S(2)}, u32[]{:S(2)}) %collective-permute-start.13) | collective-permute-done | bytes 63776 | tf_op jit(solution)/shard_map/ppermute | solution.py:210
  84.5 6.0 %encode.1 = (bf16[4,90,512]{2,1,0:T(8,128)(2,1)S(1)}, bf16[4,90,512]{2,1,0:T(8,128)(2,1)}) custom-call(bf16[4,83,384]{2,1,0:T(8,128)(2,1)S(1)} %add.47.refs_0_, bf16[4,83,384]{2,1,0:T(8,128)(2,1)S(1)} %add_add_fusion.1.refs_1_, bf16[4,83,384]{2,1,0:T(8,128)(2,1)S(1)} %add_add_fusion.refs_2_, bf16[4,83,384]{2,1,0:T(8,128)(2,1)S(1)} %add.56.refs_3_, ...), custom_call_target="tpu_custom_call" | custom-call | tf_op jit(solution)/shard_map/encode/pallas_call | solution.py:153
  90.5 0.7 copy-done
  91.3 0.1 eq.48
  91.3 1.1 reshape.91
  92.4 0.7 collective-permute-done.16
  93.2 0.1 reshape.92
  93.3 1.3 fusion.1
  94.6 39.9 %all_to_all.5 = bf16[4,360,512]{2,1,0:T(8,128)(2,1)S(1)} all-to-all(bf16[4,360,512]{2,1,0:T(8,128)(2,1)S(1)} %bitcast.36), channel_id=1, replica_groups=mesh['groups'=2,'band'=4,'lon'=2,'mp'=2] {'band'}, dimensions={0} | all-to-all | bytes 2949120 | tf_op jit(solution)/shard_map/all_to_all | solution.py:246
  134.5 1.1 copy.36
  (36 shorter events, 0.2 us)
Async XLA Ops:
  12.2 10.0 %collective-permute-start = (bf16[4,83,384]{2,1,0:T(8,128)(2,1)}, bf16[4,83,384]{2,1,0:T(8,128)(2,1)}, u32[]{:S(2)}, u32[]{:S(2)}) collective-permute-start(bf16[4,83,384]{2,1,0:T(8,128)(2,1)} %get-tuple-element.30), channel_id=1, source_target_pairs={{0,1},{1,0},{2,3},{3,2},{4,5},{5,4},{6,7},{7,6},{8,9},{9,8},{10,11... | collective-permute-start | bytes 764936 | tf_op jit(solution)/shard_map/ppermute | solution.py:16
  12.2 8.6 %copy-start.2 = (bf16[1328,512]{1,0:T(8,128)(2,1)S(1)}, bf16[1328,512]{1,0:T(8,128)(2,1)}, u32[]{:S(2)}) copy-start(bf16[1328,512]{1,0:T(8,128)(2,1)} %param.9) | copy-start | bytes 4079620
  12.2 11.9 %collective-permute-start.1 = (bf16[4,83,384]{2,1,0:T(8,128)(2,1)}, bf16[4,83,384]{2,1,0:T(8,128)(2,1)S(1)}, u32[]{:S(2)}, u32[]{:S(2)}) collective-permute-start(bf16[4,83,384]{2,1,0:T(8,128)(2,1)} %get-tuple-element.32), channel_id=1, source_target_pairs={{0,1},{1,0},{2,3},{3,2},{4,5},{5,4},{6,7},{7,6},{8,9},{9,8},{10,11... | collective-permute-start | bytes 764936 | tf_op jit(solution)/shard_map/ppermute | solution.py:16
  20.3 13.2 %collective-permute-start.6 = (bf16[4,83,384]{2,1,0:T(8,128)(2,1)}, bf16[4,83,384]{2,1,0:T(8,128)(2,1)}, u32[]{:S(2)}, u32[]{:S(2)}) collective-permute-start(bf16[4,83,384]{2,1,0:T(8,128)(2,1)} %get-tuple-element.41), channel_id=1, source_target_pairs={{0,1},{1,0},{2,3},{3,2},{4,5},{5,4},{6,7},{7,6},{8,9},{9,8},{10,11... | collective-permute-start | bytes 764936 | tf_op jit(solution)/shard_map/ppermute | solution.py:16
  20.3 15.0 %collective-permute-start.7 = (bf16[4,83,384]{2,1,0:T(8,128)(2,1)}, bf16[4,83,384]{2,1,0:T(8,128)(2,1)}, u32[]{:S(2)}, u32[]{:S(2)}) collective-permute-start(bf16[4,83,384]{2,1,0:T(8,128)(2,1)} %get-tuple-element.43), channel_id=1, source_target_pairs={{0,1},{1,0},{2,3},{3,2},{4,5},{5,4},{6,7},{7,6},{8,9},{9,8},{10,11... | collective-permute-start | bytes 764936 | tf_op jit(solution)/shard_map/ppermute | solution.py:16
  21.4 0.7 copy-start.8
  21.4 1.0 copy-start.4
  21.4 3.4 %copy-start.3 = (bf16[4,83,384]{2,1,0:T(8,128)(2,1)S(1)}, bf16[4,83,384]{2,1,0:T(8,128)(2,1)}, u32[]{:S(2)}) copy-start(bf16[4,83,384]{2,1,0:T(8,128)(2,1)} %get-tuple-element.31) | copy-start | bytes 764932
  21.6 62.9 %collective-permute-start.14 = (bf16[4,4,96,512]{3,2,1,0:T(8,128)(2,1)S(1)}, bf16[4,4,96,512]{3,2,1,0:T(8,128)(2,1)S(1)}, u32[]{:S(2)}, u32[]{:S(2)}) collective-permute-start(bf16[4,4,96,512]{3,2,1,0:T(8,128)(2,1)S(1)} %pad.14), channel_id=1, source_target_pairs={{0,1},{1,0},{2,3},{3,2},{4,5},{5,4},{6,7},{7,6},{8,9},{9,8},{10,11... | collective-permute-start | bytes 4718600 | tf_op jit(solution)/shard_map/ppermute | solution.py:16
  24.1 0.7 copy-start.5
  33.4 16.4 %collective-permute-start.4 = (bf16[4,83,384]{2,1,0:T(8,128)(2,1)}, bf16[4,83,384]{2,1,0:T(8,128)(2,1)}, u32[]{:S(2)}, u32[]{:S(2)}) collective-permute-start(bf16[4,83,384]{2,1,0:T(8,128)(2,1)} %get-tuple-element.39), channel_id=1, source_target_pairs={{0,1},{1,0},{2,3},{3,2},{4,5},{5,4},{6,7},{7,6},{8,9},{9,8},{10,11... | collective-permute-start | bytes 764936 | tf_op jit(solution)/shard_map/ppermute | solution.py:16
  46.2 5.5 %collective-permute-start.9 = (bf16[4,83,384]{2,1,0:T(8,128)(2,1)}, bf16[4,83,384]{2,1,0:T(8,128)(2,1)}, u32[]{:S(2)}, u32[]{:S(2)}) collective-permute-start(bf16[4,83,384]{2,1,0:T(8,128)(2,1)} %get-tuple-element.48), channel_id=1, source_target_pairs={{0,1},{1,0},{2,3},{3,2},{4,5},{5,4},{6,7},{7,6},{8,9},{9,8},{10,11... | collective-permute-start | bytes 764936 | tf_op jit(solution)/shard_map/ppermute | solution.py:16
  47.4 9.4 %collective-permute-start.2 = (bf16[4,83,384]{2,1,0:T(8,128)(2,1)S(1)}, bf16[4,83,384]{2,1,0:T(8,128)(2,1)}, u32[]{:S(2)}, u32[]{:S(2)}) collective-permute-start(bf16[4,83,384]{2,1,0:T(8,128)(2,1)S(1)} %add.46), channel_id=1, source_target_pairs={{0,2},{2,0},{1,3},{3,1},{4,6},{6,4},{5,7},{7,5},{8,10},{10,8},{9,1... | collective-permute-start | bytes 764936 | tf_op jit(solution)/shard_map/ppermute | solution.py:204
  47.4 15.2 %collective-permute-start.11 = (bf16[4,83,384]{2,1,0:T(8,128)(2,1)}, bf16[4,83,384]{2,1,0:T(8,128)(2,1)}, u32[]{:S(2)}, u32[]{:S(2)}) collective-permute-start(bf16[4,83,384]{2,1,0:T(8,128)(2,1)} %add.52), channel_id=1, source_target_pairs={{0,2},{2,0},{1,3},{3,1},{4,6},{6,4},{5,7},{7,5},{8,10},{10,8},{9,1... | collective-permute-start | bytes 764936 | tf_op jit(solution)/shard_map/ppermute | solution.py:204
  49.8 21.9 %collective-permute-start.3 = (bf16[4,83,384]{2,1,0:T(8,128)(2,1)}, bf16[4,83,384]{2,1,0:T(8,128)(2,1)}, u32[]{:S(2)}, u32[]{:S(2)}) collective-permute-start(bf16[4,83,384]{2,1,0:T(8,128)(2,1)} %get-tuple-element.37), channel_id=1, source_target_pairs={{0,1},{1,0},{2,3},{3,2},{4,5},{5,4},{6,7},{7,6},{8,9},{9,8},{10,11... | collective-permute-start | bytes 764936 | tf_op jit(solution)/shard_map/ppermute | solution.py:16
  51.7 20.2 %collective-permute-start.5 = (bf16[4,83,384]{2,1,0:T(8,128)(2,1)}, bf16[4,83,384]{2,1,0:T(8,128)(2,1)}, u32[]{:S(2)}, u32[]{:S(2)}) collective-permute-start(bf16[4,83,384]{2,1,0:T(8,128)(2,1)} %add.49), channel_id=1, source_target_pairs={{0,2},{2,0},{1,3},{3,1},{4,6},{6,4},{5,7},{7,5},{8,10},{10,8},{9,1... | collective-permute-start | bytes 764936 | tf_op jit(solution)/shard_map/ppermute | solution.py:204
  56.8 20.9 %collective-permute-start.8 = (bf16[4,83,384]{2,1,0:T(8,128)(2,1)}, bf16[4,83,384]{2,1,0:T(8,128)(2,1)}, u32[]{:S(2)}, u32[]{:S(2)}) collective-permute-start(bf16[4,83,384]{2,1,0:T(8,128)(2,1)} %get-tuple-element.46), channel_id=1, source_target_pairs={{0,1},{1,0},{2,3},{3,2},{4,5},{5,4},{6,7},{7,6},{8,9},{9,8},{10,11... | collective-permute-start | bytes 764936 | tf_op jit(solution)/shard_map/ppermute | solution.py:16
  62.6 16.6 %collective-permute-start.10 = (bf16[4,83,384]{2,1,0:T(8,128)(2,1)}, bf16[4,83,384]{2,1,0:T(8,128)(2,1)}, u32[]{:S(2)}, u32[]{:S(2)}) collective-permute-start(bf16[4,83,384]{2,1,0:T(8,128)(2,1)} %add.54), channel_id=1, source_target_pairs={{0,2},{2,0},{1,3},{3,1},{4,6},{6,4},{5,7},{7,5},{8,10},{10,8},{9,1... | collective-permute-start | bytes 764936 | tf_op jit(solution)/shard_map/ppermute | solution.py:204
  67.5 4.3 %copy-start.1 = (f32[512]{0:T(512)S(1)}, f32[512]{0:T(512)}, u32[]{:S(2)}) copy-start(f32[512]{0:T(512)} %param.10) | copy-start | bytes 6148
  69.5 7.2 %copy-start.6 = (bf16[4,83,384]{2,1,0:T(8,128)(2,1)S(1)}, bf16[4,83,384]{2,1,0:T(8,128)(2,1)}, u32[]{:S(2)}) copy-start(bf16[4,83,384]{2,1,0:T(8,128)(2,1)} %get-tuple-element.36) | copy-start | bytes 764932
  69.5 9.7 %copy-start.7 = (bf16[4,83,384]{2,1,0:T(8,128)(2,1)S(1)}, bf16[4,83,384]{2,1,0:T(8,128)(2,1)}, u32[]{:S(2)}) copy-start(bf16[4,83,384]{2,1,0:T(8,128)(2,1)} %get-tuple-element.45) | copy-start | bytes 764932
  71.8 8.5 %collective-permute-start.15 = (f32[1,512]{1,0:T(1,128)S(1)}, f32[1,512]{1,0:T(1,128)S(1)}, u32[]{:S(2)}, u32[]{:S(2)}) collective-permute-start(f32[1,512]{1,0:T(1,128)S(1)} %bitcast.31), channel_id=1, source_target_pairs={{0,1},{1,0},{2,3},{3,2},{4,5},{5,4},{6,7},{7,6},{8,9},{9,8},{10,11... | collective-permute-start | bytes 6152 | tf_op jit(solution)/shard_map/ppermute | solution.py:16
  71.9 8.4 %collective-permute-start.12 = (bf16[1,83,384]{2,1,0:T(8,128)(2,1)S(1)}, bf16[1,83,384]{2,1,0:T(8,128)(2,1)S(1)}, u32[]{:S(2)}, u32[]{:S(2)}) collective-permute-start(bf16[1,83,384]{2,1,0:T(8,128)(2,1)S(1)} %slice.34), channel_id=1, source_target_pairs={{0,4},{4,8},{8,12},{1,5},{5,9},{9,13},{2,6},{6,10},{10,14},{3,7},{... | collective-permute-start | bytes 191240 | tf_op jit(solution)/shard_map/ppermute | solution.py:209
  77.7 6.8 %collective-permute-start.13 = (bf16[1,83,384]{2,1,0:T(8,128)(2,1)S(1)}, bf16[1,83,384]{2,1,0:T(8,128)(2,1)S(1)}, u32[]{:S(2)}, u32[]{:S(2)}) collective-permute-start(bf16[1,83,384]{2,1,0:T(8,128)(2,1)S(1)} %slice.35), channel_id=1, source_target_pairs={{4,0},{8,4},{12,8},{5,1},{9,5},{13,9},{6,2},{10,6},{14,10},{7,3},{... | collective-permute-start | bytes 191240 | tf_op jit(solution)/shard_map/ppermute | solution.py:210
  90.5 0.7 copy-start
  91.2 1.9 %collective-permute-start.16 = (bf16[4,90,512]{2,1,0:T(8,128)(2,1)}, bf16[4,90,512]{2,1,0:T(8,128)(2,1)S(1)}, u32[]{:S(2)}, u32[]{:S(2)}) collective-permute-start(bf16[4,90,512]{2,1,0:T(8,128)(2,1)} %get-tuple-element.52), channel_id=1, source_target_pairs={{0,1},{1,0},{2,3},{3,2},{4,5},{5,4},{6,7},{7,6},{8,9},{9,8},{10,11... | collective-permute-start | bytes 1105928 | tf_op jit(solution)/shard_map/ppermute | solution.py:16

commit v4 on v1

--- a/solution.py
+++ b/solution.py
@@ -1,6 +1,10 @@
+import functools
+
 import jax
 import jax.numpy as jnp
 from jax import lax
+from jax.experimental import pallas as pl
+from jax.experimental.pallas import tpu as pltpu
 from jax.sharding import PartitionSpec as P
 
 NOUT = 1440
@@ -36,21 +40,72 @@
     )
 
 
-def stencil(padded, weights, stride):
-    wide = padded.astype(jnp.float32)
-    rows = padded.shape[0] - 2
-    phase = jnp.arange(PATCH * stride, dtype=jnp.int32) // stride
-    one = jnp.roll(wide, -1, axis=2)
-    centre = jnp.where(phase < PATCH - 1, wide, one)
-    left = jnp.roll(wide, stride, axis=2)
-    right = jnp.where(
-        phase < PATCH - 2, jnp.roll(wide, -stride, axis=2), jnp.roll(wide, -stride - 1, axis=2)
-    )
-    total = centre[1 : rows + 1]
-    for first in range(3):
-        for second, shifted in enumerate((left, centre, right)):
-            total = total + weights[3 * first + second][:, None, :] * shifted[first : first + rows]
-    return total.astype(jnp.bfloat16)
+def encode_kernel(nchunks, cells, *refs):
+    chunk_refs, (before_ref, after_ref) = refs[:nchunks], refs[nchunks : nchunks + 2]
+    metric_ref, weight_a, weight_b, bias_a, bias_b, out_a, out_b, patches = refs[nchunks + 2 :]
+    step, nvars, span = chunk_refs[0].shape
+    stride = span // PATCH
+    rows = nchunks * step
+    lanes = patches.shape[1]
+    vpad = patches.shape[0] // (PATCH * PATCH)
+    phase_at = lax.broadcasted_iota(jnp.int32, (1, span), 1)
+
+    def views(row):
+        if row < 0:
+            block = before_ref[0]
+        elif row >= rows:
+            block = after_ref[0]
+        else:
+            block = chunk_refs[row // step][row % step]
+        wide = block.astype(jnp.float32)
+        centre = jnp.where(
+            phase_at < (PATCH - 1) * stride, wide, pltpu.roll(wide, span - 1, 1)
+        )
+        left = pltpu.roll(wide, stride, 1)
+        right = jnp.where(
+            phase_at < (PATCH - 2) * stride,
+            pltpu.roll(wide, span - stride, 1),
+            pltpu.roll(wide, span - stride - 1, 1),
+        )
+        return left, centre, right
+
+    patches[...] = jnp.zeros_like(patches)
+    window = [views(-1), views(0), None]
+    for q in range(rows // PATCH):
+        for a in range(PATCH):
+            row = q * PATCH + a
+            window[2] = views(row + 1)
+            result = window[1][1]
+            for first in range(3):
+                for second in range(3):
+                    coeff = metric_ref[3 * first + second, row : row + 1, :]
+                    result = result + coeff * window[first][second]
+            window = [window[1], window[2], None]
+            for b in range(PATCH):
+                moved = pltpu.roll(result, (span - b * stride) % span, 1) if b else result
+                base = (a * PATCH + b) * vpad
+                patches[base : base + nvars, :] = moved[:, :lanes].astype(jnp.bfloat16)
+        tokens = patches[...].T
+        for weight, bias, out in ((weight_b, bias_b, out_b), (weight_a, bias_a, out_a)):
+            value = jnp.dot(tokens, weight[...], preferred_element_type=jnp.float32) + bias[...]
+            out[q] = value[:cells].astype(jnp.bfloat16)
+
+
+def encode(chunks, before, after, metric, weights, biases, cells):
+    step, nvars, span = chunks[0].shape
+    rows_dev = len(chunks) * step // PATCH
+    depth, width = weights[0].shape
+    out = jax.ShapeDtypeStruct((rows_dev, cells, width), jnp.bfloat16)
+    vmem = pl.BlockSpec(memory_space=pltpu.VMEM)
+    return pl.pallas_call(
+        functools.partial(encode_kernel, len(chunks), cells),
+        out_shape=(out, out),
+        in_specs=[vmem] * (len(chunks) + 7),
+        out_specs=(vmem, vmem),
+        scratch_shapes=[pltpu.VMEM((depth, -(-cells // 128) * 128), jnp.bfloat16)],
+        compiler_params=pltpu.CompilerParams(vmem_limit_bytes=40 * 1024 * 1024),
+        name="encode",
+    )(*chunks, before, after, metric, *weights, *biases)
 
 
 def per_device(cycle_field, cycle_length, metric_weight, patch_weight, patch_bias, owner):
@@ -61,8 +116,8 @@
     nlon = lax.axis_size("lon")
     lon, mp = lax.axis_index("lon"), lax.axis_index("mp")
     bands = lax.axis_size("band")
+    kstart = (lon * 2 + mp) * pts_local
     width = patch_weight.shape[1]
-    kstart = (lon * 2 + mp) * pts_local
 
     kpad = -nvars % 16
     weight4 = patch_weight.reshape(PATCH, nvars, PATCH, width).transpose(0, 2, 1, 3)
@@ -103,22 +158,17 @@
     up = [(i, i + 1) for i in range(bands - 1)]
     before = lax.ppermute(gridded[-1][-1:], "band", up)
     after = lax.ppermute(gridded[0][:1], "band", [(b, a) for a, b in up])
-    padded = jnp.concatenate([before] + gridded + [after], axis=0)
-    stenciled = stencil(padded, metric, stride)
     rows_dev = cycle_rows // PATCH
-    patches = stenciled.reshape(rows_dev, PATCH, nvars, PATCH, stride)[..., :cells]
-    patches = patches.transpose(0, 1, 3, 2, 4)
-    patches = jnp.pad(patches, ((0, 0), (0, 0), (0, 0), (0, kpad), (0, 0)))
-    patches = patches.reshape(rows_dev, -1, cells)
-
-    def encode(weight, offset):
-        out = jnp.einsum(
-            "qkc,kw->qcw", patches, weight.reshape(-1, width), preferred_element_type=jnp.float32
-        )
-        return (out + offset[None]).astype(jnp.bfloat16)
-
-    partner = swap(encode(partner_weight, partner_bias))
-    mine = encode(weight4, bias)
+    mine, others = encode(
+        gridded,
+        before,
+        after,
+        metric,
+        (weight4.reshape(-1, width), partner_weight.reshape(-1, width)),
+        (bias, partner_bias),
+        cells,
+    )
+    partner = swap(others)
 
     dest = owner.reshape(-1)
     count_tok = dest.shape[0]

time: 130 us -> 117 us (0.900)
  local copies, waits for them, and re-layouts: 29.3 us -> 17 us
  other arithmetic: 9.97 us -> 2.78 us
  Pallas kernels: 0 us -> 5.97 us
  waiting for transfers between devices: 5.23 us -> 10.3 us
  matrix products: 32.4 us -> 27.4 us
    slice x16 -> x1, local copies, waits for them, and re-layouts: 10.4 us -> 0.22 us  [the longest x10 8.59 us: stencil(): weights[3 * first + second][:, None, :] * shifted[first:first + rows]]
    pallas_call x0 -> x1, Pallas kernels: none -> 5.97 us  [encode(): pl.pallas_call(functools.partial(encode_kernel, len(chunks), cells), out_...]
    dot_general x2 -> x0, matrix products: 5.16 us -> none  [encode(): jnp.einsum('qkc,kw->qcw', patches, weight.reshape(-1, width), preferred_e...]
    convert_element_type x1 -> x0, other arithmetic: 4.53 us -> none  [stencil(): return total.astype(jnp.bfloat16)]
    ppermute x1, waiting for transfers between devices: 0.01 us -> 3.45 us  [per_device(): after = lax.ppermute(gridded[0][:1], 'band', [(b, a) for a, b in up])]
    reshape x1, local copies, waits for them, and re-layouts: 3.05 us -> 1.14 us  [per_device(): metric = metric.reshape(9, cycle_rows, PATCH * stride)]
    unnamed x50 -> x42, local copies, waits for them, and re-layouts: 4.16 us -> 5.65 us
  transfers between devices with their start and end apart: 13 -> 13, of which waited for: 1 -> 4; matrix products, arithmetic and copies ran while one was open for 44% -> 31% of each run, Pallas kernels for 0% -> 0%
where the time goes in v4:
time: 117 us; the launch traced here: 116 us
  blocking collectives  38.8 us (33%)
  matrix products  27.4 us (23%)
  local copies, waits for them, and re-layouts  17 us (15%)
  starting transfers between devices  13.6 us (12%)
  waiting for transfers between devices  10.3 us (9%)
  Pallas kernels  5.97 us (5%)
  other arithmetic  2.78 us (2%)
    all_to_all x1, blocking collectives, per_device(): lax.all_to_all(outbox, 'band', split_axis=0, concat_axis=0, tiled=True)  38.8 us
    dot_general x8, matrix products, interpolate(): jnp.einsum('rvk,rkj->rvj', field, matrix, preferred_element_type=jnp.floa...  26 us
    ppermute x4, starting transfers between devices, per_device(): lax.ppermute(both[:, :, d * span:(d + 1) * span], 'lon', [(i, (i + d) % n...  6.53 us
    ppermute x4, waiting for transfers between devices, per_device(): lax.ppermute(both[:, :, d * span:(d + 1) * span], 'lon', [(i, (i + d) % n...  6.14 us
    pallas_call x1, Pallas kernels, encode(): pl.pallas_call(functools.partial(encode_kernel, len(chunks), cells), out_...  5.97 us
    unnamed x42, local copies, waits for them, and re-layouts  5.65 us
    convert_element_type x4, local copies, waits for them, and re-layouts, interpolate(): jnp.einsum('rvk,rkj->rvj', field, matrix, preferred_element_type=jnp.floa...  3.99 us
    ppermute x1, starting transfers between devices, per_device(): before = lax.ppermute(gridded[-1][-1:], 'band', up)  3.49 us
  transfers between devices with their start and end apart: 13, of which 4 were waited for; matrix products, arithmetic and copies ran while one was open for 31% of the time, Pallas kernels for 0%

profile of v4, /device:TPU:0, one launch (start us, length us, event | category | flops | bytes accessed | tf_op | source)
XLA Modules:
  0.0 116.3 jit_solution(7557315403824681216)
XLA Ops:
  0.0 0.9 slice_convert_fusion
  0.9 2.9 %fusion.155 = (bf16[4,83,768]{2,0,1:T(4,128)(2,1)S(1)}, bf16[4,83,768]{2,0,1:T(4,128)(2,1)S(1)}, bf16[4,83,768]{2,0,1:T(4,128)(2,1)S(1)}, bf16[4,83,768]{2,0,1:T(4,128)(2,1)S(1)}) fusion(bf16[16,83,768]{2,0,1:T(8,128)(2,1)} %param.6), kind=kLoop, calls=%fused_computation.159 | loop fusion | bytes 4079616 | tf_op jit(solution)/shard_map/slice | solution.py:146
  4.0 0.1 compare_convert_fusion
  4.1 0.1 multiply_multiply_fusion
  4.2 2.7 %fusion.93 = bf16[4,83,768]{2,1,0:T(8,128)(2,1)S(1)} fusion(f32[4,768]{1,0:T(4,128)S(1)} %get-tuple-element.26, f32[4,768]{1,0:T(4,128)S(1)} %get-tuple-element.22, f32[4]{0:T(128)S(1)} %get-tuple-element.36, f32[768]{0:T(1024)S(1)} %add_convert_fusion.2, bf16[4,83,768]{2,0,1:T(4,128)(2,1)S(1)} %get-tuple-element.14), kind=kOutput, calls=%fused_computation.67 | convolution fusion | flops 410772480 | bytes 1047568 | tf_op jit(solution)/shard_map/rvk,rkj->rvj/dot_general | solution.py:38
  6.8 1.0 copy.33
  7.8 0.5 collective-permute-start
  8.3 2.7 %fusion.87 = bf16[4,83,768]{2,1,0:T(8,128)(2,1)S(1)} fusion(f32[4,768]{1,0:T(4,128)S(1)} %get-tuple-element.24, f32[4,768]{1,0:T(4,128)S(1)} %get-tuple-element.20, f32[4]{0:T(128)S(1)} %get-tuple-element.35, f32[768]{0:T(1024)S(1)} %add_convert_fusion.2, bf16[4,83,768]{2,0,1:T(4,128)(2,1)S(1)} %get-tuple-element.13), kind=kOutput, calls=%fused_computation.65 | convolution fusion | flops 410772480 | bytes 1047568 | tf_op jit(solution)/shard_map/rvk,rkj->rvj/dot_general | solution.py:38
  11.0 1.0 copy.36
  12.0 0.1 collective-permute-start.2
  12.0 2.7 %fusion.81 = bf16[4,83,768]{2,1,0:T(8,128)(2,1)S(1)} fusion(f32[4,768]{1,0:T(4,128)S(1)} %get-tuple-element.25, f32[4,768]{1,0:T(4,128)S(1)} %get-tuple-element.21, f32[4]{0:T(128)S(1)} %get-tuple-element.37, f32[768]{0:T(1024)S(1)} %add_convert_fusion.2, bf16[4,83,768]{2,0,1:T(4,128)(2,1)S(1)} %get-tuple-element.12), kind=kOutput, calls=%fused_computation.63 | convolution fusion | flops 410772480 | bytes 1047568 | tf_op jit(solution)/shard_map/rvk,rkj->rvj/dot_general | solution.py:38
  14.7 1.0 copy.39
  15.7 0.5 collective-permute-start.4
  16.2 2.8 %fusion.75 = bf16[4,83,768]{2,1,0:T(8,128)(2,1)S(1)} fusion(f32[4,768]{1,0:T(4,128)S(1)} %get-tuple-element.23, f32[4,768]{1,0:T(4,128)S(1)} %get-tuple-element.19, f32[4]{0:T(128)S(1)} %get-tuple-element.34, f32[768]{0:T(1024)S(1)} %add_convert_fusion.2, bf16[4,83,768]{2,0,1:T(4,128)(2,1)S(1)} %get-tuple-element.11), kind=kOutput, calls=%fused_computation.61 | convolution fusion | flops 410772480 | bytes 1047568 | tf_op jit(solution)/shard_map/rvk,rkj->rvj/dot_general | solution.py:38
  19.0 1.0 copy.42
  20.0 0.1 collective-permute-start.6
  20.0 0.3 reshape.460
  20.4 0.3 copy.84
  20.7 0.0 copy-start.18
  20.7 0.0 copy-start.10
  20.7 0.2 pad.14
  20.9 0.5 collective-permute-start.10
  21.4 0.1 mul.241
  21.5 1.1 reduce-window.6
  22.7 0.2 slice_reduce_fusion
  22.9 0.2 reduce-window.9
  23.1 0.1 add_bitcast_fusion
  23.2 0.1 reduce_sum.12
  23.3 0.0 copy-start.1
  23.3 1.7 %copy.44 = f32[9,16,360]{1,2,0:T(8,128)} copy(f32[9,16,360]{2,1,0:T(8,128)S(1)} %copy-done.10) | data formatting | bytes 414720 | tf_op args[2]
  25.0 2.0 %copy.52 = f32[9,16,4,90]{3,2,1,0:T(4,128)S(1)} copy(f32[9,16,4,90]{1,2,3,0:T(4,128)} %bitcast.55) | data formatting | bytes 414720
  27.0 0.8 pad.13.clone
  27.8 1.1 reshape.459.refs_6_
  28.9 0.0 collective-permute-done
  29.0 0.5 collective-permute-start.11
  29.5 3.9 %copy_add_fusion.3 = bf16[4,83,768]{2,1,0:T(8,128)(2,1)S(1)} fusion(bf16[4,83,768]{2,0,1:T(4,128)(2,1)} %collective-permute-done, bf16[4,83,768]{2,0,1:T(4,128)(2,1)} %copy-done.9, f32[4,768]{1,0:T(4,128)S(1)} %get-tuple-element.22, f32[4]{0:T(128)} %copy-done.17, f32[4,768]{1,0:T(4,128)S(1)} %get-tuple-element.30, f32[768]{0:T(1024)S(1)} %add_convert_fusion.2), kind=kOutput, calls=%fused_computation.75 | convolution fusion | flops 411027456 | bytes 1557520 | tf_op jit(solution)/shard_map/rvk,rkj->rvj/dot_general | solution.py:38
  33.5 0.0 collective-permute-done.2
  33.5 2.6 %collective-permute-start.1 = (bf16[4,83,384]{2,1,0:T(8,128)(2,1)S(1)}, bf16[4,83,384]{2,1,0:T(8,128)(2,1)S(1)}, u32[]{:S(2)}, u32[]{:S(2)}) collective-permute-start(bf16[4,83,384]{2,1,0:T(8,128)(2,1)S(1)} %slice.99), channel_id=1, source_target_pairs={{0,2},{2,0},{1,3},{3,1},{4,6},{6,4},{5,7},{7,5},{8,10},{10,8},{9,1... | collective-permute-start | bytes 764936 | tf_op jit(solution)/shard_map/ppermute | solution.py:152
  36.1 3.8 %copy_add_fusion.2 = bf16[4,83,768]{2,1,0:T(8,128)(2,1)S(1)} fusion(bf16[4,83,768]{2,0,1:T(4,128)(2,1)} %collective-permute-done.2, bf16[4,83,768]{2,0,1:T(4,128)(2,1)S(1)} %copy-done.8, f32[4,768]{1,0:T(4,128)S(1)} %get-tuple-element.20, f32[4]{0:T(128)S(1)} %copy-done.16, f32[4,768]{1,0:T(4,128)S(1)} %get-tuple-element.32, f32[768]{0:T(1024)S(1)} %add_convert_fusion.2), kind=kOutput, calls=%fused_computation.74 | convolution fusion | flops 411027456 | bytes 1557520 | tf_op jit(solution)/shard_map/rvk,rkj->rvj/dot_general | solution.py:38
  39.9 0.0 collective-permute-done.6
  39.9 0.1 collective-permute-start.3
  40.1 3.8 %copy_add_fusion = bf16[4,83,768]{2,1,0:T(8,128)(2,1)S(1)} fusion(bf16[4,83,768]{2,0,1:T(4,128)(2,1)} %collective-permute-done.6, bf16[4,83,768]{2,0,1:T(4,128)(2,1)S(1)} %copy-done.6, f32[4,768]{1,0:T(4,128)S(1)} %get-tuple-element.19, f32[4]{0:T(128)S(1)} %copy-done.14, f32[4,768]{1,0:T(4,128)S(1)} %get-tuple-element.33, f32[768]{0:T(1024)S(1)} %add_convert_fusion.2), kind=kOutput, calls=%fused_computation.72 | convolution fusion | flops 411027456 | bytes 1557520 | tf_op jit(solution)/shard_map/rvk,rkj->rvj/dot_general | solution.py:38
  43.9 0.0 collective-permute-done.4
  43.9 2.1 %collective-permute-start.7 = (bf16[4,83,384]{2,1,0:T(8,128)(2,1)S(1)}, bf16[4,83,384]{2,1,0:T(8,128)(2,1)S(1)}, u32[]{:S(2)}, u32[]{:S(2)}) collective-permute-start(bf16[4,83,384]{2,1,0:T(8,128)(2,1)S(1)} %slice.105), channel_id=1, source_target_pairs={{0,2},{2,0},{1,3},{3,1},{4,6},{6,4},{5,7},{7,5},{8,10},{10,8},{9,1... | collective-permute-start | bytes 764936 | tf_op jit(solution)/shard_map/ppermute | solution.py:152
  46.0 3.7 %copy_add_fusion.1 = bf16[4,83,768]{2,1,0:T(8,128)(2,1)S(1)} fusion(bf16[4,83,768]{2,0,1:T(4,128)(2,1)} %collective-permute-done.4, bf16[4,83,768]{2,0,1:T(4,128)(2,1)S(1)} %copy-done.4, f32[4,768]{1,0:T(4,128)S(1)} %get-tuple-element.21, f32[4]{0:T(128)S(1)} %copy-done.12, f32[4,768]{1,0:T(4,128)S(1)} %get-tuple-element.31, f32[768]{0:T(1024)S(1)} %add_convert_fusion.2), kind=kOutput, calls=%fused_computation.73 | convolution fusion | flops 411027456 | bytes 1557520 | tf_op jit(solution)/shard_map/rvk,rkj->rvj/dot_general | solution.py:38
  49.7 5.0 %collective-permute-done.7 = bf16[4,83,384]{2,1,0:T(8,128)(2,1)S(1)} collective-permute-done((bf16[4,83,384]{2,1,0:T(8,128)(2,1)S(1)}, bf16[4,83,384]{2,1,0:T(8,128)(2,1)S(1)}, u32[]{:S(2)}, u32[]{:S(2)}) %collective-permute-start.7) | collective-permute-done | bytes 255008 | tf_op jit(solution)/shard_map/ppermute | solution.py:152
  54.8 1.8 %collective-permute-start.5 = (bf16[4,83,384]{2,1,0:T(8,128)(2,1)S(1)}, bf16[4,83,384]{2,1,0:T(8,128)(2,1)S(1)}, u32[]{:S(2)}, u32[]{:S(2)}) collective-permute-start(bf16[4,83,384]{2,1,0:T(8,128)(2,1)S(1)} %slice.103), channel_id=1, source_target_pairs={{0,2},{2,0},{1,3},{3,1},{4,6},{6,4},{5,7},{7,5},{8,10},{10,8},{9,1... | collective-permute-start | bytes 764936 | tf_op jit(solution)/shard_map/ppermute | solution.py:152
  56.6 0.0 collective-permute-done.1
  56.6 3.5 %collective-permute-start.8 = (bf16[1,83,384]{2,1,0:T(8,128)(2,1)S(1)}, bf16[1,83,384]{2,1,0:T(8,128)(2,1)S(1)}, u32[]{:S(2)}, u32[]{:S(2)}) collective-permute-start(bf16[1,83,384]{2,1,0:T(8,128)(2,1)S(1)} %slice.106), channel_id=1, source_target_pairs={{0,4},{4,8},{8,12},{1,5},{5,9},{9,13},{2,6},{6,10},{10,14},{3,7},{... | collective-permute-start | bytes 191240 | tf_op jit(solution)/shard_map/ppermute | solution.py:159
  60.1 0.0 collective-permute-done.3
  60.1 1.5 %collective-permute-start.9 = (bf16[1,83,384]{2,1,0:T(8,128)(2,1)S(1)}, bf16[1,83,384]{2,1,0:T(8,128)(2,1)S(1)}, u32[]{:S(2)}, u32[]{:S(2)}) collective-permute-start(bf16[1,83,384]{2,1,0:T(8,128)(2,1)S(1)} %slice.107), channel_id=1, source_target_pairs={{4,0},{8,4},{12,8},{5,1},{9,5},{13,9},{6,2},{10,6},{14,10},{7,3},{... | collective-permute-start | bytes 191240 | tf_op jit(solution)/shard_map/ppermute | solution.py:160
  61.7 1.1 collective-permute-done.5
  62.9 0.0 collective-permute-done.11.refs_10_
  62.9 0.0 collective-permute-done.8.refs_4_
  62.9 3.5 %collective-permute-done.9.refs_5_ = bf16[1,83,384]{2,1,0:T(8,128)(2,1)S(1)} collective-permute-done((bf16[1,83,384]{2,1,0:T(8,128)(2,1)S(1)}, bf16[1,83,384]{2,1,0:T(8,128)(2,1)S(1)}, u32[]{:S(2)}, u32[]{:S(2)}) %collective-permute-start.9) | collective-permute-done | bytes 63776 | tf_op jit(solution)/shard_map/ppermute | solution.py:160
  66.3 6.0 %encode.1 = (bf16[4,90,512]{2,1,0:T(8,128)(2,1)S(1)}, bf16[4,90,512]{2,1,0:T(8,128)(2,1)}) custom-call(bf16[4,83,384]{2,1,0:T(8,128)(2,1)S(1)} %slice_add_fusion.3.refs_0_, bf16[4,83,384]{2,1,0:T(8,128)(2,1)S(1)} %slice_add_fusion.2.refs_1_, bf16[4,83,384]{2,1,0:T(8,128)(2,1)S(1)} %slice_add_fusion.1.refs_2_, bf16[4,83,384]{2,1,0:T(8,128)(2,1)S(1)} %slice_add_fusion.refs_3_, ...), custom_call_target="tpu_custom_call" | custom-call | tf_op jit(solution)/shard_map/encode/pallas_call | solution.py:100
  72.3 0.7 copy-done
  73.1 0.1 eq.82
  73.2 1.1 reshape.463
  74.3 0.7 collective-permute-done.12
  75.0 0.1 reshape.464
  75.1 1.3 %fusion.49 = bf16[1440,512]{1,0:T(8,128)(2,1)S(1)} fusion(s32[720]{0:T(1024)S(1)} %eq.82, bf16[360,512]{1,0:T(8,128)(2,1)S(1)} %reshape.464, bf16[360,512]{1,0:T(8,128)(2,1)S(1)} %reshape.463), kind=kOutput, calls=%fused_computation.50 | convolution fusion | flops 1064931840 | bytes 2214720 | tf_op jit(solution)/shard_map/dot_general | solution.py:192
  76.4 38.8 %all_to_all.5 = bf16[4,360,512]{2,1,0:T(8,128)(2,1)S(1)} all-to-all(bf16[4,360,512]{2,1,0:T(8,128)(2,1)S(1)} %bitcast.58), channel_id=1, replica_groups=mesh['groups'=2,'band'=4,'lon'=2,'mp'=2] {'band'}, dimensions={0} | all-to-all | bytes 2949120 | tf_op jit(solution)/shard_map/all_to_all | solution.py:196
  115.2 1.1 copy.87
  (61 shorter events, 0.6 us)
Async XLA Ops:
  0.9 5.9 %copy-start.17 = (f32[4]{0:T(128)}, f32[4]{0:T(128)S(1)}, u32[]{:S(2)}) copy-start(f32[4]{0:T(128)S(1)} %get-tuple-element.36) | copy-start | bytes 52
  0.9 7.4 %copy-start.15 = (f32[4]{0:T(128)}, f32[4]{0:T(128)S(1)}, u32[]{:S(2)}) copy-start(f32[4]{0:T(128)S(1)} %get-tuple-element.35) | copy-start | bytes 52
  0.9 11.1 %copy-start.11 = (f32[4]{0:T(128)}, f32[4]{0:T(128)S(1)}, u32[]{:S(2)}) copy-start(f32[4]{0:T(128)S(1)} %get-tuple-element.37) | copy-start | bytes 52
  0.9 15.3 %copy-start.13 = (f32[4]{0:T(128)}, f32[4]{0:T(128)S(1)}, u32[]{:S(2)}) copy-start(f32[4]{0:T(128)S(1)} %get-tuple-element.34) | copy-start | bytes 52
  3.8 3.0 %copy-start.9 = (bf16[4,83,768]{2,0,1:T(4,128)(2,1)}, bf16[4,83,768]{2,0,1:T(4,128)(2,1)S(1)}, u32[]{:S(2)}) copy-start(bf16[4,83,768]{2,0,1:T(4,128)(2,1)S(1)} %get-tuple-element.14) | copy-start | bytes 1529860
  3.9 4.4 %copy-start.7 = (bf16[4,83,768]{2,0,1:T(4,128)(2,1)}, bf16[4,83,768]{2,0,1:T(4,128)(2,1)S(1)}, u32[]{:S(2)}) copy-start(bf16[4,83,768]{2,0,1:T(4,128)(2,1)S(1)} %get-tuple-element.13) | copy-start | bytes 1529860
  3.9 8.2 %copy-start.3 = (bf16[4,83,768]{2,0,1:T(4,128)(2,1)}, bf16[4,83,768]{2,0,1:T(4,128)(2,1)S(1)}, u32[]{:S(2)}) copy-start(bf16[4,83,768]{2,0,1:T(4,128)(2,1)S(1)} %get-tuple-element.12) | copy-start | bytes 1529860
  3.9 12.3 %copy-start.5 = (bf16[4,83,768]{2,0,1:T(4,128)(2,1)}, bf16[4,83,768]{2,0,1:T(4,128)(2,1)S(1)}, u32[]{:S(2)}) copy-start(bf16[4,83,768]{2,0,1:T(4,128)(2,1)S(1)} %get-tuple-element.11) | copy-start | bytes 1529860
  7.8 21.1 %collective-permute-start = (bf16[4,83,768]{2,0,1:T(4,128)(2,1)}, bf16[4,83,768]{2,0,1:T(4,128)(2,1)}, u32[]{:S(2)}, u32[]{:S(2)}) collective-permute-start(bf16[4,83,768]{2,0,1:T(4,128)(2,1)} %copy.33), channel_id=1, source_target_pairs={{0,1},{1,0},{2,3},{3,2},{4,5},{5,4},{6,7},{7,6},{8,9},{9,8},{10,11... | collective-permute-start | bytes 1529864 | tf_op jit(solution)/shard_map/ppermute | solution.py:16
  12.0 21.5 %collective-permute-start.2 = (bf16[4,83,768]{2,0,1:T(4,128)(2,1)}, bf16[4,83,768]{2,0,1:T(4,128)(2,1)}, u32[]{:S(2)}, u32[]{:S(2)}) collective-permute-start(bf16[4,83,768]{2,0,1:T(4,128)(2,1)} %copy.36), channel_id=1, source_target_pairs={{0,1},{1,0},{2,3},{3,2},{4,5},{5,4},{6,7},{7,6},{8,9},{9,8},{10,11... | collective-permute-start | bytes 1529864 | tf_op jit(solution)/shard_map/ppermute | solution.py:16
  15.7 28.2 %collective-permute-start.4 = (bf16[4,83,768]{2,0,1:T(4,128)(2,1)}, bf16[4,83,768]{2,0,1:T(4,128)(2,1)}, u32[]{:S(2)}, u32[]{:S(2)}) collective-permute-start(bf16[4,83,768]{2,0,1:T(4,128)(2,1)} %copy.39), channel_id=1, source_target_pairs={{0,1},{1,0},{2,3},{3,2},{4,5},{5,4},{6,7},{7,6},{8,9},{9,8},{10,11... | collective-permute-start | bytes 1529864 | tf_op jit(solution)/shard_map/ppermute | solution.py:16
  16.2 3.9 %copy-start.2 = (bf16[1328,512]{1,0:T(8,128)(2,1)S(1)}, bf16[1328,512]{1,0:T(8,128)(2,1)}, u32[]{:S(2)}) copy-start(bf16[1328,512]{1,0:T(8,128)(2,1)} %param.9) | copy-start | bytes 4079620
  20.0 19.9 %collective-permute-start.6 = (bf16[4,83,768]{2,0,1:T(4,128)(2,1)}, bf16[4,83,768]{2,0,1:T(4,128)(2,1)}, u32[]{:S(2)}, u32[]{:S(2)}) collective-permute-start(bf16[4,83,768]{2,0,1:T(4,128)(2,1)} %copy.42), channel_id=1, source_target_pairs={{0,1},{1,0},{2,3},{3,2},{4,5},{5,4},{6,7},{7,6},{8,9},{9,8},{10,11... | collective-permute-start | bytes 1529864 | tf_op jit(solution)/shard_map/ppermute | solution.py:16
  20.7 0.7 copy-start.18
  20.7 2.6 %copy-start.10 = (f32[9,16,360]{2,1,0:T(8,128)S(1)}, f32[9,16,360]{2,1,0:T(8,128)}, u32[]{:S(2)}) copy-start(f32[9,16,360]{2,1,0:T(8,128)} %param.8) | copy-start | bytes 622084
  20.9 45.5 %collective-permute-start.10 = (bf16[4,4,96,512]{3,2,1,0:T(8,128)(2,1)S(1)}, bf16[4,4,96,512]{3,2,1,0:T(8,128)(2,1)S(1)}, u32[]{:S(2)}, u32[]{:S(2)}) collective-permute-start(bf16[4,4,96,512]{3,2,1,0:T(8,128)(2,1)S(1)} %pad.14), channel_id=1, source_target_pairs={{0,1},{1,0},{2,3},{3,2},{4,5},{5,4},{6,7},{7,6},{8,9},{9,8},{10,11... | collective-permute-start | bytes 4718600 | tf_op jit(solution)/shard_map/ppermute | solution.py:16
  23.3 5.7 %copy-start.1 = (f32[512]{0:T(512)S(1)}, f32[512]{0:T(512)}, u32[]{:S(2)}) copy-start(f32[512]{0:T(512)} %param.10) | copy-start | bytes 6148
  29.0 33.9 %collective-permute-start.11 = (f32[1,512]{1,0:T(1,128)S(1)}, f32[1,512]{1,0:T(1,128)S(1)}, u32[]{:S(2)}, u32[]{:S(2)}) collective-permute-start(f32[1,512]{1,0:T(1,128)S(1)} %bitcast.53), channel_id=1, source_target_pairs={{0,1},{1,0},{2,3},{3,2},{4,5},{5,4},{6,7},{7,6},{8,9},{9,8},{10,11... | collective-permute-start | bytes 6152 | tf_op jit(solution)/shard_map/ppermute | solution.py:16
  29.5 6.6 %copy-start.8 = (bf16[4,83,768]{2,0,1:T(4,128)(2,1)S(1)}, bf16[4,83,768]{2,0,1:T(4,128)(2,1)}, u32[]{:S(2)}) copy-start(bf16[4,83,768]{2,0,1:T(4,128)(2,1)} %copy-done.7) | copy-start | bytes 1529860
  29.5 6.6 %copy-start.16 = (f32[4]{0:T(128)S(1)}, f32[4]{0:T(128)}, u32[]{:S(2)}) copy-start(f32[4]{0:T(128)} %copy-done.15) | copy-start | bytes 52
  33.5 23.1 %collective-permute-start.1 = (bf16[4,83,384]{2,1,0:T(8,128)(2,1)S(1)}, bf16[4,83,384]{2,1,0:T(8,128)(2,1)S(1)}, u32[]{:S(2)}, u32[]{:S(2)}) collective-permute-start(bf16[4,83,384]{2,1,0:T(8,128)(2,1)S(1)} %slice.99), channel_id=1, source_target_pairs={{0,2},{2,0},{1,3},{3,1},{4,6},{6,4},{5,7},{7,5},{8,10},{10,8},{9,1... | collective-permute-start | bytes 764936 | tf_op jit(solution)/shard_map/ppermute | solution.py:152
  36.1 4.0 %copy-start.6 = (bf16[4,83,768]{2,0,1:T(4,128)(2,1)S(1)}, bf16[4,83,768]{2,0,1:T(4,128)(2,1)}, u32[]{:S(2)}) copy-start(bf16[4,83,768]{2,0,1:T(4,128)(2,1)} %copy-done.5) | copy-start | bytes 1529860
  36.1 4.0 %copy-start.14 = (f32[4]{0:T(128)S(1)}, f32[4]{0:T(128)}, u32[]{:S(2)}) copy-start(f32[4]{0:T(128)} %copy-done.13) | copy-start | bytes 52
  39.9 20.2 %collective-permute-start.3 = (bf16[4,83,384]{2,1,0:T(8,128)(2,1)S(1)}, bf16[4,83,384]{2,1,0:T(8,128)(2,1)S(1)}, u32[]{:S(2)}, u32[]{:S(2)}) collective-permute-start(bf16[4,83,384]{2,1,0:T(8,128)(2,1)S(1)} %slice.101), channel_id=1, source_target_pairs={{0,2},{2,0},{1,3},{3,1},{4,6},{6,4},{5,7},{7,5},{8,10},{10,8},{9,1... | collective-permute-start | bytes 764936 | tf_op jit(solution)/shard_map/ppermute | solution.py:152
  40.1 5.9 %copy-start.4 = (bf16[4,83,768]{2,0,1:T(4,128)(2,1)S(1)}, bf16[4,83,768]{2,0,1:T(4,128)(2,1)}, u32[]{:S(2)}) copy-start(bf16[4,83,768]{2,0,1:T(4,128)(2,1)} %copy-done.3) | copy-start | bytes 1529860
  40.1 5.9 %copy-start.12 = (f32[4]{0:T(128)S(1)}, f32[4]{0:T(128)}, u32[]{:S(2)}) copy-start(f32[4]{0:T(128)} %copy-done.11) | copy-start | bytes 52
  43.9 10.9 %collective-permute-start.7 = (bf16[4,83,384]{2,1,0:T(8,128)(2,1)S(1)}, bf16[4,83,384]{2,1,0:T(8,128)(2,1)S(1)}, u32[]{:S(2)}, u32[]{:S(2)}) collective-permute-start(bf16[4,83,384]{2,1,0:T(8,128)(2,1)S(1)} %slice.105), channel_id=1, source_target_pairs={{0,2},{2,0},{1,3},{3,1},{4,6},{6,4},{5,7},{7,5},{8,10},{10,8},{9,1... | collective-permute-start | bytes 764936 | tf_op jit(solution)/shard_map/ppermute | solution.py:152
  54.8 8.1 %collective-permute-start.5 = (bf16[4,83,384]{2,1,0:T(8,128)(2,1)S(1)}, bf16[4,83,384]{2,1,0:T(8,128)(2,1)S(1)}, u32[]{:S(2)}, u32[]{:S(2)}) collective-permute-start(bf16[4,83,384]{2,1,0:T(8,128)(2,1)S(1)} %slice.103), channel_id=1, source_target_pairs={{0,2},{2,0},{1,3},{3,1},{4,6},{6,4},{5,7},{7,5},{8,10},{10,8},{9,1... | collective-permute-start | bytes 764936 | tf_op jit(solution)/shard_map/ppermute | solution.py:152
  56.6 6.3 %collective-permute-start.8 = (bf16[1,83,384]{2,1,0:T(8,128)(2,1)S(1)}, bf16[1,83,384]{2,1,0:T(8,128)(2,1)S(1)}, u32[]{:S(2)}, u32[]{:S(2)}) collective-permute-start(bf16[1,83,384]{2,1,0:T(8,128)(2,1)S(1)} %slice.106), channel_id=1, source_target_pairs={{0,4},{4,8},{8,12},{1,5},{5,9},{9,13},{2,6},{6,10},{10,14},{3,7},{... | collective-permute-start | bytes 191240 | tf_op jit(solution)/shard_map/ppermute | solution.py:159
  60.1 6.2 %collective-permute-start.9 = (bf16[1,83,384]{2,1,0:T(8,128)(2,1)S(1)}, bf16[1,83,384]{2,1,0:T(8,128)(2,1)S(1)}, u32[]{:S(2)}, u32[]{:S(2)}) collective-permute-start(bf16[1,83,384]{2,1,0:T(8,128)(2,1)S(1)} %slice.107), channel_id=1, source_target_pairs={{4,0},{8,4},{12,8},{5,1},{9,5},{13,9},{6,2},{10,6},{14,10},{7,3},{... | collective-permute-start | bytes 191240 | tf_op jit(solution)/shard_map/ppermute | solution.py:160
  72.3 0.7 copy-start
  73.0 1.9 %collective-permute-start.12 = (bf16[4,90,512]{2,1,0:T(8,128)(2,1)}, bf16[4,90,512]{2,1,0:T(8,128)(2,1)S(1)}, u32[]{:S(2)}, u32[]{:S(2)}) collective-permute-start(bf16[4,90,512]{2,1,0:T(8,128)(2,1)} %get-tuple-element.8), channel_id=1, source_target_pairs={{0,1},{1,0},{2,3},{3,2},{4,5},{5,4},{6,7},{7,6},{8,9},{9,8},{10,11... | collective-permute-start | bytes 1105928 | tf_op jit(solution)/shard_map/ppermute | solution.py:16

commit v5 on v4

--- a/solution.py
+++ b/solution.py
@@ -142,17 +142,24 @@
     step = cycle_rows // CHUNKS
     span = PATCH * stride
     gridded = [None] * CHUNKS
-    for chunk in [0, CHUNKS - 1] + list(range(1, CHUNKS - 1)):
+    order = [0, CHUNKS - 1] + list(range(1, CHUNKS - 1))
+    messages = {}
+    for index, chunk in enumerate(order):
         field = cycle_field[chunk * step : (chunk + 1) * step]
         length = cycle_length[chunk * step : (chunk + 1) * step]
+        if index >= 2:
+            earlier_chunk = order[index - 2]
+            length, messages[earlier_chunk] = lax.optimization_barrier(
+                (length, messages[earlier_chunk])
+            )
         sent = swap(interpolate(field, length, kstart, other_cols))
         both = interpolate(field, length, kstart, own_cols) + sent
-        total = both[:, :, :span]
+        messages[chunk] = [both[:, :, d * span : (d + 1) * span] for d in range(nlon)]
+    for chunk in order:
+        total = messages[chunk][0]
         for d in range(1, nlon):
             total = total + lax.ppermute(
-                both[:, :, d * span : (d + 1) * span],
-                "lon",
-                [(i, (i + d) % nlon) for i in range(nlon)],
+                messages[chunk][d], "lon", [(i, (i + d) % nlon) for i in range(nlon)]
             )
         gridded[chunk] = total
     up = [(i, i + 1) for i in range(bands - 1)]

time: 117 us -> 114 us (0.974)
  waiting for transfers between devices: 10.3 us -> 3.32 us
  other arithmetic: 2.78 us -> 7.17 us
  local copies, waits for them, and re-layouts: 17 us -> 19.8 us
  matrix products: 27.4 us -> 25.3 us
  starting transfers between devices: 13.6 us -> 12.3 us
    ppermute x4, waiting for transfers between devices: 6.14 us -> 0.01 us  [per_device(): lax.ppermute(messages[chunk][d], 'lon', [(i, (i + d) % nlon) for i in ran...]
    add x4, other arithmetic: 0.16 us -> 4.26 us  [per_device(): total + lax.ppermute(messages[chunk][d], 'lon', [(i, (i + d) % nlon) for...]
    slice x5, local copies, waits for them, and re-layouts: 0.33 us -> 3.55 us  [the longest x4 3.34 us: per_device(): messages[chunk] = [both[:, :, d * span:(d + 1) * span] for d in range(nlon)]]
    dot_general x8, matrix products: 26 us -> 24 us  [interpolate(): jnp.einsum('rvk,rkj->rvj', field, matrix, preferred_element_type=jnp.floa...]
    convert_element_type x4, local copies, waits for them, and re-layouts: 3.99 us -> 2.36 us  [interpolate(): jnp.einsum('rvk,rkj->rvj', field, matrix, preferred_element_type=jnp.floa...]
    ppermute x4, starting transfers between devices: 6.53 us -> 5.01 us  [per_device(): lax.ppermute(messages[chunk][d], 'lon', [(i, (i + d) % nlon) for i in ran...]
    unnamed x42 -> x32, local copies, waits for them, and re-layouts: 5.65 us -> 5.72 us
  transfers between devices with their start and end apart: 13 -> 13, of which waited for: 4 -> 2; matrix products, arithmetic and copies ran while one was open for 31% -> 35% of each run, Pallas kernels for 0% -> 0%
where the time goes in v5:
time: 114 us; the launch traced here: 113 us
  blocking collectives  38.8 us (34%)
  matrix products  25.3 us (22%)
  local copies, waits for them, and re-layouts  19.8 us (17%)
  starting transfers between devices  12.3 us (11%)
  other arithmetic  7.17 us (6%)
  Pallas kernels  5.96 us (5%)
  waiting for transfers between devices  3.32 us (3%)
    all_to_all x1, blocking collectives, per_device(): lax.all_to_all(outbox, 'band', split_axis=0, concat_axis=0, tiled=True)  38.8 us
    dot_general x8, matrix products, interpolate(): jnp.einsum('rvk,rkj->rvj', field, matrix, preferred_element_type=jnp.floa...  24 us
    pallas_call x1, Pallas kernels, encode(): pl.pallas_call(functools.partial(encode_kernel, len(chunks), cells), out_...  5.96 us
    unnamed x32, local copies, waits for them, and re-layouts  5.72 us
    ppermute x4, starting transfers between devices, per_device(): lax.ppermute(messages[chunk][d], 'lon', [(i, (i + d) % nlon) for i in ran...  5.01 us
    add x4, other arithmetic, per_device(): total + lax.ppermute(messages[chunk][d], 'lon', [(i, (i + d) % nlon) for...  4.26 us
    slice x1, local copies, waits for them, and re-layouts, per_device(): field = cycle_field[chunk * step:(chunk + 1) * step]  4.01 us
    ppermute x1, starting transfers between devices, per_device(): before = lax.ppermute(gridded[-1][-1:], 'band', up)  3.98 us
  transfers between devices with their start and end apart: 13, of which 2 were waited for; matrix products, arithmetic and copies ran while one was open for 35% of the time, Pallas kernels for 0%

profile of v5, /device:TPU:0, one launch (start us, length us, event | category | flops | bytes accessed | tf_op | source)
XLA Modules:
  0.0 113.1 jit_solution(4487853137293575966)
XLA Ops:
  0.0 0.9 slice_convert_fusion
  0.9 4.0 %fusion.155 = (bf16[4,83,768]{2,0,1:T(4,128)(2,1)}, bf16[4,83,768]{2,0,1:T(4,128)(2,1)S(1)}, bf16[4,83,768]{2,0,1:T(4,128)(2,1)}, bf16[4,83,768]{2,0,1:T(4,128)(2,1)S(1)}) fusion(bf16[16,83,768]{2,0,1:T(8,128)(2,1)} %param.6), kind=kLoop, calls=%fused_computation.155 | loop fusion | bytes 4079616 | tf_op jit(solution)/shard_map/slice | solution.py:148
  5.0 0.1 compare_convert_fusion.1
  5.1 0.1 multiply_multiply_fusion.2
  5.1 2.7 %fusion.93 = bf16[4,83,768]{2,1,0:T(8,128)(2,1)S(1)} fusion(f32[4,768]{1,0:T(4,128)S(1)} %get-tuple-element.42, f32[4,768]{1,0:T(4,128)S(1)} %get-tuple-element.40, f32[4]{0:T(128)S(1)} %get-tuple-element.51, f32[768]{0:T(1024)S(1)} %add_convert_fusion.2, bf16[4,83,768]{2,0,1:T(4,128)(2,1)S(1)} %get-tuple-element.26), kind=kOutput, calls=%fused_computation.67 | convolution fusion | flops 410772480 | bytes 1047568 | tf_op jit(solution)/shard_map/rvk,rkj->rvj/dot_general | solution.py:38
  7.8 1.0 copy.33
  8.8 0.5 collective-permute-start
  9.3 2.7 %fusion.81 = bf16[4,83,768]{2,1,0:T(8,128)(2,1)S(1)} fusion(f32[4,768]{1,0:T(4,128)S(1)} %get-tuple-element.41, f32[4,768]{1,0:T(4,128)S(1)} %get-tuple-element.39, f32[4]{0:T(128)S(1)} %get-tuple-element.50, f32[768]{0:T(1024)S(1)} %add_convert_fusion.2, bf16[4,83,768]{2,0,1:T(4,128)(2,1)S(1)} %get-tuple-element.24), kind=kOutput, calls=%fused_computation.63 | convolution fusion | flops 410772480 | bytes 1047568 | tf_op jit(solution)/shard_map/rvk,rkj->rvj/dot_general | solution.py:38
  11.9 1.0 copy.39
  12.9 0.1 collective-permute-start.4
  13.0 0.3 reshape.460
  13.3 0.3 copy.84
  13.6 0.2 pad.14
  13.7 0.5 collective-permute-start.10
  14.3 1.3 %reduce-window.6 = s32[4,6,128]{2,1,0:T(8,128)S(1)} reduce-window(s32[4,6,128]{2,1,0:T(8,128)S(1)} %reshape.467, s32[]{:T(128)} %constant.97.clone.1), window={size=1x1x128 pad=0_0x0_0x127_0}, to_apply=%region_0.1 | reduce-window | flops 390144 | bytes 24580 | tf_op jit(solution)/shard_map/reduce-window
  15.7 0.2 slice_reduce_fusion
  15.9 0.2 reduce-window.9
  16.1 0.1 add_bitcast_fusion
  16.2 3.9 %copy_add_fusion.3 = bf16[4,83,768]{2,1,0:T(8,128)(2,1)S(1)} fusion(bf16[4,83,768]{2,0,1:T(4,128)(2,1)} %collective-permute-done, bf16[4,83,768]{2,0,1:T(4,128)(2,1)} %copy-done.11, f32[4,768]{1,0:T(4,128)S(1)} %get-tuple-element.40, f32[4]{0:T(128)S(1)} %get-tuple-element.51, f32[4,768]{1,0:T(4,128)S(1)} %get-tuple-element.46, f32[768]{0:T(1024)S(1)} %add_convert_fusion.2), kind=kOutput, calls=%fused_computation.75 | convolution fusion | flops 411027456 | bytes 1557520 | tf_op jit(solution)/shard_map/rvk,rkj->rvj/dot_general | solution.py:38
  20.1 0.9 fusion.157
  21.0 3.8 %copy_add_fusion.1 = bf16[4,83,768]{2,1,0:T(8,128)(2,1)S(1)} fusion(bf16[4,83,768]{2,0,1:T(4,128)(2,1)} %collective-permute-done.4, bf16[4,83,768]{2,0,1:T(4,128)(2,1)S(1)} %copy-done.10, f32[4,768]{1,0:T(4,128)S(1)} %get-tuple-element.39, f32[4]{0:T(128)S(1)} %get-tuple-element.50, f32[4,768]{1,0:T(4,128)S(1)} %get-tuple-element.47, ...), kind=kOutput, calls=%fused_computation.73 | convolution fusion | flops 411027456 | bytes 1557520 | tf_op jit(solution)/shard_map/rvk,rkj->rvj/dot_general | solution.py:38
  24.8 0.9 fusion.156
  25.7 0.1 multiply_multiply_fusion
  25.8 0.1 compare_convert_fusion
  25.8 2.9 %collective-permute-start.1 = (bf16[4,83,384]{2,1,0:T(8,128)(2,1)}, bf16[4,83,384]{2,1,0:T(8,128)(2,1)}, u32[]{:S(2)}, u32[]{:S(2)}) collective-permute-start(bf16[4,83,384]{2,1,0:T(8,128)(2,1)} %get-tuple-element.14), channel_id=1, source_target_pairs={{0,2},{2,0},{1,3},{3,1},{4,6},{6,4},{5,7},{7,5},{8,10},{10,8},{9,1... | collective-permute-start | bytes 764936 | tf_op jit(solution)/shard_map/ppermute | solution.py:161
  28.8 2.7 %fusion.87 = bf16[4,83,768]{2,1,0:T(8,128)(2,1)S(1)} fusion(f32[4,768]{1,0:T(4,128)S(1)} %get-tuple-element.36, f32[4,768]{1,0:T(4,128)S(1)} %get-tuple-element.34, f32[4]{0:T(128)S(1)} %convert_element_type.201, f32[768]{0:T(1024)S(1)} %add_convert_fusion.2, bf16[4,83,768]{2,0,1:T(4,128)(2,1)S(1)} %copy-done.8), kind=kOutput, calls=%fused_computation.65 | convolution fusion | flops 410772480 | bytes 1047568 | tf_op jit(solution)/shard_map/rvk,rkj->rvj/dot_general | solution.py:38
  31.4 0.2 copy.36
  31.6 0.1 collective-permute-start.2
  31.7 2.7 %fusion.75 = bf16[4,83,768]{2,1,0:T(8,128)(2,1)S(1)} fusion(f32[4,768]{1,0:T(4,128)S(1)} %get-tuple-element.35, f32[4,768]{1,0:T(4,128)S(1)} %get-tuple-element.33, f32[4]{0:T(128)S(1)} %convert_element_type.217, f32[768]{0:T(1024)S(1)} %add_convert_fusion.2, bf16[4,83,768]{2,0,1:T(4,128)(2,1)S(1)} %copy-done.7), kind=kOutput, calls=%fused_computation.61 | convolution fusion | flops 410772480 | bytes 1047568 | tf_op jit(solution)/shard_map/rvk,rkj->rvj/dot_general | solution.py:38
  34.4 0.2 copy.42
  34.6 0.6 collective-permute-start.5
  35.2 0.0 collective-permute-start.7
  35.2 2.9 %copy_add_fusion.2 = bf16[4,83,768]{2,1,0:T(8,128)(2,1)S(1)} fusion(bf16[4,83,768]{2,0,1:T(4,128)(2,1)S(1)} %collective-permute-done.2, bf16[4,83,768]{2,0,1:T(4,128)(2,1)S(1)} %copy-done.8, f32[4,768]{1,0:T(4,128)S(1)} %get-tuple-element.34, f32[4]{0:T(128)S(1)} %convert_element_type.201, f32[4,768]{1,0:T(4,128)S(1)} %get-tuple-element.48, ...), kind=kOutput, calls=%fused_computation.74 | convolution fusion | flops 411027456 | bytes 1557520 | tf_op jit(solution)/shard_map/rvk,rkj->rvj/dot_general | solution.py:38
  38.1 0.0 copy-start.3
  38.1 0.8 slice.101
  38.9 2.0 %collective-permute-start.3 = (bf16[4,83,384]{2,1,0:T(8,128)(2,1)}, bf16[4,83,384]{2,1,0:T(8,128)(2,1)}, u32[]{:S(2)}, u32[]{:S(2)}) collective-permute-start(bf16[4,83,384]{2,1,0:T(8,128)(2,1)} %slice.101), channel_id=1, source_target_pairs={{0,2},{2,0},{1,3},{3,1},{4,6},{6,4},{5,7},{7,5},{8,10},{10,8},{9,1... | collective-permute-start | bytes 764936 | tf_op jit(solution)/shard_map/ppermute | solution.py:161
  40.9 2.7 %copy_add_fusion = bf16[4,83,768]{2,1,0:T(8,128)(2,1)S(1)} fusion(bf16[4,83,768]{2,0,1:T(4,128)(2,1)S(1)} %collective-permute-done.5, bf16[4,83,768]{2,0,1:T(4,128)(2,1)S(1)} %copy-done.7, f32[4,768]{1,0:T(4,128)S(1)} %get-tuple-element.33, f32[4]{0:T(128)S(1)} %convert_element_type.217, f32[4,768]{1,0:T(4,128)S(1)} %get-tuple-element.49, ...), kind=kOutput, calls=%fused_computation.72 | convolution fusion | flops 411027456 | bytes 1557520 | tf_op jit(solution)/shard_map/rvk,rkj->rvj/dot_general | solution.py:38
  43.6 0.8 slice.105
  44.4 0.1 copy-done.5
  44.5 0.0 collective-permute-start.6
  44.6 0.1 mul.241
  44.6 0.1 reduce_sum.12
  44.7 0.0 copy-start.1
  44.8 1.7 %copy.44 = f32[9,16,360]{1,2,0:T(8,128)} copy(f32[9,16,360]{2,1,0:T(8,128)S(1)} %copy-done.12) | data formatting | bytes 414720 | tf_op args[2]
  46.5 2.0 %copy.52 = f32[9,16,4,90]{3,2,1,0:T(4,128)S(1)} copy(f32[9,16,4,90]{1,2,3,0:T(4,128)} %bitcast.55) | data formatting | bytes 414720
  48.5 0.8 pad.13.clone
  49.3 1.1 %reshape.459.refs_6_ = f32[9,16,384]{2,1,0:T(8,128)S(1)} reshape(f32[9,16,4,96]{3,2,1,0:T(4,128)} %pad.13.clone) | data formatting | bytes 442368 | tf_op jit(solution)/shard_map/reshape | solution.py:131
  50.5 0.1 collective-permute-start.11
  50.5 1.2 %add.252.refs_3_ = bf16[4,83,384]{2,1,0:T(8,128)(2,1)S(1)} add(bf16[4,83,384]{2,1,0:T(8,128)(2,1)} %get-tuple-element.17, bf16[4,83,384]{2,1,0:T(8,128)(2,1)} %collective-permute-done.7) | non-fusion elementwise | flops 127488 | bytes 764928 | tf_op jit(solution)/shard_map/add | solution.py:161
  51.7 4.0 %collective-permute-start.8 = (bf16[1,83,384]{2,1,0:T(8,128)(2,1)S(1)}, bf16[1,83,384]{2,1,0:T(8,128)(2,1)S(1)}, u32[]{:S(2)}, u32[]{:S(2)}) collective-permute-start(bf16[1,83,384]{2,1,0:T(8,128)(2,1)S(1)} %slice.106), channel_id=1, source_target_pairs={{0,4},{4,8},{8,12},{1,5},{5,9},{9,13},{2,6},{6,10},{10,14},{3,7},{... | collective-permute-start | bytes 191240 | tf_op jit(solution)/shard_map/ppermute | solution.py:166
  55.7 1.1 add.246.refs_0_
  56.9 1.6 %collective-permute-start.9 = (bf16[1,83,384]{2,1,0:T(8,128)(2,1)S(1)}, bf16[1,83,384]{2,1,0:T(8,128)(2,1)S(1)}, u32[]{:S(2)}, u32[]{:S(2)}) collective-permute-start(bf16[1,83,384]{2,1,0:T(8,128)(2,1)S(1)} %slice.107), channel_id=1, source_target_pairs={{4,0},{8,4},{12,8},{5,1},{9,5},{13,9},{6,2},{10,6},{14,10},{7,3},{... | collective-permute-start | bytes 191240 | tf_op jit(solution)/shard_map/ppermute | solution.py:167
  58.4 1.0 slice_add_fusion.1.refs_1_
  59.4 1.0 slice_add_fusion.refs_2_
  60.5 2.6 %collective-permute-done.9.refs_5_ = bf16[1,83,384]{2,1,0:T(8,128)(2,1)S(1)} collective-permute-done((bf16[1,83,384]{2,1,0:T(8,128)(2,1)S(1)}, bf16[1,83,384]{2,1,0:T(8,128)(2,1)S(1)}, u32[]{:S(2)}, u32[]{:S(2)}) %collective-permute-start.9) | collective-permute-done | bytes 63776 | tf_op jit(solution)/shard_map/ppermute | solution.py:167
  63.0 6.0 %encode.1 = (bf16[4,90,512]{2,1,0:T(8,128)(2,1)S(1)}, bf16[4,90,512]{2,1,0:T(8,128)(2,1)}) custom-call(bf16[4,83,384]{2,1,0:T(8,128)(2,1)S(1)} %add.246.refs_0_, bf16[4,83,384]{2,1,0:T(8,128)(2,1)S(1)} %slice_add_fusion.1.refs_1_, bf16[4,83,384]{2,1,0:T(8,128)(2,1)S(1)} %slice_add_fusion.refs_2_, bf16[4,83,384]{2,1,0:T(8,128)(2,1)S(1)} %add.252.refs_3_, ...), custom_call_target="tpu_custom_call" | custom-call | tf_op jit(solution)/shard_map/encode/pallas_call | solution.py:100
  69.0 0.8 copy-done
  69.8 0.1 eq.82
  69.9 1.1 reshape.463
  71.0 0.7 collective-permute-done.12
  71.7 0.1 reshape.464
  71.8 1.3 %fusion.49 = bf16[1440,512]{1,0:T(8,128)(2,1)S(1)} fusion(s32[720]{0:T(1024)S(1)} %eq.82, bf16[360,512]{1,0:T(8,128)(2,1)S(1)} %reshape.464, bf16[360,512]{1,0:T(8,128)(2,1)S(1)} %reshape.463), kind=kOutput, calls=%fused_computation.50 | convolution fusion | flops 1064931840 | bytes 2214720 | tf_op jit(solution)/shard_map/dot_general | solution.py:199
  73.1 38.8 %all_to_all.5 = bf16[4,360,512]{2,1,0:T(8,128)(2,1)S(1)} all-to-all(bf16[4,360,512]{2,1,0:T(8,128)(2,1)S(1)} %bitcast.58), channel_id=1, replica_groups=mesh['groups'=2,'band'=4,'lon'=2,'mp'=2] {'band'}, dimensions={0} | all-to-all | bytes 2949120 | tf_op jit(solution)/shard_map/all_to_all | solution.py:203
  111.9 1.1 copy.87
  (55 shorter events, 0.3 us)
Async XLA Ops:
  4.9 2.9 %copy-start.11 = (bf16[4,83,768]{2,0,1:T(4,128)(2,1)}, bf16[4,83,768]{2,0,1:T(4,128)(2,1)S(1)}, u32[]{:S(2)}) copy-start(bf16[4,83,768]{2,0,1:T(4,128)(2,1)S(1)} %get-tuple-element.26) | copy-start | bytes 1529860
  4.9 4.4 %copy-start.9 = (bf16[4,83,768]{2,0,1:T(4,128)(2,1)}, bf16[4,83,768]{2,0,1:T(4,128)(2,1)S(1)}, u32[]{:S(2)}) copy-start(bf16[4,83,768]{2,0,1:T(4,128)(2,1)S(1)} %get-tuple-element.24) | copy-start | bytes 1529860
  8.8 7.3 %collective-permute-start = (bf16[4,83,768]{2,0,1:T(4,128)(2,1)}, bf16[4,83,768]{2,0,1:T(4,128)(2,1)}, u32[]{:S(2)}, u32[]{:S(2)}) collective-permute-start(bf16[4,83,768]{2,0,1:T(4,128)(2,1)} %copy.33), channel_id=1, source_target_pairs={{0,1},{1,0},{2,3},{3,2},{4,5},{5,4},{6,7},{7,6},{8,9},{9,8},{10,11... | collective-permute-start | bytes 1529864 | tf_op jit(solution)/shard_map/ppermute | solution.py:16
  9.3 3.7 %copy-start.2 = (bf16[1328,512]{1,0:T(8,128)(2,1)S(1)}, bf16[1328,512]{1,0:T(8,128)(2,1)}, u32[]{:S(2)}) copy-start(bf16[1328,512]{1,0:T(8,128)(2,1)} %param.9) | copy-start | bytes 4079620
  12.9 8.1 %collective-permute-start.4 = (bf16[4,83,768]{2,0,1:T(4,128)(2,1)}, bf16[4,83,768]{2,0,1:T(4,128)(2,1)}, u32[]{:S(2)}, u32[]{:S(2)}) collective-permute-start(bf16[4,83,768]{2,0,1:T(4,128)(2,1)} %copy.39), channel_id=1, source_target_pairs={{0,1},{1,0},{2,3},{3,2},{4,5},{5,4},{6,7},{7,6},{8,9},{9,8},{10,11... | collective-permute-start | bytes 1529864 | tf_op jit(solution)/shard_map/ppermute | solution.py:16
  13.6 0.7 copy-start.13
  13.7 49.3 %collective-permute-start.10 = (bf16[4,4,96,512]{3,2,1,0:T(8,128)(2,1)S(1)}, bf16[4,4,96,512]{3,2,1,0:T(8,128)(2,1)S(1)}, u32[]{:S(2)}, u32[]{:S(2)}) collective-permute-start(bf16[4,4,96,512]{3,2,1,0:T(8,128)(2,1)S(1)} %pad.14), channel_id=1, source_target_pairs={{0,1},{1,0},{2,3},{3,2},{4,5},{5,4},{6,7},{7,6},{8,9},{9,8},{10,11... | collective-permute-start | bytes 4718600 | tf_op jit(solution)/shard_map/ppermute | solution.py:16
  16.1 4.8 %copy-start.10 = (bf16[4,83,768]{2,0,1:T(4,128)(2,1)S(1)}, bf16[4,83,768]{2,0,1:T(4,128)(2,1)}, u32[]{:S(2)}) copy-start(bf16[4,83,768]{2,0,1:T(4,128)(2,1)} %copy-done.9) | copy-start | bytes 1529860
  21.0 7.8 %copy-start.8 = (bf16[4,83,768]{2,0,1:T(4,128)(2,1)S(1)}, bf16[4,83,768]{2,0,1:T(4,128)(2,1)}, u32[]{:S(2)}) copy-start(bf16[4,83,768]{2,0,1:T(4,128)(2,1)} %get-tuple-element.25) | copy-start | bytes 1529860
  25.8 25.9 %collective-permute-start.1 = (bf16[4,83,384]{2,1,0:T(8,128)(2,1)}, bf16[4,83,384]{2,1,0:T(8,128)(2,1)}, u32[]{:S(2)}, u32[]{:S(2)}) collective-permute-start(bf16[4,83,384]{2,1,0:T(8,128)(2,1)} %get-tuple-element.14), channel_id=1, source_target_pairs={{0,2},{2,0},{1,3},{3,1},{4,6},{6,4},{5,7},{7,5},{8,10},{10,8},{9,1... | collective-permute-start | bytes 764936 | tf_op jit(solution)/shard_map/ppermute | solution.py:161
  28.8 3.0 %copy-start.7 = (bf16[4,83,768]{2,0,1:T(4,128)(2,1)S(1)}, bf16[4,83,768]{2,0,1:T(4,128)(2,1)}, u32[]{:S(2)}) copy-start(bf16[4,83,768]{2,0,1:T(4,128)(2,1)} %get-tuple-element.23) | copy-start | bytes 1529860
  31.6 3.5 %collective-permute-start.2 = (bf16[4,83,768]{2,0,1:T(4,128)(2,1)S(1)}, bf16[4,83,768]{2,0,1:T(4,128)(2,1)S(1)}, u32[]{:S(2)}, u32[]{:S(2)}) collective-permute-start(bf16[4,83,768]{2,0,1:T(4,128)(2,1)S(1)} %copy.36), channel_id=1, source_target_pairs={{0,1},{1,0},{2,3},{3,2},{4,5},{5,4},{6,7},{7,6},{8,9},{9,8},{10,11... | collective-permute-start | bytes 1529864 | tf_op jit(solution)/shard_map/ppermute | solution.py:16
  34.6 6.3 %collective-permute-start.5 = (bf16[4,83,768]{2,0,1:T(4,128)(2,1)S(1)}, bf16[4,83,768]{2,0,1:T(4,128)(2,1)S(1)}, u32[]{:S(2)}, u32[]{:S(2)}) collective-permute-start(bf16[4,83,768]{2,0,1:T(4,128)(2,1)S(1)} %copy.42), channel_id=1, source_target_pairs={{0,1},{1,0},{2,3},{3,2},{4,5},{5,4},{6,7},{7,6},{8,9},{9,8},{10,11... | collective-permute-start | bytes 1529864 | tf_op jit(solution)/shard_map/ppermute | solution.py:16
  35.2 15.3 %collective-permute-start.7 = (bf16[4,83,384]{2,1,0:T(8,128)(2,1)}, bf16[4,83,384]{2,1,0:T(8,128)(2,1)}, u32[]{:S(2)}, u32[]{:S(2)}) collective-permute-start(bf16[4,83,384]{2,1,0:T(8,128)(2,1)} %get-tuple-element.18), channel_id=1, source_target_pairs={{0,2},{2,0},{1,3},{3,1},{4,6},{6,4},{5,7},{7,5},{8,10},{10,8},{9,1... | collective-permute-start | bytes 764936 | tf_op jit(solution)/shard_map/ppermute | solution.py:161
  38.1 5.5 %copy-start.3 = (bf16[4,83,768]{2,1,0:T(8,128)(2,1)}, bf16[4,83,768]{2,1,0:T(8,128)(2,1)S(1)}, u32[]{:S(2)}) copy-start(bf16[4,83,768]{2,1,0:T(8,128)(2,1)S(1)} %copy_add_fusion.2) | copy-start | bytes 1529860
  38.9 17.9 %collective-permute-start.3 = (bf16[4,83,384]{2,1,0:T(8,128)(2,1)}, bf16[4,83,384]{2,1,0:T(8,128)(2,1)}, u32[]{:S(2)}, u32[]{:S(2)}) collective-permute-start(bf16[4,83,384]{2,1,0:T(8,128)(2,1)} %slice.101), channel_id=1, source_target_pairs={{0,2},{2,0},{1,3},{3,1},{4,6},{6,4},{5,7},{7,5},{8,10},{10,8},{9,1... | collective-permute-start | bytes 764936 | tf_op jit(solution)/shard_map/ppermute | solution.py:161
  40.9 3.8 %copy-start.12 = (f32[9,16,360]{2,1,0:T(8,128)S(1)}, f32[9,16,360]{2,1,0:T(8,128)}, u32[]{:S(2)}) copy-start(f32[9,16,360]{2,1,0:T(8,128)} %param.8) | copy-start | bytes 622084
  43.6 0.9 copy-start.5
  44.5 14.9 %collective-permute-start.6 = (bf16[4,83,384]{2,1,0:T(8,128)(2,1)}, bf16[4,83,384]{2,1,0:T(8,128)(2,1)}, u32[]{:S(2)}, u32[]{:S(2)}) collective-permute-start(bf16[4,83,384]{2,1,0:T(8,128)(2,1)} %slice.105), channel_id=1, source_target_pairs={{0,2},{2,0},{1,3},{3,1},{4,6},{6,4},{5,7},{7,5},{8,10},{10,8},{9,1... | collective-permute-start | bytes 764936 | tf_op jit(solution)/shard_map/ppermute | solution.py:161
  44.7 5.7 %copy-start.1 = (f32[512]{0:T(512)S(1)}, f32[512]{0:T(512)}, u32[]{:S(2)}) copy-start(f32[512]{0:T(512)} %param.10) | copy-start | bytes 6148
  50.4 8.0 %copy-start.4 = (bf16[4,83,768]{2,1,0:T(8,128)(2,1)S(1)}, bf16[4,83,768]{2,1,0:T(8,128)(2,1)}, u32[]{:S(2)}) copy-start(bf16[4,83,768]{2,1,0:T(8,128)(2,1)} %copy-done.3) | copy-start | bytes 1529860
  50.4 9.0 %copy-start.6 = (bf16[4,83,768]{2,1,0:T(8,128)(2,1)S(1)}, bf16[4,83,768]{2,1,0:T(8,128)(2,1)}, u32[]{:S(2)}) copy-start(bf16[4,83,768]{2,1,0:T(8,128)(2,1)} %copy-done.5) | copy-start | bytes 1529860
  50.5 10.0 %collective-permute-start.11 = (f32[1,512]{1,0:T(1,128)S(1)}, f32[1,512]{1,0:T(1,128)S(1)}, u32[]{:S(2)}, u32[]{:S(2)}) collective-permute-start(f32[1,512]{1,0:T(1,128)S(1)} %bitcast.53), channel_id=1, source_target_pairs={{0,1},{1,0},{2,3},{3,2},{4,5},{5,4},{6,7},{7,6},{8,9},{9,8},{10,11... | collective-permute-start | bytes 6152 | tf_op jit(solution)/shard_map/ppermute | solution.py:16
  51.7 8.7 %collective-permute-start.8 = (bf16[1,83,384]{2,1,0:T(8,128)(2,1)S(1)}, bf16[1,83,384]{2,1,0:T(8,128)(2,1)S(1)}, u32[]{:S(2)}, u32[]{:S(2)}) collective-permute-start(bf16[1,83,384]{2,1,0:T(8,128)(2,1)S(1)} %slice.106), channel_id=1, source_target_pairs={{0,4},{4,8},{8,12},{1,5},{5,9},{9,13},{2,6},{6,10},{10,14},{3,7},{... | collective-permute-start | bytes 191240 | tf_op jit(solution)/shard_map/ppermute | solution.py:166
  56.9 6.2 %collective-permute-start.9 = (bf16[1,83,384]{2,1,0:T(8,128)(2,1)S(1)}, bf16[1,83,384]{2,1,0:T(8,128)(2,1)S(1)}, u32[]{:S(2)}, u32[]{:S(2)}) collective-permute-start(bf16[1,83,384]{2,1,0:T(8,128)(2,1)S(1)} %slice.107), channel_id=1, source_target_pairs={{4,0},{8,4},{12,8},{5,1},{9,5},{13,9},{6,2},{10,6},{14,10},{7,3},{... | collective-permute-start | bytes 191240 | tf_op jit(solution)/shard_map/ppermute | solution.py:167
  69.0 0.8 copy-start
  69.8 1.9 %collective-permute-start.12 = (bf16[4,90,512]{2,1,0:T(8,128)(2,1)}, bf16[4,90,512]{2,1,0:T(8,128)(2,1)S(1)}, u32[]{:S(2)}, u32[]{:S(2)}) collective-permute-start(bf16[4,90,512]{2,1,0:T(8,128)(2,1)} %get-tuple-element.20), channel_id=1, source_target_pairs={{0,1},{1,0},{2,3},{3,2},{4,5},{5,4},{6,7},{7,6},{8,9},{9,8},{10,11... | collective-permute-start | bytes 1105928 | tf_op jit(solution)/shard_map/ppermute | solution.py:16
